TPU v7x, 32 devices: a whole 2x2x4 slice. The times are simulated.
32 devices in a mesh: gz: 8 (over z, x), gy: 4 (over y, core).
Axes of the slice: x: 2, y: 2, z: 4, core: 2. Of those that a mesh axis runs over, the one named last changes fastest.
Arguments:
- populations: float32 [19, 8, 128, 256], P(None, 'gz', 'gy'), may hold values from 0 to 0.5, as said below
- solid_fraction: float32 [8, 128, 256], P('gz', 'gy'), may hold values from 0 to 1
- labels: int32 [8, 128, 256], P('gz', 'gy'), may hold values from 0 to 4, as said below
Outputs:
- sensitivity: float32 [8, 128, 256], P('gz', 'gy')
- adjoint_populations: float32 [19, 8, 128, 256], P(None, 'gz', 'gy')
Inputs may be any that keep to these rules, and one draw needn't show every extreme that they name: `populations`: each population is w_q times a factor between 0.7 and 1.3. labels 3 appear only in the first plane along the feeding direction and 4 only in the last, in voxels that are not solid.
All inputs are finite; a program needn't handle non-finite values.
Results may differ from a plain program's by a relative error of at most 0.00028.
Values sent between devices are 32-bit elements; how exact they have to be, the bound alone decides.
No kernel may reach another device: no remote copies, remote signals or barrier semaphores. Data moves between devices by JAX's collectives and lax.ppermute only.
A program may use at most 64 MiB of HBM per device.

v0:
```python
import jax
import jax.numpy as jnp
from jax import lax
from jax.sharding import PartitionSpec as P

STEPS = 2


OMEGA = 0.9
INLET_SPEED = 0.05


def passed_along(array, axis, by):
    count = lax.axis_size(axis)
    return lax.ppermute(array, axis, [(i, (i + by) % count) for i in range(count)])


def velocity_table():
    velocities = [(0, 0, 0)]
    for axis in range(3):
        for sign in (1, -1):
            vector = [0, 0, 0]
            vector[axis] = sign
            velocities.append(tuple(vector))
    for first in range(3):
        for second in range(first + 1, 3):
            for sign_a in (1, -1):
                for sign_b in (1, -1):
                    vector = [0, 0, 0]
                    vector[first] = sign_a
                    vector[second] = sign_b
                    velocities.append(tuple(vector))
    weights = [1.0 / 3.0] + [1.0 / 18.0] * 6 + [1.0 / 36.0] * 12
    opposite = [velocities.index(tuple((-e for e in vector))) for vector in velocities]
    return (velocities, weights, opposite)


def equilibrium(density, vel_x, vel_y, vel_z):
    velocities, weights, opposite = velocity_table()
    rows = []
    speed = vel_x * vel_x + vel_y * vel_y + vel_z * vel_z
    for index in range(19):
        cx, cy, cz = velocities[index]
        along = cx * vel_x + cy * vel_y + cz * vel_z
        rows.append(
            weights[index] * density * (1.0 + 3.0 * along + 4.5 * along * along - 1.5 * speed)
        )
    return jnp.stack(rows)


def moments(field):
    velocities, weights, opposite = velocity_table()
    density = jnp.sum(field, axis=0)
    mom_x = sum((velocities[q][0] * field[q] for q in range(19) if velocities[q][0] != 0))
    mom_y = sum((velocities[q][1] * field[q] for q in range(19) if velocities[q][1] != 0))
    mom_z = sum((velocities[q][2] * field[q] for q in range(19) if velocities[q][2] != 0))
    return (density, mom_x, mom_y, mom_z)


def collide(field, s_eff, labels):
    velocities, weights, opposite = velocity_table()
    density, mom_x, mom_y, mom_z = moments(field)
    feq = equilibrium(density, mom_x / density, mom_y / density, mom_z / density)
    rate = jnp.where(labels == 4, jnp.float32(1.0), jnp.float32(OMEGA))
    relaxed = field - rate * (field - feq)
    flipped = jnp.stack([field[opposite[q]] for q in range(19)])
    mixed = (1.0 - s_eff) * relaxed + s_eff * flipped
    ones = jnp.ones_like(density)
    inlet = equilibrium(ones, 0.0 * ones, 0.0 * ones, INLET_SPEED * ones)
    return jnp.where(labels == 3, inlet, mixed)


def energy(field, s_eff):
    density, mom_x, mom_y, mom_z = moments(field)
    return jnp.sum((1.0 - s_eff) * (mom_x * mom_x + mom_y * mom_y + mom_z * mom_z) / density)


def stream(field, sense):
    velocities, weights, opposite = velocity_table()
    offsets = [(sense * v[0], sense * v[1], sense * v[2]) for v in velocities]
    raise_z = [q for q in range(19) if offsets[q][2] == 1]
    lower_z = [q for q in range(19) if offsets[q][2] == -1]
    tops = jnp.stack([field[q, -1:] for q in raise_z])
    bottoms = jnp.stack([field[q, :1] for q in lower_z])
    from_below = passed_along(tops, "gz", 1)
    from_above = passed_along(bottoms, "gz", -1)
    sectioned = []
    for q in range(19):
        if offsets[q][2] == 1:
            sectioned.append(jnp.concatenate([from_below[raise_z.index(q)], field[q, :-1]], axis=0))
        elif offsets[q][2] == -1:
            sectioned.append(jnp.concatenate([field[q, 1:], from_above[lower_z.index(q)]], axis=0))
        else:
            sectioned.append(field[q])
    raise_y = [q for q in range(19) if offsets[q][1] == 1]
    lower_y = [q for q in range(19) if offsets[q][1] == -1]
    tops_y = jnp.stack([sectioned[q][:, -1:] for q in raise_y])
    bottoms_y = jnp.stack([sectioned[q][:, :1] for q in lower_y])
    below_y = passed_along(tops_y, "gy", 1)
    above_y = passed_along(bottoms_y, "gy", -1)
    moved = []
    for q in range(19):
        if offsets[q][1] == 1:
            moved.append(jnp.concatenate([below_y[raise_y.index(q)], sectioned[q][:, :-1]], axis=1))
        elif offsets[q][1] == -1:
            moved.append(jnp.concatenate([sectioned[q][:, 1:], above_y[lower_y.index(q)]], axis=1))
        else:
            moved.append(sectioned[q])
    return jnp.stack([jnp.roll(moved[q], offsets[q][0], axis=2) for q in range(19)])


def global_energy(value):
    return lax.psum(value, ("gz", "gy"))


def on_device(populations, solid_fraction, labels):
    s_eff = jnp.where(
        labels == 1, solid_fraction, jnp.where(labels == 2, jnp.float32(1.0), jnp.float32(0.0))
    )
    states = [populations]
    total = jnp.float32(0.0)
    for step in range(STEPS):
        nxt = stream(collide(states[-1], s_eff, labels), 1)
        states.append(nxt)
        total = total + global_energy(energy(nxt, s_eff))
    energy_grad = jax.grad(energy, argnums=(0, 1))
    adjoint = jnp.zeros_like(populations)
    fraction_grad = jnp.zeros_like(solid_fraction)
    for step in reversed(range(STEPS)):
        grad_field, grad_frac = energy_grad(states[step + 1], s_eff)
        adjoint = adjoint + grad_field
        fraction_grad = fraction_grad + grad_frac
        pulled = stream(adjoint, -1)
        unused, pullback = jax.vjp(
            lambda field, frac: collide(field, frac, labels), states[step], s_eff
        )
        adjoint, grad_frac = pullback(pulled)
        fraction_grad = fraction_grad + grad_frac
    cells = (
        populations.shape[1]
        * populations.shape[2]
        * populations.shape[3]
        * lax.axis_size("gz")
        * lax.axis_size("gy")
    )
    mean_energy = total / (STEPS * cells)
    sensitivity = jnp.where(labels == 1, fraction_grad, jnp.float32(0.0)) / mean_energy
    return (sensitivity, adjoint / mean_energy)


def solution(mesh):
    in_specs = (P(None, "gz", "gy", None), P("gz", "gy", None), P("gz", "gy", None))
    out_specs = (P("gz", "gy", None), P(None, "gz", "gy", None))
    return jax.shard_map(
        on_device, mesh=mesh, in_specs=in_specs, out_specs=out_specs, check_vma=False
    )
```

profile of v0, /device:TPU:0, one launch (start us, length us, event | category | flops | bytes accessed | tf_op | source)
XLA Modules:
  0.0 159.6 jit_solution(8150943439482164210)
XLA Ops:
  1.4 0.8 constant_dynamic-update-slice_fusion.50
  2.2 1.1 reduce_sum.1963
  6.0 6.0 %collective-permute-start.1 = (f32[5,1,32,256]{3,2,1,0:T(8,128)S(1)}, f32[5,1,32,256]{3,2,1,0:T(8,128)S(1)}, u32[]{:S(2)}, u32[]{:S(2)}) collective-permute-start(f32[5,1,32,256]{3,2,1,0:T(8,128)S(1)} %get-tuple-element.171), channel_id=1, source_target_pairs={{0,28},{4,0},{8,4},{12,8},{16,12},{20,16},{24,20},{28,24},{1,29},{... | collective-permute-start | bytes 491528 | tf_op jit(solution)/shard_map/ppermute | solution.py:15
  17.5 2.9 %collective-permute-done = f32[5,1,32,256]{3,2,1,0:T(8,128)S(1)} collective-permute-done((f32[5,1,32,256]{3,2,1,0:T(8,128)S(1)}, f32[5,1,32,256]{3,2,1,0:T(8,128)S(1)}, u32[]{:S(2)}, u32[]{:S(2)}) %collective-permute-start) | collective-permute-done | bytes 163872 | tf_op jit(solution)/shard_map/ppermute | solution.py:15
  21.7 1.7 %collective-permute-start.3 = (f32[5,1,1,256]{3,2,1,0:T(1,128)S(1)}, f32[5,1,1,256]{3,2,1,0:T(1,128)S(1)}, u32[]{:S(2)}, u32[]{:S(2)}) collective-permute-start(f32[5,1,1,256]{3,2,1,0:T(1,128)S(1)} %constant_dynamic-update-slice_fusion.66), channel_id=1, source_target_pairs={{0,3},{1,0},{2,1},{3,2},{4,7},{5,4},{6,5},{7,6},{8,11},{9,8},{10,9... | collective-permute-start | bytes 15368 | tf_op jit(solution)/shard_map/ppermute | solution.py:15
  23.5 1.3 collective-permute-done.2
  39.9 4.7 %collective-permute-start.5 = (f32[5,1,32,256]{3,2,1,0:T(8,128)S(1)}, f32[5,1,32,256]{3,2,1,0:T(8,128)S(1)}, u32[]{:S(2)}, u32[]{:S(2)}) collective-permute-start(f32[5,1,32,256]{3,2,1,0:T(8,128)S(1)} %get-tuple-element.153), channel_id=1, source_target_pairs={{0,28},{4,0},{8,4},{12,8},{16,12},{20,16},{24,20},{28,24},{1,29},{... | collective-permute-start | bytes 491528 | tf_op jit(solution)/shard_map/ppermute | solution.py:15
  45.2 3.5 %collective-permute-done.4 = f32[5,1,32,256]{3,2,1,0:T(8,128)S(1)} collective-permute-done((f32[5,1,32,256]{3,2,1,0:T(8,128)S(1)}, f32[5,1,32,256]{3,2,1,0:T(8,128)S(1)}, u32[]{:S(2)}, u32[]{:S(2)}) %collective-permute-start.4) | collective-permute-done | bytes 163872 | tf_op jit(solution)/shard_map/ppermute | solution.py:15
  48.8 1.6 %collective-permute-done.5 = f32[5,1,32,256]{3,2,1,0:T(8,128)S(1)} collective-permute-done((f32[5,1,32,256]{3,2,1,0:T(8,128)S(1)}, f32[5,1,32,256]{3,2,1,0:T(8,128)S(1)}, u32[]{:S(2)}, u32[]{:S(2)}) %collective-permute-start.5) | collective-permute-done | bytes 163872 | tf_op jit(solution)/shard_map/ppermute | solution.py:15
  51.9 1.9 %collective-permute-done.6 = f32[5,1,1,256]{3,2,1,0:T(1,128)S(1)} collective-permute-done((f32[5,1,1,256]{3,2,1,0:T(1,128)S(1)}, f32[5,1,1,256]{3,2,1,0:T(1,128)S(1)}, u32[]{:S(2)}, u32[]{:S(2)}) %collective-permute-start.6) | collective-permute-done | bytes 5152 | tf_op jit(solution)/shard_map/ppermute | solution.py:15
  54.1 1.8 %divide_reduce_fusion = (f32[]{:T(128)}, f32[]{:T(128)}, f32[1,32,256]{2,1,0:T(8,128)S(1)}, f32[1,32,256]{2,1,0:T(8,128)S(1)}, f32[1,32,256]{2,1,0:T(8,128)}, /*...) fusion(f32[1,32,256]{2,1,0:T(8,128)S(1)} %get-tuple-element.70,, ...), kind=kLoop, calls=%fused_computation.1450 | loop fusion | flops 1368062 | bytes 1671176 | tf_op jit(solution)/shard_map/reduce_sum | solution.py:75
  62.3 3.6 %collective-permute-start.8 = (f32[5,1,32,256]{3,2,1,0:T(8,128)}, f32[5,1,32,256]{3,2,1,0:T(8,128)}, u32[]{:S(2)}, u32[]{:S(2)}) collective-permute-start(f32[5,1,32,256]{3,2,1,0:T(8,128)} %get-tuple-element.134), channel_id=1, source_target_pairs={{0,28},{4,0},{8,4},{12,8},{16,12},{20,16},{24,20},{28,24},{1,29},{... | collective-permute-start | bytes 491528 | tf_op jit(solution)/shard_map/ppermute | solution.py:15
  67.1 1.2 constant_dynamic-update-slice_fusion.166
  68.3 1.3 constant_dynamic-update-slice_fusion.165
  69.6 1.2 constant_dynamic-update-slice_fusion.161
  70.8 1.3 constant_dynamic-update-slice_fusion.160
  72.1 1.5 multiply_bitcast_fusion.1
  73.7 36.8 %psum.16 = f32[]{:T(128)} all-reduce(f32[]{:T(128)S(6)} %add.7521), channel_id=1, replica_groups=mesh['gz'=8,'gy'=4] {'gz','gy'}, use_global_device_ids=true, to_apply=%region_6.7 | all-reduce | flops 1 | bytes 8 | tf_op jit(solution)/shard_map/psum | solution.py:113
  110.5 1.4 slice.1591
  114.1 2.3 %collective-permute-start.9 = (f32[5,1,32,256]{3,2,1,0:T(8,128)}, f32[5,1,32,256]{3,2,1,0:T(8,128)}, u32[]{:S(2)}, u32[]{:S(2)}) collective-permute-start(f32[5,1,32,256]{3,2,1,0:T(8,128)} %copy-done.85), channel_id=1, source_target_pairs={{0,4},{4,8},{8,12},{12,16},{16,20},{20,24},{24,28},{28,0},{1,5},{5... | collective-permute-start | bytes 491528 | tf_op jit(solution)/shard_map/ppermute | solution.py:15
  117.0 0.8 constant_dynamic-update-slice_fusion.184
  117.8 0.8 slice_bitcast_fusion.21
  118.6 3.8 %collective-permute-done.9 = f32[5,1,32,256]{3,2,1,0:T(8,128)} collective-permute-done((f32[5,1,32,256]{3,2,1,0:T(8,128)}, f32[5,1,32,256]{3,2,1,0:T(8,128)}, u32[]{:S(2)}, u32[]{:S(2)}) %collective-permute-start.9) | collective-permute-done | bytes 163872 | tf_op jit(solution)/shard_map/ppermute | solution.py:15
  122.4 0.8 slice_bitcast_fusion.20
  124.7 2.6 %collective-permute-done.11 = f32[5,1,1,256]{3,2,1,0:T(1,128)S(1)} collective-permute-done((f32[5,1,1,256]{3,2,1,0:T(1,128)S(1)}, f32[5,1,1,256]{3,2,1,0:T(1,128)S(1)}, u32[]{:S(2)}, u32[]{:S(2)}) %collective-permute-start.11) | collective-permute-done | bytes 5152 | tf_op jit(solution)/shard_map/ppermute | solution.py:15
  127.3 0.8 slice_bitcast_fusion.17
  128.1 0.8 slice_bitcast_fusion.16
  135.7 1.6 fusion.454
  138.7 4.7 %collective-permute-start.12 = (f32[5,1,32,256]{3,2,1,0:T(8,128)S(1)}, f32[5,1,32,256]{3,2,1,0:T(8,128)S(1)}, u32[]{:S(2)}, u32[]{:S(2)}) collective-permute-start(f32[5,1,32,256]{3,2,1,0:T(8,128)S(1)} %get-tuple-element.97), channel_id=1, source_target_pairs={{0,28},{4,0},{8,4},{12,8},{16,12},{20,16},{24,20},{28,24},{1,29},{... | collective-permute-start | bytes 491528 | tf_op jit(solution)/shard_map/ppermute | solution.py:15
  143.6 6.1 %collective-permute-done.12 = f32[5,1,32,256]{3,2,1,0:T(8,128)S(1)} collective-permute-done((f32[5,1,32,256]{3,2,1,0:T(8,128)S(1)}, f32[5,1,32,256]{3,2,1,0:T(8,128)S(1)}, u32[]{:S(2)}, u32[]{:S(2)}) %collective-permute-start.12) | collective-permute-done | bytes 163872 | tf_op jit(solution)/shard_map/ppermute | solution.py:15
  151.1 2.0 %collective-permute-done.15 = f32[5,1,1,256]{3,2,1,0:T(1,128)S(1)} collective-permute-done((f32[5,1,1,256]{3,2,1,0:T(1,128)S(1)}, f32[5,1,1,256]{3,2,1,0:T(1,128)S(1)}, u32[]{:S(2)}, u32[]{:S(2)}) %collective-permute-start.15) | collective-permute-done | bytes 5152 | tf_op jit(solution)/shard_map/ppermute | solution.py:15
  158.5 1.1 add_divide_fusion
  (518 shorter events, 51.4 us)
Async XLA Ops:
  0.6 2.7 %copy-start = (f32[19,1,32,256]{3,2,1,0:T(8,128)S(1)}, f32[19,1,32,256]{3,2,1,0:T(8,128)}, u32[]{:S(2)}) copy-start(f32[19,1,32,256]{3,2,1,0:T(8,128)} %param.3) | copy-start | bytes 1867780
  1.4 3.7 %copy-start.26 = (pred[32,256]{1,0:T(8,128)(4,1)}, pred[32,256]{1,0:T(8,128)(4,1)S(1)}, u32[]{:S(2)}) copy-start(pred[32,256]{1,0:T(8,128)(4,1)S(1)} %compare_bitcast_fusion) | copy-start | bytes 24580
  6.0 10.2 %collective-permute-start.1 = (f32[5,1,32,256]{3,2,1,0:T(8,128)S(1)}, f32[5,1,32,256]{3,2,1,0:T(8,128)S(1)}, u32[]{:S(2)}, u32[]{:S(2)}) collective-permute-start(f32[5,1,32,256]{3,2,1,0:T(8,128)S(1)} %get-tuple-element.171), channel_id=1, source_target_pairs={{0,28},{4,0},{8,4},{12,8},{16,12},{20,16},{24,20},{28,24},{1,29},{... | collective-permute-start | bytes 491528 | tf_op jit(solution)/shard_map/ppermute | solution.py:15
  12.1 8.4 %collective-permute-start = (f32[5,1,32,256]{3,2,1,0:T(8,128)S(1)}, f32[5,1,32,256]{3,2,1,0:T(8,128)S(1)}, u32[]{:S(2)}, u32[]{:S(2)}) collective-permute-start(f32[5,1,32,256]{3,2,1,0:T(8,128)S(1)} %get-tuple-element.172), channel_id=1, source_target_pairs={{0,4},{4,8},{8,12},{12,16},{16,20},{20,24},{24,28},{28,0},{1,5},{5... | collective-permute-start | bytes 491528 | tf_op jit(solution)/shard_map/ppermute | solution.py:15
  16.2 37.9 %copy-start.23 = (f32[5,1,32,256]{3,2,1,0:T(8,128)}, f32[5,1,32,256]{3,2,1,0:T(8,128)S(1)}, u32[]{:S(2)}) copy-start(f32[5,1,32,256]{3,2,1,0:T(8,128)S(1)} %collective-permute-done.1) | copy-start | bytes 491524
  20.4 33.7 %copy-start.17 = (f32[5,1,32,256]{3,2,1,0:T(8,128)}, f32[5,1,32,256]{3,2,1,0:T(8,128)S(1)}, u32[]{:S(2)}) copy-start(f32[5,1,32,256]{3,2,1,0:T(8,128)S(1)} %collective-permute-done) | copy-start | bytes 491524
  21.7 3.0 %collective-permute-start.2 = (f32[5,1,1,256]{3,2,1,0:T(1,128)S(1)}, f32[5,1,1,256]{3,2,1,0:T(1,128)S(1)}, u32[]{:S(2)}, u32[]{:S(2)}) collective-permute-start(f32[5,1,1,256]{3,2,1,0:T(1,128)S(1)} %constant_dynamic-update-slice_fusion.61), channel_id=1, source_target_pairs={{0,1},{1,2},{2,3},{3,0},{4,5},{5,6},{6,7},{7,4},{8,9},{9,10},{10,1... | collective-permute-start | bytes 15368 | tf_op jit(solution)/shard_map/ppermute | solution.py:15
  21.7 3.8 %collective-permute-start.3 = (f32[5,1,1,256]{3,2,1,0:T(1,128)S(1)}, f32[5,1,1,256]{3,2,1,0:T(1,128)S(1)}, u32[]{:S(2)}, u32[]{:S(2)}) collective-permute-start(f32[5,1,1,256]{3,2,1,0:T(1,128)S(1)} %constant_dynamic-update-slice_fusion.66), channel_id=1, source_target_pairs={{0,3},{1,0},{2,1},{3,2},{4,7},{5,4},{6,5},{7,6},{8,11},{9,8},{10,9... | collective-permute-start | bytes 15368 | tf_op jit(solution)/shard_map/ppermute | solution.py:15
  25.5 28.5 %copy-start.13 = (f32[1,32,1]{2,1,0:T(8,128)}, f32[1,32,1]{2,1,0:T(8,128)S(1)}, u32[]{:S(2)}) copy-start(f32[1,32,1]{2,1,0:T(8,128)S(1)} %fusion.724) | copy-start | bytes 388
  26.2 27.9 %copy-start.15 = (f32[1,32,1]{2,1,0:T(8,128)}, f32[1,32,1]{2,1,0:T(8,128)S(1)}, u32[]{:S(2)}) copy-start(f32[1,32,1]{2,1,0:T(8,128)S(1)} %fusion.723) | copy-start | bytes 388
  26.2 27.9 %copy-start.24 = (f32[1,32,1]{2,1,0:T(8,128)}, f32[1,32,1]{2,1,0:T(8,128)S(1)}, u32[]{:S(2)}) copy-start(f32[1,32,1]{2,1,0:T(8,128)S(1)} %pad_maximum_fusion.74) | copy-start | bytes 388
  33.3 2.1 %copy-start.7 = (f32[1,1,32,256]{3,2,1,0:T(8,128)}, f32[1,1,32,256]{3,2,1,0:T(8,128)S(1)}, u32[]{:S(2)}) copy-start(f32[1,1,32,256]{3,2,1,0:T(8,128)S(1)} %get-tuple-element.53) | copy-start | bytes 98308
  33.3 2.7 %copy-start.9 = (f32[1,1,32,256]{3,2,1,0:T(8,128)}, f32[1,1,32,256]{3,2,1,0:T(8,128)S(1)}, u32[]{:S(2)}) copy-start(f32[1,1,32,256]{3,2,1,0:T(8,128)S(1)} %get-tuple-element.51) | copy-start | bytes 98308
  33.4 3.3 %copy-start.11 = (f32[1,1,32,256]{3,2,1,0:T(8,128)}, f32[1,1,32,256]{3,2,1,0:T(8,128)S(1)}, u32[]{:S(2)}) copy-start(f32[1,1,32,256]{3,2,1,0:T(8,128)S(1)} %get-tuple-element.49) | copy-start | bytes 98308
  38.9 9.8 %collective-permute-start.4 = (f32[5,1,32,256]{3,2,1,0:T(8,128)S(1)}, f32[5,1,32,256]{3,2,1,0:T(8,128)S(1)}, u32[]{:S(2)}, u32[]{:S(2)}) collective-permute-start(f32[5,1,32,256]{3,2,1,0:T(8,128)S(1)} %get-tuple-element.154), channel_id=1, source_target_pairs={{0,4},{4,8},{8,12},{12,16},{16,20},{20,24},{24,28},{28,0},{1,5},{5... | collective-permute-start | bytes 491528 | tf_op jit(solution)/shard_map/ppermute | solution.py:15
  39.9 10.5 %collective-permute-start.5 = (f32[5,1,32,256]{3,2,1,0:T(8,128)S(1)}, f32[5,1,32,256]{3,2,1,0:T(8,128)S(1)}, u32[]{:S(2)}, u32[]{:S(2)}) collective-permute-start(f32[5,1,32,256]{3,2,1,0:T(8,128)S(1)} %get-tuple-element.153), channel_id=1, source_target_pairs={{0,28},{4,0},{8,4},{12,8},{16,12},{20,16},{24,20},{28,24},{1,29},{... | collective-permute-start | bytes 491528 | tf_op jit(solution)/shard_map/ppermute | solution.py:15
  50.4 1.4 collective-permute-start.7
  50.8 3.0 %collective-permute-start.6 = (f32[5,1,1,256]{3,2,1,0:T(1,128)S(1)}, f32[5,1,1,256]{3,2,1,0:T(1,128)S(1)}, u32[]{:S(2)}, u32[]{:S(2)}) collective-permute-start(f32[5,1,1,256]{3,2,1,0:T(1,128)S(1)} %constant_dynamic-update-slice_fusion.138), channel_id=1, source_target_pairs={{0,1},{1,2},{2,3},{3,0},{4,5},{5,6},{6,7},{7,4},{8,9},{9,10},{10,1... | collective-permute-start | bytes 15368 | tf_op jit(solution)/shard_map/ppermute | solution.py:15
  59.8 1.9 %copy-start.49 = (f32[1,32,256]{2,1,0:T(8,128)}, f32[1,32,256]{2,1,0:T(8,128)S(1)}, u32[]{:S(2)}) copy-start(f32[1,32,256]{2,1,0:T(8,128)S(1)} %get-tuple-element.137) | copy-start | bytes 98308
  59.8 2.4 %copy-start.85 = (f32[5,1,32,256]{3,2,1,0:T(8,128)}, f32[5,1,32,256]{3,2,1,0:T(8,128)S(1)}, u32[]{:S(2)}) copy-start(f32[5,1,32,256]{3,2,1,0:T(8,128)S(1)} %get-tuple-element.133) | copy-start | bytes 491524
  62.3 55.6 %collective-permute-start.8 = (f32[5,1,32,256]{3,2,1,0:T(8,128)}, f32[5,1,32,256]{3,2,1,0:T(8,128)}, u32[]{:S(2)}, u32[]{:S(2)}) collective-permute-start(f32[5,1,32,256]{3,2,1,0:T(8,128)} %get-tuple-element.134), channel_id=1, source_target_pairs={{0,28},{4,0},{8,4},{12,8},{16,12},{20,16},{24,20},{28,24},{1,29},{... | collective-permute-start | bytes 491528 | tf_op jit(solution)/shard_map/ppermute | solution.py:15
  114.1 8.3 %collective-permute-start.9 = (f32[5,1,32,256]{3,2,1,0:T(8,128)}, f32[5,1,32,256]{3,2,1,0:T(8,128)}, u32[]{:S(2)}, u32[]{:S(2)}) collective-permute-start(f32[5,1,32,256]{3,2,1,0:T(8,128)} %copy-done.85), channel_id=1, source_target_pairs={{0,4},{4,8},{8,12},{12,16},{16,20},{20,24},{24,28},{28,0},{1,5},{5... | collective-permute-start | bytes 491528 | tf_op jit(solution)/shard_map/ppermute | solution.py:15
  123.2 1.4 collective-permute-start.10
  123.9 3.3 %collective-permute-start.11 = (f32[5,1,1,256]{3,2,1,0:T(1,128)S(1)}, f32[5,1,1,256]{3,2,1,0:T(1,128)S(1)}, u32[]{:S(2)}, u32[]{:S(2)}) collective-permute-start(f32[5,1,1,256]{3,2,1,0:T(1,128)S(1)} %constant_dynamic-update-slice_fusion.163), channel_id=1, source_target_pairs={{0,1},{1,2},{2,3},{3,0},{4,5},{5,6},{6,7},{7,4},{8,9},{9,10},{10,1... | collective-permute-start | bytes 15368 | tf_op jit(solution)/shard_map/ppermute | solution.py:15
  124.7 2.6 %copy-start.46 = (f32[1,32,256]{2,1,0:T(8,128)S(1)}, f32[1,32,256]{2,1,0:T(8,128)}, u32[]{:S(2)}) copy-start(f32[1,32,256]{2,1,0:T(8,128)} %copy-done.45) | copy-start | bytes 98308
  135.7 1.6 %copy-start.53 = (f32[1,1,32,256]{3,2,1,0:T(8,128)S(1)}, f32[1,1,32,256]{3,2,1,0:T(8,128)}, u32[]{:S(2)}) copy-start(f32[1,1,32,256]{3,2,1,0:T(8,128)} %get-tuple-element.301) | copy-start | bytes 98308
  135.7 1.6 %copy-start.54 = (f32[1,1,32,256]{3,2,1,0:T(8,128)S(1)}, f32[1,1,32,256]{3,2,1,0:T(8,128)}, u32[]{:S(2)}) copy-start(f32[1,1,32,256]{3,2,1,0:T(8,128)} %get-tuple-element.302) | copy-start | bytes 98308
  135.7 1.6 %copy-start.55 = (f32[1,1,32,256]{3,2,1,0:T(8,128)S(1)}, f32[1,1,32,256]{3,2,1,0:T(8,128)}, u32[]{:S(2)}) copy-start(f32[1,1,32,256]{3,2,1,0:T(8,128)} %get-tuple-element.34) | copy-start | bytes 98308
  138.7 11.0 %collective-permute-start.13 = (f32[5,1,32,256]{3,2,1,0:T(8,128)S(1)}, f32[5,1,32,256]{3,2,1,0:T(8,128)S(1)}, u32[]{:S(2)}, u32[]{:S(2)}) collective-permute-start(f32[5,1,32,256]{3,2,1,0:T(8,128)S(1)} %get-tuple-element.96), channel_id=1, source_target_pairs={{0,4},{4,8},{8,12},{12,16},{16,20},{20,24},{24,28},{28,0},{1,5},{5... | collective-permute-start | bytes 491528 | tf_op jit(solution)/shard_map/ppermute | solution.py:15
  138.7 11.0 %collective-permute-start.12 = (f32[5,1,32,256]{3,2,1,0:T(8,128)S(1)}, f32[5,1,32,256]{3,2,1,0:T(8,128)S(1)}, u32[]{:S(2)}, u32[]{:S(2)}) collective-permute-start(f32[5,1,32,256]{3,2,1,0:T(8,128)S(1)} %get-tuple-element.97), channel_id=1, source_target_pairs={{0,28},{4,0},{8,4},{12,8},{16,12},{20,16},{24,20},{28,24},{1,29},{... | collective-permute-start | bytes 491528 | tf_op jit(solution)/shard_map/ppermute | solution.py:15
  149.7 1.4 collective-permute-start.14
  149.9 3.3 %collective-permute-start.15 = (f32[5,1,1,256]{3,2,1,0:T(1,128)S(1)}, f32[5,1,1,256]{3,2,1,0:T(1,128)S(1)}, u32[]{:S(2)}, u32[]{:S(2)}) collective-permute-start(f32[5,1,1,256]{3,2,1,0:T(1,128)S(1)} %constant_dynamic-update-slice_fusion.202), channel_id=1, source_target_pairs={{0,1},{1,2},{2,3},{3,0},{4,5},{5,6},{6,7},{7,4},{8,9},{9,10},{10,1... | collective-permute-start | bytes 15368 | tf_op jit(solution)/shard_map/ppermute | solution.py:15
  (79 other events, 70.9 us)
where the time goes:
time: 162 us; the launch traced here: 160 us
  local copies, waits for them, and re-layouts  41.6 us (26%)
  blocking collectives  36.8 us (23%)
  waiting for transfers between devices  27.4 us (17%)
  other arithmetic  24.8 us (15%)
  starting transfers between devices  24.6 us (15%)
  between operations  4.38 us (3%)
    psum x1, blocking collectives, global_energy(): return lax.psum(value, ('gz', 'gy'))  36.8 us
    ppermute x16, waiting for transfers between devices, passed_along(): lax.ppermute(array, axis, [(i, (i + by) % count) for i in range(count)])  27.4 us
    ppermute x16, starting transfers between devices, passed_along(): lax.ppermute(array, axis, [(i, (i + by) % count) for i in range(count)])  24.6 us
    unnamed x273, local copies, waits for them, and re-layouts  19 us
    unnamed x91, other arithmetic  8.48 us
    concatenate x12, local copies, waits for them, and re-layouts, stream(): jnp.roll(moved[q], offsets[q][0], axis=2)  7.7 us
  transfers between devices with their start and end apart: 16, of which 12 were waited for; matrix products, arithmetic and copies ran while one was open for 12% of the time, Pallas kernels for 0%

commit v1 on v0

v1 whole, which is shorter than its diff:
```python
import functools

import jax
import jax.numpy as jnp
from jax import lax
from jax.experimental import pallas as pl
from jax.experimental.pallas import tpu as pltpu
from jax.sharding import PartitionSpec as P

STEPS = 2
OMEGA = 0.9
INLET_SPEED = 0.05
HALO = 4


def velocity_table():
    velocities = [(0, 0, 0)]
    for axis in range(3):
        for sign in (1, -1):
            vector = [0, 0, 0]
            vector[axis] = sign
            velocities.append(tuple(vector))
    for first in range(3):
        for second in range(first + 1, 3):
            for sign_a in (1, -1):
                for sign_b in (1, -1):
                    vector = [0, 0, 0]
                    vector[first] = sign_a
                    vector[second] = sign_b
                    velocities.append(tuple(vector))
    weights = [1.0 / 3.0] + [1.0 / 18.0] * 6 + [1.0 / 36.0] * 12
    opposite = [velocities.index(tuple((-e for e in vector))) for vector in velocities]
    return (velocities, weights, opposite)


VEL, WEIGHT, OPP = velocity_table()
Q = len(VEL)
FLAT = [q for q in range(Q) if VEL[q][2] == 0]
RISE = [q for q in range(Q) if VEL[q][2] == 1]
FALL = [q for q in range(Q) if VEL[q][2] == -1]


def inlet_value(q):
    along = VEL[q][2] * INLET_SPEED
    return WEIGHT[q] * (1.0 + 3.0 * along + 4.5 * along * along - 1.5 * INLET_SPEED * INLET_SPEED)


def signed_sum(terms):
    total = None
    for sign, term in terms:
        if total is None:
            total = term if sign > 0 else -term
        else:
            total = total + term if sign > 0 else total - term
    return total


def first_moments(f):
    out = []
    for axis in range(3):
        out.append(signed_sum(sorted(((VEL[q][axis], f[q]) for q in range(Q) if VEL[q][axis]), key=lambda t: -t[0])))
    return out


def dot_c(q, vector):
    return signed_sum(sorted(((VEL[q][a], vector[a]) for a in range(3) if VEL[q][a]), key=lambda t: -t[0]))


def macroscopic(f):
    rho = functools.reduce(lambda a, b: a + b, f)
    mom = first_moments(f)
    inv = 1.0 / rho
    u = [m * inv for m in mom]
    speed = u[0] * u[0] + u[1] * u[1] + u[2] * u[2]
    return rho, u, speed


def collide(f, s, lab):
    rho, u, speed = macroscopic(f)
    rate = jnp.where(lab == 4.0, 1.0, OMEGA)
    inlet = lab == 3.0
    free = 1.0 - s
    keep = free * (1.0 - rate)
    gain = free * rate * rho
    base = 1.0 - 1.5 * speed
    post = [None] * Q
    for q in range(Q):
        o = OPP[q]
        if o < q:
            continue
        scaled = gain * WEIGHT[q]
        if q == 0:
            post[0] = (keep + s) * f[0] + scaled * base
            continue
        along = dot_c(q, u)
        even = scaled * (base + 4.5 * along * along)
        odd = scaled * (3.0 * along)
        post[q] = keep * f[q] + s * f[o] + (even + odd)
        post[o] = keep * f[o] + s * f[q] + (even - odd)
    return [jnp.where(inlet, inlet_value(q), post[q]) for q in range(Q)], rho, u, speed


def pull_back(lam, f, s, lab):
    rho, u, speed = macroscopic(f)
    rate = jnp.where(lab == 4.0, 1.0, OMEGA)
    inlet = lab == 3.0
    lam = [jnp.where(inlet, 0.0, v) for v in lam]
    wsum = [None] * Q
    s0 = WEIGHT[0] * lam[0]
    axis_sum = functools.reduce(lambda a, b: a + b, [lam[q] for q in range(1, 7)])
    diag_sum = functools.reduce(lambda a, b: a + b, [lam[q] for q in range(7, Q)])
    s0 = s0 + WEIGHT[1] * axis_sum + WEIGHT[7] * diag_sum
    s1, tens = [], {}
    for a in range(3):
        near = signed_sum(sorted(((VEL[q][a], lam[q]) for q in range(1, 7) if VEL[q][a]), key=lambda t: -t[0]))
        far = signed_sum(sorted(((VEL[q][a], lam[q]) for q in range(7, Q) if VEL[q][a]), key=lambda t: -t[0]))
        s1.append(WEIGHT[1] * near + WEIGHT[7] * far)
        near = functools.reduce(lambda x, y: x + y, [lam[q] for q in range(1, 7) if VEL[q][a]])
        far = functools.reduce(lambda x, y: x + y, [lam[q] for q in range(7, Q) if VEL[q][a]])
        tens[a, a] = WEIGHT[1] * near + WEIGHT[7] * far
    for a in range(3):
        for b in range(a + 1, 3):
            cross = signed_sum(sorted(((VEL[q][a] * VEL[q][b], lam[q]) for q in range(7, Q) if VEL[q][a] * VEL[q][b]), key=lambda t: -t[0]))
            tens[a, b] = tens[b, a] = WEIGHT[7] * cross
    tu = [tens[a, 0] * u[0] + tens[a, 1] * u[1] + tens[a, 2] * u[2] for a in range(3)]
    utu = tu[0] * u[0] + tu[1] * u[1] + tu[2] * u[2]
    free = 1.0 - s
    by_rho = s0 * (1.0 + 1.5 * speed) - 4.5 * utu
    by_mom = [3.0 * s1[a] + 9.0 * tu[a] - 3.0 * u[a] * s0 for a in range(3)]
    keep = free * (1.0 - rate)
    gain = free * rate
    g0 = gain * by_rho
    gm = [gain * by_mom[a] for a in range(3)]
    out = [None] * Q
    bounce = lam[0] * f[0]
    plain = lam[0] * f[0]
    for q in range(Q):
        o = OPP[q]
        if o < q:
            continue
        if q == 0:
            out[0] = (keep + s) * lam[0] + g0
            continue
        along = dot_c(q, gm)
        out[q] = keep * lam[q] + s * lam[o] + (g0 + along)
        out[o] = keep * lam[o] + s * lam[q] + (g0 - along)
        bounce = bounce + (lam[q] * f[o] + lam[o] * f[q])
        plain = plain + (lam[q] * f[q] + lam[o] * f[o])
    s1u = s1[0] * u[0] + s1[1] * u[1] + s1[2] * u[2]
    at_eq = rho * (s0 * (1.0 - 1.5 * speed) + 3.0 * s1u + 4.5 * utu)
    by_s = bounce - (1.0 - rate) * plain - rate * at_eq
    return out, by_s, rho, u, speed


def shifted(value, dx, dy):
    if dx:
        value = pltpu.roll(value, dx % value.shape[1], 1)
    if dy:
        value = pltpu.roll(value, dy % value.shape[0], 0)
    return value


def tiles(rows):
    return [pl.ds(8 * t, 8) for t in range(rows // 8)]


def kernel_one(pop, frac, lab, from_low, from_high, mid, up, down, field, post):
    own = pop.shape[1]
    rows = own + 2 * HALO
    field[:Q, own : own + HALO, :] = from_high[:Q]
    field[:Q, own + HALO : rows, :] = from_low[:Q]
    mid[9:11, own : own + HALO, :] = from_high[Q : Q + 2]
    mid[9:11, own + HALO : rows, :] = from_low[Q : Q + 2]
    for t in tiles(rows):
        if t.start < own:
            label = lab[t, :].astype(jnp.float32)
            s = frac[t, :]
            f = [pop[q, t, :] for q in range(Q)]
        else:
            label = mid[10, t, :]
            s = mid[9, t, :]
            f = [field[q, t, :] for q in range(Q)]
        s = jnp.where(label == 1.0, s, jnp.where(label == 2.0, 1.0, 0.0))
        mid[9, t, :] = s
        mid[10, t, :] = label
        out, _, _, _ = collide(f, s, label)
        for q in range(Q):
            post[q, t, :] = out[q]
    for ref, group in ((mid, FLAT), (up, RISE), (down, FALL)):
        for i, q in enumerate(group):
            ref[i] = shifted(post[q], VEL[q][0], VEL[q][1])


def gather(q, mid, below, above):
    if VEL[q][2] == 0:
        return mid, FLAT.index(q)
    if VEL[q][2] == 1:
        return below, RISE.index(q)
    return above, FALL.index(q)


def kernel_two(mid, below, above, mom, up, down, part, post):
    rows = mid.shape[1]
    own = rows - 2 * HALO
    total = None
    for t in tiles(rows):
        f = []
        for q in range(Q):
            ref, i = gather(q, mid, below, above)
            f.append(ref[i, t, :])
        s = mid[9, t, :]
        out, rho, u, speed = collide(f, s, mid[10, t, :])
        for q in range(Q):
            post[q, t, :] = out[q]
        if t.start < own:
            e = (1.0 - s) * (rho * speed)
            total = e if total is None else total + e
    part[...] = total
    for ref, group in ((mom, FLAT), (up, RISE), (down, FALL)):
        sums = [None, None, None]
        for q in group:
            cx, cy, _ = VEL[q]
            v = shifted(post[q], cx, cy)
            for k, sign in ((0, 1), (1, cx), (2, cy)):
                if sign:
                    if sums[k] is None:
                        sums[k] = v if sign > 0 else -v
                    else:
                        sums[k] = sums[k] + v if sign > 0 else sums[k] - v
        for k in range(3):
            ref[k] = sums[k]


def kernel_three(mom, below, above, mid, part, mine, up, down, kinetic, out):
    rows = mom.shape[1]
    own = rows - 2 * HALO
    total = part[...]
    for t in tiles(rows):
        rho = mom[0, t, :] + below[0, t, :] + above[0, t, :]
        inv = 1.0 / rho
        ux = (mom[1, t, :] + below[1, t, :] + above[1, t, :]) * inv
        uy = (mom[2, t, :] + below[2, t, :] + above[2, t, :]) * inv
        uz = (below[0, t, :] - above[0, t, :]) * inv
        speed = ux * ux + uy * uy + uz * uz
        free = 1.0 - mid[9, t, :]
        two = 2.0 * free
        ax, ay, az, b = two * ux, two * uy, two * uz, free * speed
        mine[0, t, :] = ax
        mine[1, t, :] = ay
        mine[2, t, :] = b
        down[0, t, :] = ax
        down[1, t, :] = ay
        down[2, t, :] = az - b
        up[0, t, :] = ax
        up[1, t, :] = ay
        up[2, t, :] = -az - b
        if t.start < own:
            k = rho * speed
            kinetic[t, :] = k
            total = total + free * k
    half = total.shape[1] // 2
    out[...] = total[:, :half] + total[:, half:]


def kernel_four(mid, below, above, mine, low, high, kinetic, flat, up, down, lam, adj):
    rows = mid.shape[1]
    own = rows - 2 * HALO
    for q in range(Q):
        cx, cy, cz = VEL[q]
        ref = {0: mine, 1: high, -1: low}[cz]
        value = ref[2]
        if cz == 0:
            value = -value
        if cx:
            value = value + ref[0] if cx > 0 else value - ref[0]
        if cy:
            value = value + ref[1] if cy > 0 else value - ref[1]
        lam[q] = shifted(value, -cx, -cy)
    for t in tiles(rows):
        f = []
        for q in range(Q):
            ref, i = gather(q, mid, below, above)
            f.append(ref[i, t, :])
        s = mid[9, t, :]
        out, by_s, rho, u, speed = pull_back([lam[q, t, :] for q in range(Q)], f, s, mid[10, t, :])
        free = 1.0 - s
        two = [2.0 * free * u[a] for a in range(3)]
        less = free * speed
        for q in range(Q):
            e = out[q] - less
            adj[q, t, :] = e + dot_c(q, two) if q else e
        if t.start < own:
            flat[9, t, :] = by_s - rho * speed - kinetic[t, :]
    for ref, group in ((flat, FLAT), (up, FALL), (down, RISE)):
        for i, q in enumerate(group):
            ref[i] = shifted(adj[q], -VEL[q][0], -VEL[q][1])[:own]


def kernel_five(cells, pop, frac, lab, flat, low, high, energy, sens, out):
    own = pop.shape[1]
    scale = cells / jnp.sum(energy[...], keepdims=True)
    scale = jnp.broadcast_to(scale, (8, pop.shape[2]))
    for t in tiles(own):
        label = lab[t, :].astype(jnp.float32)
        s = jnp.where(label == 1.0, frac[t, :], jnp.where(label == 2.0, 1.0, 0.0))
        lam = []
        for q in range(Q):
            ref, i = {0: (flat, FLAT), 1: (high, RISE), -1: (low, FALL)}[VEL[q][2]]
            lam.append(ref[i.index(q), t, :])
        grads, by_s, _, _, _ = pull_back(lam, [pop[q, t, :] for q in range(Q)], s, label)
        for q in range(Q):
            out[q, t, :] = grads[q] * scale
        sens[t, :] = jnp.where(label == 1.0, (by_s + flat[9, t, :]) * scale, 0.0)


def call(kernel, shapes, scratch, *args):
    return pl.pallas_call(
        kernel,
        out_shape=[jax.ShapeDtypeStruct(s, jnp.float32) for s in shapes],
        in_specs=[pl.BlockSpec(memory_space=pltpu.VMEM)] * len(args),
        out_specs=[pl.BlockSpec(memory_space=pltpu.VMEM)] * len(shapes),
        scratch_shapes=[pltpu.VMEM(s, jnp.float32) for s in scratch],
        compiler_params=pltpu.CompilerParams(vmem_limit_bytes=16 * 1024 * 1024),
    )(*args)


def passed_along(array, axis, by):
    count = lax.axis_size(axis)
    return lax.ppermute(array, axis, [(i, (i + by) % count) for i in range(count)])


def total_over(value, axes):
    for axis in axes:
        count = lax.axis_size(axis)
        if count & (count - 1):
            value = lax.psum(value, axis)
            continue
        step = 1
        while step < count:
            value = value + lax.ppermute(value, axis, [(i, i ^ step) for i in range(count)])
            step *= 2
    return value


def on_device(populations, solid_fraction, labels):
    _, _, own, wide = populations.shape
    rows = own + 2 * HALO
    pop = populations.reshape(Q, own, wide)
    frac = solid_fraction.reshape(own, wide)
    lab = labels.reshape(own, wide)

    def edge(cut):
        return jnp.concatenate([pop[:, cut], frac[None, cut], lab[None, cut].astype(jnp.float32)], axis=0)

    from_low = passed_along(edge(slice(own - HALO, own)), "gy", 1)
    from_high = passed_along(edge(slice(0, HALO)), "gy", -1)
    full = lambda n: (n, rows, wide)
    mid, up, down = call(
        kernel_one, [full(11), full(5), full(5)], [full(Q), full(Q)], pop, frac, lab, from_low, from_high
    )
    below, above = passed_along(up, "gz", 1), passed_along(down, "gz", -1)
    mom, up, down, part = call(
        kernel_two, [full(3), full(3), full(3), (8, wide)], [full(Q)], mid, below, above
    )
    low, high = passed_along(up, "gz", 1), passed_along(down, "gz", -1)
    mine, up, down, kinetic, energy = call(
        kernel_three, [full(3), full(3), full(3), (own, wide), (8, wide // 2)], [], mom, low, high, mid, part
    )
    energy = total_over(energy, ("gy", "gz"))
    low, high = passed_along(up, "gz", 1), passed_along(down, "gz", -1)
    less = lambda n: (n, own, wide)
    flat, up, down = call(
        kernel_four, [less(10), less(5), less(5)], [full(Q), full(Q)], mid, below, above, mine, low, high, kinetic
    )
    low, high = passed_along(up, "gz", 1), passed_along(down, "gz", -1)
    cells = float(STEPS * own * wide * populations.shape[1] * lax.axis_size("gz") * lax.axis_size("gy"))
    sens, out = call(
        functools.partial(kernel_five, cells), [(own, wide), less(Q)], [], pop, frac, lab, flat, low, high, energy
    )
    return sens.reshape(solid_fraction.shape), out.reshape(populations.shape)


def solution(mesh):
    in_specs = (P(None, "gz", "gy", None), P("gz", "gy", None), P("gz", "gy", None))
    out_specs = (P("gz", "gy", None), P(None, "gz", "gy", None))
    return jax.shard_map(on_device, mesh=mesh, in_specs=in_specs, out_specs=out_specs, check_vma=False)
```

time: 162 us -> 64.6 us (0.40); the launches traced: 160 us -> 64.3 us
  local copies, waits for them, and re-layouts: 41.6 us -> 1.81 us
  blocking collectives: 36.8 us -> 0 us
  other arithmetic: 24.8 us -> 0.78 us
  waiting for transfers between devices: 27.4 us -> 34.9 us
  between operations: 4.38 us -> 0.71 us
  Pallas kernels: 0 us -> 3.19 us
  starting transfers between devices: 24.6 us -> 22.9 us
    psum x1 -> x0, blocking collectives: 36.8 us -> none  [global_energy(): return lax.psum(value, ('gz', 'gy'))]
    unnamed x273 -> x6, local copies, waits for them, and re-layouts: 19 us -> 0.01 us
    ppermute x0 -> x5, waiting for transfers between devices: none -> 15.2 us  [total_over(): lax.ppermute(value, axis, [(i, i ^ step) for i in range(count)])]
    concatenate x22 -> x0, local copies, waits for them, and re-layouts: 12.7 us -> none  [the longest x12 7.7 us: stream(): jnp.roll(moved[q], offsets[q][0], axis=2)]
    unnamed x91 -> x0, other arithmetic: 8.48 us -> none
    ppermute x16 -> x10, waiting for transfers between devices: 27.4 us -> 19.7 us  [passed_along(): lax.ppermute(array, axis, [(i, (i + by) % count) for i in range(count)])]
    slice x44 -> x2, local copies, waits for them, and re-layouts: 5.83 us -> 1.8 us  [the longest x1 1.02 us: edge(): pop[:, cut]]
    squeeze x19 -> x0, local copies, waits for them, and re-layouts: 3.99 us -> none  [the longest x6 1.62 us: stream(): from_above[lower_z.index(q)]]
  transfers between devices with their start and end apart: 16 -> 15, of which waited for: 12 -> 13; matrix products, arithmetic and copies ran while one was open for 12% -> 0% of each run, Pallas kernels for 0% -> 0%
where the time goes in v1:
time: 64.6 us; the launch traced here: 64.3 us
  waiting for transfers between devices  34.9 us (54%)
  starting transfers between devices  22.9 us (35%)
  Pallas kernels  3.19 us (5%)
  local copies, waits for them, and re-layouts  1.81 us (3%)
  other arithmetic  0.78 us (1%)
  between operations  0.71 us (1%)
    ppermute x10, starting transfers between devices, passed_along(): lax.ppermute(array, axis, [(i, (i + by) % count) for i in range(count)])  21.6 us
    ppermute x10, waiting for transfers between devices, passed_along(): lax.ppermute(array, axis, [(i, (i + by) % count) for i in range(count)])  19.7 us
    ppermute x5, waiting for transfers between devices, total_over(): lax.ppermute(value, axis, [(i, i ^ step) for i in range(count)])  15.2 us
    pallas_call x5, Pallas kernels, call(): pl.pallas_call(kernel, out_shape=[jax.ShapeDtypeStruct(s, jnp.float32) fo...  3.19 us
  transfers between devices with their start and end apart: 15, of which 13 were waited for; matrix products, arithmetic and copies ran while one was open for 0% of the time, Pallas kernels for 0%

profile of v1, /device:TPU:0, one launch (start us, length us, event | category | flops | bytes accessed | tf_op | source)
XLA Modules:
  0.0 64.3 jit_solution(18064728007189533105)
XLA Ops:
  0.6 0.8 %fusion.1 = (f32[1,4,256]{2,1,0:T(4,128)S(1)}, f32[1,4,256]{2,1,0:T(4,128)S(1)}) fusion(f32[1,32,256]{2,1,0:T(8,128)} %param.4), kind=kLoop, calls=%fused_computation.5 | loop fusion | bytes 16384 | tf_op jit(solution)/shard_map/slice | solution.py:353
  1.4 0.7 %slice_convert_fusion = (f32[1,4,256]{2,1,0:T(4,128)S(1)}, f32[1,4,256]{2,1,0:T(4,128)S(1)}) fusion(s32[1,32,256]{2,1,0:T(8,128)} %param.5), kind=kLoop, calls=%fused_computation.2 | loop fusion | flops 2048 | bytes 16384 | tf_op jit(solution)/shard_map/convert_element_type | solution.py:353
  2.1 1.0 %fusion = (f32[19,4,256]{2,1,0:T(4,128)S(1)}, f32[19,4,256]{2,1,0:T(4,128)S(1)}) fusion(f32[19,32,256]{2,1,0:T(8,128)} %bitcast.7), kind=kLoop, calls=%fused_computation.4 | loop fusion | bytes 311296 | tf_op jit(solution)/shard_map/slice | solution.py:353
  3.2 0.5 collective-permute-start
  3.7 2.0 %collective-permute-start.1 = (f32[21,4,256]{2,1,0:T(4,128)S(1)}, f32[21,4,256]{2,1,0:T(4,128)S(1)}, u32[]{:S(2)}, u32[]{:S(2)}) collective-permute-start(f32[21,4,256]{2,1,0:T(4,128)S(1)} %pad_maximum_fusion.1), channel_id=1, source_target_pairs={{0,3},{1,0},{2,1},{3,2},{4,7},{5,4},{6,5},{7,6},{8,11},{9,8},{10,9... | collective-permute-start | bytes 258056 | tf_op jit(solution)/shard_map/ppermute | solution.py:329
  5.8 2.1 %collective-permute-done.from_low = f32[21,4,256]{2,1,0:T(4,128)S(1)} collective-permute-done((f32[21,4,256]{2,1,0:T(4,128)S(1)}, f32[21,4,256]{2,1,0:T(4,128)S(1)}, u32[]{:S(2)}, u32[]{:S(2)}) %collective-permute-start) | collective-permute-done | bytes 86048 | tf_op jit(solution)/shard_map/ppermute | solution.py:329
  7.8 0.7 %collective-permute-done.1.from_high = f32[21,4,256]{2,1,0:T(4,128)S(1)} collective-permute-done((f32[21,4,256]{2,1,0:T(4,128)S(1)}, f32[21,4,256]{2,1,0:T(4,128)S(1)}, u32[]{:S(2)}, u32[]{:S(2)}) %collective-permute-start.1) | collective-permute-done | bytes 86048 | tf_op jit(solution)/shard_map/ppermute | solution.py:329
  8.6 0.5 shard_map.50
  9.1 1.6 %collective-permute-start.2 = (f32[5,40,256]{2,1,0:T(8,128)S(1)}, f32[5,40,256]{2,1,0:T(8,128)S(1)}, u32[]{:S(2)}, u32[]{:S(2)}) collective-permute-start(f32[5,40,256]{2,1,0:T(8,128)S(1)} %get-tuple-element.20), channel_id=1, source_target_pairs={{0,4},{4,8},{8,12},{12,16},{16,20},{20,24},{24,28},{28,0},{1,5},{5... | collective-permute-start | bytes 614408 | tf_op jit(solution)/shard_map/ppermute | solution.py:329
  10.7 3.2 %collective-permute-start.3 = (f32[5,40,256]{2,1,0:T(8,128)S(1)}, f32[5,40,256]{2,1,0:T(8,128)S(1)}, u32[]{:S(2)}, u32[]{:S(2)}) collective-permute-start(f32[5,40,256]{2,1,0:T(8,128)S(1)} %get-tuple-element.21), channel_id=1, source_target_pairs={{0,28},{4,0},{8,4},{12,8},{16,12},{20,16},{24,20},{28,24},{1,29},{... | collective-permute-start | bytes 614408 | tf_op jit(solution)/shard_map/ppermute | solution.py:329
  13.9 6.0 %collective-permute-done.2.below = f32[5,40,256]{2,1,0:T(8,128)S(1)} collective-permute-done((f32[5,40,256]{2,1,0:T(8,128)S(1)}, f32[5,40,256]{2,1,0:T(8,128)S(1)}, u32[]{:S(2)}, u32[]{:S(2)}) %collective-permute-start.2) | collective-permute-done | bytes 204832 | tf_op jit(solution)/shard_map/ppermute | solution.py:329
  19.8 2.8 %collective-permute-done.3.above = f32[5,40,256]{2,1,0:T(8,128)S(1)} collective-permute-done((f32[5,40,256]{2,1,0:T(8,128)S(1)}, f32[5,40,256]{2,1,0:T(8,128)S(1)}, u32[]{:S(2)}, u32[]{:S(2)}) %collective-permute-start.3) | collective-permute-done | bytes 204832 | tf_op jit(solution)/shard_map/ppermute | solution.py:329
  22.6 0.5 shard_map.51
  23.1 0.1 collective-permute-start.4
  23.2 4.7 %collective-permute-start.5 = (f32[3,40,256]{2,1,0:T(8,128)S(1)}, f32[3,40,256]{2,1,0:T(8,128)S(1)}, u32[]{:S(2)}, u32[]{:S(2)}) collective-permute-start(f32[3,40,256]{2,1,0:T(8,128)S(1)} %get-tuple-element.24), channel_id=1, source_target_pairs={{0,28},{4,0},{8,4},{12,8},{16,12},{20,16},{24,20},{28,24},{1,29},{... | collective-permute-start | bytes 368648 | tf_op jit(solution)/shard_map/ppermute | solution.py:329
  27.9 3.5 %collective-permute-done.4.below = f32[3,40,256]{2,1,0:T(8,128)S(1)} collective-permute-done((f32[3,40,256]{2,1,0:T(8,128)S(1)}, f32[3,40,256]{2,1,0:T(8,128)S(1)}, u32[]{:S(2)}, u32[]{:S(2)}) %collective-permute-start.4) | collective-permute-done | bytes 122912 | tf_op jit(solution)/shard_map/ppermute | solution.py:329
  31.4 0.5 collective-permute-done.5.above
  31.9 0.1 shard_map.52
  32.0 0.1 collective-permute-start.6
  32.0 4.7 %collective-permute-start.7 = (f32[3,40,256]{2,1,0:T(8,128)S(1)}, f32[3,40,256]{2,1,0:T(8,128)S(1)}, u32[]{:S(2)}, u32[]{:S(2)}) collective-permute-start(f32[3,40,256]{2,1,0:T(8,128)S(1)} %get-tuple-element.28), channel_id=1, source_target_pairs={{0,28},{4,0},{8,4},{12,8},{16,12},{20,16},{24,20},{28,24},{1,29},{... | collective-permute-start | bytes 368648 | tf_op jit(solution)/shard_map/ppermute | solution.py:329
  36.7 3.0 %collective-permute-done.6.low = f32[3,40,256]{2,1,0:T(8,128)S(1)} collective-permute-done((f32[3,40,256]{2,1,0:T(8,128)S(1)}, f32[3,40,256]{2,1,0:T(8,128)S(1)}, u32[]{:S(2)}, u32[]{:S(2)}) %collective-permute-start.6) | collective-permute-done | bytes 122912 | tf_op jit(solution)/shard_map/ppermute | solution.py:329
  39.7 1.1 %collective-permute-done.7.high = f32[3,40,256]{2,1,0:T(8,128)S(1)} collective-permute-done((f32[3,40,256]{2,1,0:T(8,128)S(1)}, f32[3,40,256]{2,1,0:T(8,128)S(1)}, u32[]{:S(2)}, u32[]{:S(2)}) %collective-permute-start.7) | collective-permute-done | bytes 122912 | tf_op jit(solution)/shard_map/ppermute | solution.py:329
  40.8 0.8 %shard_map.53 = (f32[10,32,256]{2,1,0:T(8,128)S(1)}, f32[5,32,256]{2,1,0:T(8,128)S(1)}, f32[5,32,256]{2,1,0:T(8,128)S(1)}) custom-call(f32[11,40,256]{2,1,0:T(8,128)S(1)} %get-tuple-element.19.mid, f32[5,40,256]{2,1,0:T(8,128)S(1)} %collective-permute-done.2.below, f32[5,40,256]{2,1,0:T(8,128)S(1)} %collective-permute-done.3.above, ...), custom_call_target="tpu_custom_call" | custom-call | tf_op jit(solution)/shard_map/pallas_call | solution.py:317
  41.6 0.1 collective-permute-start.8
  41.7 4.7 %collective-permute-start.9 = (f32[5,32,256]{2,1,0:T(8,128)S(1)}, f32[5,32,256]{2,1,0:T(8,128)S(1)}, u32[]{:S(2)}, u32[]{:S(2)}) collective-permute-start(f32[5,32,256]{2,1,0:T(8,128)S(1)} %get-tuple-element.32), channel_id=1, source_target_pairs={{0,28},{4,0},{8,4},{12,8},{16,12},{20,16},{24,20},{28,24},{1,29},{... | collective-permute-start | bytes 491528 | tf_op jit(solution)/shard_map/ppermute | solution.py:329
  46.4 1.2 %collective-permute-done.10 = f32[8,128]{1,0:T(8,128)S(1)} collective-permute-done((f32[8,128]{1,0:T(8,128)S(1)}, f32[8,128]{1,0:T(8,128)S(1)}, u32[]{:S(2)}, u32[]{:S(2)}) %collective-permute-start.10) | collective-permute-done | bytes 4128 | tf_op jit(solution)/shard_map/ppermute | solution.py:340
  47.6 1.3 %collective-permute-start.11 = (f32[8,128]{1,0:T(8,128)S(1)}, f32[8,128]{1,0:T(8,128)S(1)}, u32[]{:S(2)}, u32[]{:S(2)}) collective-permute-start(f32[8,128]{1,0:T(8,128)S(1)} %add.15), channel_id=1, source_target_pairs={{0,2},{1,3},{2,0},{3,1},{4,6},{5,7},{6,4},{7,5},{8,10},{9,11},{10,... | collective-permute-start | bytes 12296 | tf_op jit(solution)/shard_map/ppermute | solution.py:340
  48.8 2.3 %collective-permute-done.11 = f32[8,128]{1,0:T(8,128)S(1)} collective-permute-done((f32[8,128]{1,0:T(8,128)S(1)}, f32[8,128]{1,0:T(8,128)S(1)}, u32[]{:S(2)}, u32[]{:S(2)}) %collective-permute-start.11) | collective-permute-done | bytes 4128 | tf_op jit(solution)/shard_map/ppermute | solution.py:340
  51.2 3.6 %collective-permute-done.12 = f32[8,128]{1,0:T(8,128)S(1)} collective-permute-done((f32[8,128]{1,0:T(8,128)S(1)}, f32[8,128]{1,0:T(8,128)S(1)}, u32[]{:S(2)}, u32[]{:S(2)}) %collective-permute-start.12) | collective-permute-done | bytes 4128 | tf_op jit(solution)/shard_map/ppermute | solution.py:340
  54.8 3.6 %collective-permute-done.13 = f32[8,128]{1,0:T(8,128)S(1)} collective-permute-done((f32[8,128]{1,0:T(8,128)S(1)}, f32[8,128]{1,0:T(8,128)S(1)}, u32[]{:S(2)}, u32[]{:S(2)}) %collective-permute-start.13) | collective-permute-done | bytes 4128 | tf_op jit(solution)/shard_map/ppermute | solution.py:340
  58.4 4.5 %collective-permute-done.14 = f32[8,128]{1,0:T(8,128)S(1)} collective-permute-done((f32[8,128]{1,0:T(8,128)S(1)}, f32[8,128]{1,0:T(8,128)S(1)}, u32[]{:S(2)}, u32[]{:S(2)}) %collective-permute-start.14) | collective-permute-done | bytes 4128 | tf_op jit(solution)/shard_map/ppermute | solution.py:340
  62.9 1.3 %shard_map.54 = (f32[32,256]{1,0:T(8,128)}, f32[19,32,256]{2,1,0:T(8,128)}) custom-call(f32[19,32,256]{2,1,0:T(8,128)S(1)} %bitcast.9, f32[32,256]{1,0:T(8,128)S(1)} %bitcast.11, s32[32,256]{1,0:T(8,128)S(1)} %bitcast.13, f32[10,32,256]{2,1,0:T(8,128)S(1)} %get-tuple-element.30.flat, f32[5,32,256]{2,1,0:T(8,128)S(1)} %collective-permute-done.8.low, ...), custom_call_target="tpu_custom_call" | custom-call | tf_op jit(solution)/shard_map/pallas_call | solution.py:317
  (19 shorter events, 0.1 us)
Async XLA Ops:
  0.6 7.9 %copy-start = (f32[19,1,32,256]{3,2,1,0:T(8,128)S(1)}, f32[19,1,32,256]{3,2,1,0:T(8,128)}, u32[]{:S(2)}) copy-start(f32[19,1,32,256]{3,2,1,0:T(8,128)} %param.3) | copy-start | bytes 1867780
  3.2 4.6 %collective-permute-start = (f32[21,4,256]{2,1,0:T(4,128)S(1)}, f32[21,4,256]{2,1,0:T(4,128)S(1)}, u32[]{:S(2)}, u32[]{:S(2)}) collective-permute-start(f32[21,4,256]{2,1,0:T(4,128)S(1)} %pad_maximum_fusion), channel_id=1, source_target_pairs={{0,1},{1,2},{2,3},{3,0},{4,5},{5,6},{6,7},{7,4},{8,9},{9,10},{10,1... | collective-permute-start | bytes 258056 | tf_op jit(solution)/shard_map/ppermute | solution.py:329
  3.7 4.9 %copy-start.1 = (f32[1,32,256]{2,1,0:T(8,128)S(1)}, f32[1,32,256]{2,1,0:T(8,128)}, u32[]{:S(2)}) copy-start(f32[1,32,256]{2,1,0:T(8,128)} %param.4) | copy-start | bytes 98308
  3.7 4.9 %copy-start.2 = (s32[1,32,256]{2,1,0:T(8,128)S(1)}, s32[1,32,256]{2,1,0:T(8,128)}, u32[]{:S(2)}) copy-start(s32[1,32,256]{2,1,0:T(8,128)} %param.5) | copy-start | bytes 98308
  3.7 4.8 %collective-permute-start.1 = (f32[21,4,256]{2,1,0:T(4,128)S(1)}, f32[21,4,256]{2,1,0:T(4,128)S(1)}, u32[]{:S(2)}, u32[]{:S(2)}) collective-permute-start(f32[21,4,256]{2,1,0:T(4,128)S(1)} %pad_maximum_fusion.1), channel_id=1, source_target_pairs={{0,3},{1,0},{2,1},{3,2},{4,7},{5,4},{6,5},{7,6},{8,11},{9,8},{10,9... | collective-permute-start | bytes 258056 | tf_op jit(solution)/shard_map/ppermute | solution.py:329
  9.1 10.8 %collective-permute-start.2 = (f32[5,40,256]{2,1,0:T(8,128)S(1)}, f32[5,40,256]{2,1,0:T(8,128)S(1)}, u32[]{:S(2)}, u32[]{:S(2)}) collective-permute-start(f32[5,40,256]{2,1,0:T(8,128)S(1)} %get-tuple-element.20), channel_id=1, source_target_pairs={{0,4},{4,8},{8,12},{12,16},{16,20},{20,24},{24,28},{28,0},{1,5},{5... | collective-permute-start | bytes 614408 | tf_op jit(solution)/shard_map/ppermute | solution.py:329
  10.7 12.0 %collective-permute-start.3 = (f32[5,40,256]{2,1,0:T(8,128)S(1)}, f32[5,40,256]{2,1,0:T(8,128)S(1)}, u32[]{:S(2)}, u32[]{:S(2)}) collective-permute-start(f32[5,40,256]{2,1,0:T(8,128)S(1)} %get-tuple-element.21), channel_id=1, source_target_pairs={{0,28},{4,0},{8,4},{12,8},{16,12},{20,16},{24,20},{28,24},{1,29},{... | collective-permute-start | bytes 614408 | tf_op jit(solution)/shard_map/ppermute | solution.py:329
  23.1 8.3 %collective-permute-start.4 = (f32[3,40,256]{2,1,0:T(8,128)S(1)}, f32[3,40,256]{2,1,0:T(8,128)S(1)}, u32[]{:S(2)}, u32[]{:S(2)}) collective-permute-start(f32[3,40,256]{2,1,0:T(8,128)S(1)} %get-tuple-element.23), channel_id=1, source_target_pairs={{0,4},{4,8},{8,12},{12,16},{16,20},{20,24},{24,28},{28,0},{1,5},{5... | collective-permute-start | bytes 368648 | tf_op jit(solution)/shard_map/ppermute | solution.py:329
  23.2 8.7 %collective-permute-start.5 = (f32[3,40,256]{2,1,0:T(8,128)S(1)}, f32[3,40,256]{2,1,0:T(8,128)S(1)}, u32[]{:S(2)}, u32[]{:S(2)}) collective-permute-start(f32[3,40,256]{2,1,0:T(8,128)S(1)} %get-tuple-element.24), channel_id=1, source_target_pairs={{0,28},{4,0},{8,4},{12,8},{16,12},{20,16},{24,20},{28,24},{1,29},{... | collective-permute-start | bytes 368648 | tf_op jit(solution)/shard_map/ppermute | solution.py:329
  32.0 7.7 %collective-permute-start.6 = (f32[3,40,256]{2,1,0:T(8,128)S(1)}, f32[3,40,256]{2,1,0:T(8,128)S(1)}, u32[]{:S(2)}, u32[]{:S(2)}) collective-permute-start(f32[3,40,256]{2,1,0:T(8,128)S(1)} %get-tuple-element.27), channel_id=1, source_target_pairs={{0,4},{4,8},{8,12},{12,16},{16,20},{20,24},{24,28},{28,0},{1,5},{5... | collective-permute-start | bytes 368648 | tf_op jit(solution)/shard_map/ppermute | solution.py:329
  32.0 8.8 %collective-permute-start.7 = (f32[3,40,256]{2,1,0:T(8,128)S(1)}, f32[3,40,256]{2,1,0:T(8,128)S(1)}, u32[]{:S(2)}, u32[]{:S(2)}) collective-permute-start(f32[3,40,256]{2,1,0:T(8,128)S(1)} %get-tuple-element.28), channel_id=1, source_target_pairs={{0,28},{4,0},{8,4},{12,8},{16,12},{20,16},{24,20},{28,24},{1,29},{... | collective-permute-start | bytes 368648 | tf_op jit(solution)/shard_map/ppermute | solution.py:329
  41.6 21.3 %collective-permute-start.8 = (f32[5,32,256]{2,1,0:T(8,128)S(1)}, f32[5,32,256]{2,1,0:T(8,128)S(1)}, u32[]{:S(2)}, u32[]{:S(2)}) collective-permute-start(f32[5,32,256]{2,1,0:T(8,128)S(1)} %get-tuple-element.31), channel_id=1, source_target_pairs={{0,4},{4,8},{8,12},{12,16},{16,20},{20,24},{24,28},{28,0},{1,5},{5... | collective-permute-start | bytes 491528 | tf_op jit(solution)/shard_map/ppermute | solution.py:329
  41.7 21.2 %collective-permute-start.9 = (f32[5,32,256]{2,1,0:T(8,128)S(1)}, f32[5,32,256]{2,1,0:T(8,128)S(1)}, u32[]{:S(2)}, u32[]{:S(2)}) collective-permute-start(f32[5,32,256]{2,1,0:T(8,128)S(1)} %get-tuple-element.32), channel_id=1, source_target_pairs={{0,28},{4,0},{8,4},{12,8},{16,12},{20,16},{24,20},{28,24},{1,29},{... | collective-permute-start | bytes 491528 | tf_op jit(solution)/shard_map/ppermute | solution.py:329
  46.4 1.2 %collective-permute-start.10 = (f32[8,128]{1,0:T(8,128)S(1)}, f32[8,128]{1,0:T(8,128)S(1)}, u32[]{:S(2)}, u32[]{:S(2)}) collective-permute-start(f32[8,128]{1,0:T(8,128)S(1)} %get-tuple-element.33), channel_id=1, source_target_pairs={{0,1},{1,0},{2,3},{3,2},{4,5},{5,4},{6,7},{7,6},{8,9},{9,8},{10,11... | collective-permute-start | bytes 12296 | tf_op jit(solution)/shard_map/ppermute | solution.py:340
  47.6 3.6 %collective-permute-start.11 = (f32[8,128]{1,0:T(8,128)S(1)}, f32[8,128]{1,0:T(8,128)S(1)}, u32[]{:S(2)}, u32[]{:S(2)}) collective-permute-start(f32[8,128]{1,0:T(8,128)S(1)} %add.15), channel_id=1, source_target_pairs={{0,2},{1,3},{2,0},{3,1},{4,6},{5,7},{6,4},{7,5},{8,10},{9,11},{10,... | collective-permute-start | bytes 12296 | tf_op jit(solution)/shard_map/ppermute | solution.py:340
  51.2 3.6 %collective-permute-start.12 = (f32[8,128]{1,0:T(8,128)S(1)}, f32[8,128]{1,0:T(8,128)S(1)}, u32[]{:S(2)}, u32[]{:S(2)}) collective-permute-start(f32[8,128]{1,0:T(8,128)S(1)} %add.16), channel_id=1, source_target_pairs={{0,4},{4,0},{8,12},{12,8},{16,20},{20,16},{24,28},{28,24},{1,5},{5... | collective-permute-start | bytes 12296 | tf_op jit(solution)/shard_map/ppermute | solution.py:340
  54.8 3.6 %collective-permute-start.13 = (f32[8,128]{1,0:T(8,128)S(1)}, f32[8,128]{1,0:T(8,128)S(1)}, u32[]{:S(2)}, u32[]{:S(2)}) collective-permute-start(f32[8,128]{1,0:T(8,128)S(1)} %add.17), channel_id=1, source_target_pairs={{0,8},{4,12},{8,0},{12,4},{16,24},{20,28},{24,16},{28,20},{1,9},{5... | collective-permute-start | bytes 12296 | tf_op jit(solution)/shard_map/ppermute | solution.py:340
  58.4 4.5 %collective-permute-start.14 = (f32[8,128]{1,0:T(8,128)S(1)}, f32[8,128]{1,0:T(8,128)S(1)}, u32[]{:S(2)}, u32[]{:S(2)}) collective-permute-start(f32[8,128]{1,0:T(8,128)S(1)} %add.18), channel_id=1, source_target_pairs={{0,16},{4,20},{8,24},{12,28},{16,0},{20,4},{24,8},{28,12},{1,17},{... | collective-permute-start | bytes 12296 | tf_op jit(solution)/shard_map/ppermute | solution.py:340

commit v2 on v1

--- a/solution.py
+++ b/solution.py
@@ -11,6 +11,9 @@
 OMEGA = 0.9
 INLET_SPEED = 0.05
 HALO = 4
+WORK = 20_000_000
+EARLY = 2
+ALPHA, BETA = 1, 0
 
 
 def velocity_table():
@@ -164,59 +167,79 @@
     return [pl.ds(8 * t, 8) for t in range(rows // 8)]
 
 
-def kernel_one(pop, frac, lab, from_low, from_high, mid, up, down, field, post):
+def pick(odd, first, second):
+    return jnp.where(odd, second, first)
+
+
+def write_pair(odd, to_pair, to_other, rising, falling):
+    to_pair[...] = pick(odd, rising, falling)
+    to_other[...] = pick(odd, falling, rising)
+
+
+def kernel_pack(odd_y, pop, cell, edge_pair, edge_other):
     own = pop.shape[1]
-    rows = own + 2 * HALO
-    field[:Q, own : own + HALO, :] = from_high[:Q]
-    field[:Q, own + HALO : rows, :] = from_low[:Q]
-    mid[9:11, own : own + HALO, :] = from_high[Q : Q + 2]
-    mid[9:11, own + HALO : rows, :] = from_low[Q : Q + 2]
+    oy = odd_y[0] == 1
+    for i in range(Q + 2):
+        ref = pop.at[i] if i < Q else cell.at[i - Q]
+        write_pair(oy, edge_pair.at[i], edge_other.at[i], ref[own - HALO : own, :], ref[0:HALO, :])
+
+
+def kernel_one(odd_z, odd_y, pop, cell, edge_pair, edge_other, mid, pair, other, tile, post):
+    own = pop.shape[1]
+    rows = mid.shape[1]
+    oz, oy = odd_z[0] == 1, odd_y[0] == 1
+    for i in range(Q + 2):
+        a, b = edge_pair[i], edge_other[i]
+        tile[i, :HALO, :] = pick(oy, a, b)
+        tile[i, HALO:, :] = pick(oy, b, a)
     for t in tiles(rows):
         if t.start < own:
-            label = lab[t, :].astype(jnp.float32)
-            s = frac[t, :]
             f = [pop[q, t, :] for q in range(Q)]
+            s, label = cell[0, t, :], cell[1, t, :]
         else:
-            label = mid[10, t, :]
-            s = mid[9, t, :]
-            f = [field[q, t, :] for q in range(Q)]
-        s = jnp.where(label == 1.0, s, jnp.where(label == 2.0, 1.0, 0.0))
-        mid[9, t, :] = s
-        mid[10, t, :] = label
+            f = [tile[q] for q in range(Q)]
+            s, label = tile[Q], tile[Q + 1]
+        mid[len(FLAT), t, :] = s
+        mid[len(FLAT) + 1, t, :] = label
         out, _, _, _ = collide(f, s, label)
         for q in range(Q):
             post[q, t, :] = out[q]
-    for ref, group in ((mid, FLAT), (up, RISE), (down, FALL)):
-        for i, q in enumerate(group):
-            ref[i] = shifted(post[q], VEL[q][0], VEL[q][1])
-
-
-def gather(q, mid, below, above):
-    if VEL[q][2] == 0:
-        return mid, FLAT.index(q)
-    if VEL[q][2] == 1:
-        return below, RISE.index(q)
-    return above, FALL.index(q)
-
-
-def kernel_two(mid, below, above, mom, up, down, part, post):
-    rows = mid.shape[1]
+    moved = lambda q: shifted(post[q], VEL[q][0], VEL[q][1])
+    for i, q in enumerate(FLAT):
+        mid[i] = moved(q)
+    for i in range(len(RISE)):
+        write_pair(oz, pair.at[i], other.at[i], moved(RISE[i]), moved(FALL[i]))
+
+
+def kernel_two(odd_p, mid, pair, other, field, mom, to_pair, to_other, part, post):
+    rows = field.shape[1]
     own = rows - 2 * HALO
+    odd = odd_p[0] == 1
+    for q in range(Q):
+        cz = VEL[q][2]
+        if cz == 0:
+            value = mid[FLAT.index(q)]
+        elif cz == 1:
+            i = RISE.index(q)
+            value = pick(odd, other[i], pair[i])
+        else:
+            i = FALL.index(q)
+            value = pick(odd, pair[i], other[i])
+        field[q] = value
+    for i in (0, 1):
+        field[Q + i] = mid[len(FLAT) + i]
     total = None
     for t in tiles(rows):
-        f = []
-        for q in range(Q):
-            ref, i = gather(q, mid, below, above)
-            f.append(ref[i, t, :])
-        s = mid[9, t, :]
-        out, rho, u, speed = collide(f, s, mid[10, t, :])
+        s = field[Q, t, :]
+        out, rho, u, speed = collide([field[q, t, :] for q in range(Q)], s, field[Q + 1, t, :])
         for q in range(Q):
             post[q, t, :] = out[q]
         if t.start < own:
             e = (1.0 - s) * (rho * speed)
             total = e if total is None else total + e
     part[...] = total
-    for ref, group in ((mom, FLAT), (up, RISE), (down, FALL)):
+    results = []
+    for group in (FLAT, RISE, FALL):
         sums = [None, None, None]
         for q in group:
             cx, cy, _ = VEL[q]
@@ -227,33 +250,37 @@
                         sums[k] = v if sign > 0 else -v
                     else:
                         sums[k] = sums[k] + v if sign > 0 else sums[k] - v
-        for k in range(3):
-            ref[k] = sums[k]
-
-
-def kernel_three(mom, below, above, mid, part, mine, up, down, kinetic, out):
+        results.append(sums)
+    for k in range(3):
+        mom[k] = results[0][k]
+        write_pair(odd, to_pair.at[k], to_other.at[k], results[1][k], results[2][k])
+
+
+def kernel_three(odd_p, mom, pair, other, field, part, mine, to_pair, to_other, kinetic, out):
     rows = mom.shape[1]
     own = rows - 2 * HALO
+    odd = odd_p[0] == 1
     total = part[...]
     for t in tiles(rows):
-        rho = mom[0, t, :] + below[0, t, :] + above[0, t, :]
+        below = [pick(odd, other[k, t, :], pair[k, t, :]) for k in range(3)]
+        above = [pick(odd, pair[k, t, :], other[k, t, :]) for k in range(3)]
+        rho = mom[0, t, :] + below[0] + above[0]
         inv = 1.0 / rho
-        ux = (mom[1, t, :] + below[1, t, :] + above[1, t, :]) * inv
-        uy = (mom[2, t, :] + below[2, t, :] + above[2, t, :]) * inv
-        uz = (below[0, t, :] - above[0, t, :]) * inv
+        ux = (mom[1, t, :] + below[1] + above[1]) * inv
+        uy = (mom[2, t, :] + below[2] + above[2]) * inv
+        uz = (below[0] - above[0]) * inv
         speed = ux * ux + uy * uy + uz * uz
-        free = 1.0 - mid[9, t, :]
+        free = 1.0 - field[Q, t, :]
         two = 2.0 * free
         ax, ay, az, b = two * ux, two * uy, two * uz, free * speed
         mine[0, t, :] = ax
         mine[1, t, :] = ay
         mine[2, t, :] = b
-        down[0, t, :] = ax
-        down[1, t, :] = ay
-        down[2, t, :] = az - b
-        up[0, t, :] = ax
-        up[1, t, :] = ay
-        up[2, t, :] = -az - b
+        to_pair[0, t, :] = ax
+        to_pair[1, t, :] = ay
+        to_other[0, t, :] = ax
+        to_other[1, t, :] = ay
+        write_pair(odd, to_pair.at[2, t, :], to_other.at[2, t, :], -az - b, az - b)
         if t.start < own:
             k = rho * speed
             kinetic[t, :] = k
@@ -262,9 +289,12 @@
     out[...] = total[:, :half] + total[:, half:]
 
 
-def kernel_four(mid, below, above, mine, low, high, kinetic, flat, up, down, lam, adj):
-    rows = mid.shape[1]
+def kernel_four(odd_p, field, mine, pair, other, kinetic, energy, flat, to_pair, to_other, lam, adj):
+    rows = field.shape[1]
     own = rows - 2 * HALO
+    odd = odd_p[0] == 1
+    low = [pick(odd, other[k], pair[k]) for k in range(3)]
+    high = [pick(odd, pair[k], other[k]) for k in range(3)]
     for q in range(Q):
         cx, cy, cz = VEL[q]
         ref = {0: mine, 1: high, -1: low}[cz]
@@ -277,12 +307,10 @@
             value = value + ref[1] if cy > 0 else value - ref[1]
         lam[q] = shifted(value, -cx, -cy)
     for t in tiles(rows):
-        f = []
-        for q in range(Q):
-            ref, i = gather(q, mid, below, above)
-            f.append(ref[i, t, :])
-        s = mid[9, t, :]
-        out, by_s, rho, u, speed = pull_back([lam[q, t, :] for q in range(Q)], f, s, mid[10, t, :])
+        s = field[Q, t, :]
+        out, by_s, rho, u, speed = pull_back(
+            [lam[q, t, :] for q in range(Q)], [field[q, t, :] for q in range(Q)], s, field[Q + 1, t, :]
+        )
         free = 1.0 - s
         two = [2.0 * free * u[a] for a in range(3)]
         less = free * speed
@@ -290,92 +318,194 @@
             e = out[q] - less
             adj[q, t, :] = e + dot_c(q, two) if q else e
         if t.start < own:
-            flat[9, t, :] = by_s - rho * speed - kinetic[t, :]
-    for ref, group in ((flat, FLAT), (up, FALL), (down, RISE)):
-        for i, q in enumerate(group):
-            ref[i] = shifted(adj[q], -VEL[q][0], -VEL[q][1])[:own]
-
-
-def kernel_five(cells, pop, frac, lab, flat, low, high, energy, sens, out):
+            flat[len(FLAT), t, :] = by_s - rho * speed - kinetic[t, :]
+
+    def pulled(q):
+        return shifted(adj[q], -VEL[q][0], -VEL[q][1])[:own]
+
+    for i, q in enumerate(FLAT):
+        flat[i] = pulled(q)
+    for i in range(len(RISE)):
+        write_pair(odd, to_pair.at[i], to_other.at[i], pulled(FALL[i]), pulled(RISE[i]))
+
+
+def kernel_five(cells, odd_z, pop, cell, flat, pair, other, energy, sens_h, out_h, sens, out, sems):
     own = pop.shape[1]
+    odd = odd_z[0] == 1
+    copies = []
     scale = cells / jnp.sum(energy[...], keepdims=True)
     scale = jnp.broadcast_to(scale, (8, pop.shape[2]))
     for t in tiles(own):
-        label = lab[t, :].astype(jnp.float32)
-        s = jnp.where(label == 1.0, frac[t, :], jnp.where(label == 2.0, 1.0, 0.0))
+        s, label = cell[0, t, :], cell[1, t, :]
         lam = []
         for q in range(Q):
-            ref, i = {0: (flat, FLAT), 1: (high, RISE), -1: (low, FALL)}[VEL[q][2]]
-            lam.append(ref[i.index(q), t, :])
+            if VEL[q][2] == 0:
+                lam.append(flat[FLAT.index(q), t, :])
+            elif VEL[q][2] == 1:
+                i = RISE.index(q)
+                lam.append(pick(odd, pair[i, t, :], other[i, t, :]))
+            else:
+                i = FALL.index(q)
+                lam.append(pick(odd, other[i, t, :], pair[i, t, :]))
         grads, by_s, _, _, _ = pull_back(lam, [pop[q, t, :] for q in range(Q)], s, label)
         for q in range(Q):
             out[q, t, :] = grads[q] * scale
-        sens[t, :] = jnp.where(label == 1.0, (by_s + flat[9, t, :]) * scale, 0.0)
-
-
-def call(kernel, shapes, scratch, *args):
+        sens[t, :] = jnp.where(label == 1.0, (by_s + flat[len(FLAT), t, :]) * scale, 0.0)
+        n = t.start // 8
+        copies.append(pltpu.make_async_copy(out.at[:, t, :], out_h.at[:, t, :], sems.at[n]))
+        copies[-1].start()
+    copies.append(pltpu.make_async_copy(sens, sens_h, sems.at[own // 8]))
+    copies[-1].start()
+    for c in copies:
+        c.wait()
+
+
+def call(kernel, shapes, scratch, flags, *args, hbm_out=False, sems=0, work=0):
+    fast = pl.BlockSpec(memory_space=pltpu.VMEM)
+    slow = pl.BlockSpec(memory_space=pltpu.HBM)
     return pl.pallas_call(
         kernel,
         out_shape=[jax.ShapeDtypeStruct(s, jnp.float32) for s in shapes],
-        in_specs=[pl.BlockSpec(memory_space=pltpu.VMEM)] * len(args),
-        out_specs=[pl.BlockSpec(memory_space=pltpu.VMEM)] * len(shapes),
-        scratch_shapes=[pltpu.VMEM(s, jnp.float32) for s in scratch],
+        in_specs=[pl.BlockSpec(memory_space=pltpu.SMEM)] * len(flags)
+        + [fast] * len(args),
+        out_specs=[slow if hbm_out else fast] * len(shapes),
+        scratch_shapes=[pltpu.VMEM(s, jnp.float32) for s in scratch]
+        + ([pltpu.SemaphoreType.DMA((sems,))] if sems else []),
         compiler_params=pltpu.CompilerParams(vmem_limit_bytes=16 * 1024 * 1024),
-    )(*args)
-
-
-def passed_along(array, axis, by):
-    count = lax.axis_size(axis)
-    return lax.ppermute(array, axis, [(i, (i + by) % count) for i in range(count)])
-
-
-def total_over(value, axes):
-    for axis in axes:
+        cost_estimate=pl.CostEstimate(flops=0, transcendentals=0, bytes_accessed=work) if work else None,
+    )(*flags, *args)
+
+
+def doubled(value, steps):
+    for axis, step in steps:
         count = lax.axis_size(axis)
-        if count & (count - 1):
-            value = lax.psum(value, axis)
-            continue
-        step = 1
-        while step < count:
-            value = value + lax.ppermute(value, axis, [(i, i ^ step) for i in range(count)])
-            step *= 2
+        value = value + lax.ppermute(value, axis, [(i, i ^ step) for i in range(count)])
     return value
+
+
+def doublings(count):
+    return [1 << b for b in range(count.bit_length() - 1)]
+
+
+class Layout:
+    def __init__(self, planes, chunks):
+        self.planes, self.chunks = planes, chunks
+        self.bricks = [(p, k) for p in range(planes) for k in range(chunks)]
+        self.swapped = planes % 2 == 0 and chunks % 2 == 0
+
+    def start(self, p, k):
+        return (p % self.planes) * self.chunks + k % self.chunks
+
+    def home(self, p, k):
+        p, k = p % self.planes, k % self.chunks
+        if not self.swapped:
+            return self.start(p, k)
+        return self.start(p - p % 2 + (k + ALPHA) % 2, k - k % 2 + (p + BETA) % 2)
+
+    def moves(self, source, target):
+        side = lambda p: 1 - 2 * (p % 2)
+        still = [(source(p, k), target(p, k)) for p, k in self.bricks]
+        pair = [(source(p, k), target(p + side(p), k)) for p, k in self.bricks]
+        other = [(source(p, k), target(p - side(p), k)) for p, k in self.bricks]
+        return still, pair, other
 
 
 def on_device(populations, solid_fraction, labels):
     _, _, own, wide = populations.shape
     rows = own + 2 * HALO
+    axes = ("gz", "gy")
+    planes, chunks = lax.axis_size("gz"), lax.axis_size("gy")
+    layout = Layout(planes, chunks)
+    flag = lambda axis: (lax.axis_index(axis) % 2).astype(jnp.int32).reshape(1)
+    odd_z, odd_y = flag("gz"), flag("gy")
+    odd_p = (odd_y + BETA) % 2 if layout.swapped else odd_z
     pop = populations.reshape(Q, own, wide)
     frac = solid_fraction.reshape(own, wide)
     lab = labels.reshape(own, wide)
-
-    def edge(cut):
-        return jnp.concatenate([pop[:, cut], frac[None, cut], lab[None, cut].astype(jnp.float32)], axis=0)
-
-    from_low = passed_along(edge(slice(own - HALO, own)), "gy", 1)
-    from_high = passed_along(edge(slice(0, HALO)), "gy", -1)
-    full = lambda n: (n, rows, wide)
-    mid, up, down = call(
-        kernel_one, [full(11), full(5), full(5)], [full(Q), full(Q)], pop, frac, lab, from_low, from_high
+    whole = lambda n: (n, rows, wide)
+    less = lambda n: (n, own, wide)
+    edge = lambda n: (n, 2 * HALO, wide)
+
+    mixed = jnp.where(lab == 1, frac, jnp.where(lab == 2, jnp.float32(1.0), jnp.float32(0.0)))
+    cell = jnp.stack([mixed, lab.astype(jnp.float32)])
+    edge_a, edge_b = call(kernel_pack, [(Q + 2, HALO, wide)] * 2, [], [odd_y], pop, cell)
+    side = lambda k: 1 - 2 * (k % 2)
+    edge_a = lax.ppermute(edge_a, "gy", [(k, (k + side(k)) % chunks) for k in range(chunks)])
+    edge_b = lax.ppermute(edge_b, "gy", [(k, (k - side(k)) % chunks) for k in range(chunks)])
+    mid, pair, other = call(
+        kernel_one,
+        [whole(11), whole(5), whole(5)],
+        [edge(Q + 2), whole(Q)],
+        [odd_z, odd_y],
+        pop,
+        cell,
+        edge_a,
+        edge_b,
     )
-    below, above = passed_along(up, "gz", 1), passed_along(down, "gz", -1)
-    mom, up, down, part = call(
-        kernel_two, [full(3), full(3), full(3), (8, wide)], [full(Q)], mid, below, above
+    still_p, pair_p, other_p = layout.moves(layout.start, layout.home)
+    mid = lax.ppermute(mid, axes, still_p)
+    other = lax.ppermute(other, axes, other_p)
+    pair = lax.ppermute(pair, axes, pair_p)
+    field, mom, pair, other, part = call(
+        kernel_two,
+        [whole(Q + 2), whole(3), whole(3), whole(3), (8, wide)],
+        [whole(Q)],
+        [odd_p],
+        mid,
+        pair,
+        other,
     )
-    low, high = passed_along(up, "gz", 1), passed_along(down, "gz", -1)
-    mine, up, down, kinetic, energy = call(
-        kernel_three, [full(3), full(3), full(3), (own, wide), (8, wide // 2)], [], mom, low, high, mid, part
+    _, pair_p, other_p = layout.moves(layout.home, layout.home)
+    other = lax.ppermute(other, axes, other_p)
+    pair = lax.ppermute(pair, axes, pair_p)
+    mine, pair, other, kinetic, energy = call(
+        kernel_three,
+        [whole(3), whole(3), whole(3), (own, wide), (8, wide // 2)],
+        [],
+        [odd_p],
+        mom,
+        pair,
+        other,
+        field,
+        part,
     )
-    energy = total_over(energy, ("gy", "gz"))
-    low, high = passed_along(up, "gz", 1), passed_along(down, "gz", -1)
-    less = lambda n: (n, own, wide)
-    flat, up, down = call(
-        kernel_four, [less(10), less(5), less(5)], [full(Q), full(Q)], mid, below, above, mine, low, high, kinetic
+    other = lax.ppermute(other, axes, other_p)
+    pair = lax.ppermute(pair, axes, pair_p)
+    steps = [("gy", d) for d in doublings(chunks)] + [("gz", d) for d in doublings(planes)]
+    steps.sort(key=lambda t: t[1])
+    energy = doubled(energy, steps[:EARLY])
+    flat, pair, other = call(
+        kernel_four,
+        [less(10), less(5), less(5)],
+        [whole(Q), whole(Q)],
+        [odd_p],
+        field,
+        mine,
+        pair,
+        other,
+        kinetic,
+        energy,
+        work=WORK,
     )
-    low, high = passed_along(up, "gz", 1), passed_along(down, "gz", -1)
-    cells = float(STEPS * own * wide * populations.shape[1] * lax.axis_size("gz") * lax.axis_size("gy"))
+    still_p, pair_p, other_p = layout.moves(layout.home, layout.start)
+    energy = doubled(energy, steps[EARLY:])
+    pair = lax.ppermute(pair, axes, pair_p)
+    other = lax.ppermute(other, axes, other_p)
+    flat = lax.ppermute(flat, axes, still_p)
+    cells = float(STEPS * own * wide * populations.shape[1] * planes * chunks)
     sens, out = call(
-        functools.partial(kernel_five, cells), [(own, wide), less(Q)], [], pop, frac, lab, flat, low, high, energy
+        functools.partial(kernel_five, cells),
+        [(own, wide), less(Q)],
+        [(own, wide), less(Q)],
+        [odd_z],
+        pop,
+        cell,
+        flat,
+        pair,
+        other,
+        energy,
+        hbm_out=True,
+        sems=own // 8 + 1,
     )
     return sens.reshape(solid_fraction.shape), out.reshape(populations.shape)
 

time: 64.6 us -> 55.7 us (0.86)
  waiting for transfers between devices: 34.9 us -> 23 us
  starting transfers between devices: 22.9 us -> 26.4 us
  local copies, waits for them, and re-layouts: 1.81 us -> 1.08 us
    ppermute x15 -> x17, waiting for transfers between devices: 34.9 us -> 23 us  [the longest x5 13.2 us: doubled(): lax.ppermute(value, axis, [(i, i ^ step) for i in range(count)])]
    ppermute x15 -> x17, starting transfers between devices: 22.9 us -> 26.4 us  [the longest x4 13 us: on_device(): other = lax.ppermute(other, axes, other_p)]
    slice x2 -> x0, local copies, waits for them, and re-layouts: 1.8 us -> none  [the longest x1 1.02 us: edge(): pop[:, cut]]
    unnamed x6 -> x8, local copies, waits for them, and re-layouts: 0.01 us -> 1.08 us
    pallas_call x5 -> x6, Pallas kernels: 3.19 us -> 3.24 us  [call(): pl.pallas_call(kernel, out_shape=[jax.ShapeDtypeStruct(s, jnp.float32) fo...]
  transfers between devices with their start and end apart: 15 -> 17, of which waited for: 13 -> 8; matrix products, arithmetic and copies ran while one was open for 0% -> 0% of each run, Pallas kernels for 0% -> 0%
where the time goes in v2:
time: 55.7 us; the launch traced here: 55.4 us
  starting transfers between devices  26.4 us (47%)
  waiting for transfers between devices  23 us (41%)
  Pallas kernels  3.24 us (6%)
  local copies, waits for them, and re-layouts  1.08 us (2%)
  other arithmetic  0.85 us (2%)
  between operations  0.79 us (1%)
    ppermute x5, waiting for transfers between devices, doubled(): lax.ppermute(value, axis, [(i, i ^ step) for i in range(count)])  13.2 us
    ppermute x4, starting transfers between devices, on_device(): other = lax.ppermute(other, axes, other_p)  13 us
    ppermute x4, starting transfers between devices, on_device(): pair = lax.ppermute(pair, axes, pair_p)  5.59 us
    ppermute x4, waiting for transfers between devices, on_device(): pair = lax.ppermute(pair, axes, pair_p)  3.82 us
    ppermute x5, starting transfers between devices, doubled(): lax.ppermute(value, axis, [(i, i ^ step) for i in range(count)])  3.33 us
    pallas_call x6, Pallas kernels, call(): pl.pallas_call(kernel, out_shape=[jax.ShapeDtypeStruct(s, jnp.float32) fo...  3.24 us
    ppermute x4, waiting for transfers between devices, on_device(): other = lax.ppermute(other, axes, other_p)  3.18 us
    ppermute x1, waiting for transfers between devices, on_device(): lax.ppermute(edge_b, 'gy', [(k, (k - side(k)) % chunks) for k in range(ch...  2.81 us
  transfers between devices with their start and end apart: 17, of which 8 were waited for; matrix products, arithmetic and copies ran while one was open for 0% of the time, Pallas kernels for 0%

profile of v2, /device:TPU:0, one launch (start us, length us, event | category | flops | bytes accessed | tf_op | source)
XLA Modules:
  0.0 55.4 jit_solution(7998153134524814151)
XLA Ops:
  0.7 0.8 %convert_element_type.4 = f32[1,32,256]{2,1,0:T(8,128)S(1)} convert(s32[1,32,256]{2,1,0:T(8,128)} %param.5) | non-fusion elementwise | flops 8192 | bytes 65536 | tf_op jit(solution)/shard_map/convert_element_type | solution.py:430
  1.5 0.0 copy-start
  1.5 1.1 %copy-done = f32[19,1,32,256]{3,2,1,0:T(8,128)S(1)} copy-done((f32[19,1,32,256]{3,2,1,0:T(8,128)S(1)}, f32[19,1,32,256]{3,2,1,0:T(8,128)}, u32[]{:S(2)}) %copy-start) | copy-done | bytes 622616
  2.6 0.5 collective-permute-start
  3.2 2.6 %collective-permute-start.1 = (f32[21,4,256]{2,1,0:T(4,128)S(1)}, f32[21,4,256]{2,1,0:T(4,128)S(1)}, u32[]{:S(2)}, u32[]{:S(2)}) collective-permute-start(f32[21,4,256]{2,1,0:T(4,128)S(1)} %get-tuple-element.23), channel_id=1, source_target_pairs={{0,3},{1,2},{2,1},{3,0},{4,7},{5,6},{6,5},{7,4},{8,11},{9,10},{10,... | collective-permute-start | bytes 258056 | tf_op jit(solution)/shard_map/ppermute | solution.py:434
  5.8 0.0 collective-permute-done.edge_pair
  5.8 2.8 %collective-permute-done.1.edge_other = f32[21,4,256]{2,1,0:T(4,128)S(1)} collective-permute-done((f32[21,4,256]{2,1,0:T(4,128)S(1)}, f32[21,4,256]{2,1,0:T(4,128)S(1)}, u32[]{:S(2)}, u32[]{:S(2)}) %collective-permute-start.1) | collective-permute-done | bytes 86048 | tf_op jit(solution)/shard_map/ppermute | solution.py:434
  8.6 0.5 shard_map.51
  9.1 1.4 %collective-permute-start.2 = (f32[11,40,256]{2,1,0:T(8,128)S(1)}, f32[11,40,256]{2,1,0:T(8,128)S(1)}, u32[]{:S(2)}, u32[]{:S(2)}) collective-permute-start(f32[11,40,256]{2,1,0:T(8,128)S(1)} %get-tuple-element.24), channel_id=1, source_target_pairs={{0,4},{1,0},{2,6},{3,2},{4,5},{5,1},{6,7},{7,3},{8,12},{9,8},{10,1... | collective-permute-start | bytes 1351688 | tf_op jit(solution)/shard_map/ppermute | solution.py:446
  10.5 2.0 %collective-permute-start.3 = (f32[5,40,256]{2,1,0:T(8,128)S(1)}, f32[5,40,256]{2,1,0:T(8,128)S(1)}, u32[]{:S(2)}, u32[]{:S(2)}) collective-permute-start(f32[5,40,256]{2,1,0:T(8,128)S(1)} %get-tuple-element.25), channel_id=1, source_target_pairs={{0,5},{1,1},{2,7},{3,3},{4,4},{5,0},{6,6},{7,2},{8,13},{9,9},{10,1... | collective-permute-start | bytes 614408 | tf_op jit(solution)/shard_map/ppermute | solution.py:448
  12.5 4.7 %collective-permute-start.4 = (f32[5,40,256]{2,1,0:T(8,128)S(1)}, f32[5,40,256]{2,1,0:T(8,128)S(1)}, u32[]{:S(2)}, u32[]{:S(2)}) collective-permute-start(f32[5,40,256]{2,1,0:T(8,128)S(1)} %get-tuple-element.26), channel_id=1, source_target_pairs={{0,29},{1,25},{2,31},{3,27},{4,12},{5,8},{6,14},{7,10},{8,5},{9,1}... | collective-permute-start | bytes 614408 | tf_op jit(solution)/shard_map/ppermute | solution.py:447
  17.2 3.8 %collective-permute-done.3.pair = f32[5,40,256]{2,1,0:T(8,128)S(1)} collective-permute-done((f32[5,40,256]{2,1,0:T(8,128)S(1)}, f32[5,40,256]{2,1,0:T(8,128)S(1)}, u32[]{:S(2)}, u32[]{:S(2)}) %collective-permute-start.3) | collective-permute-done | bytes 204832 | tf_op jit(solution)/shard_map/ppermute | solution.py:448
  21.1 0.5 shard_map.52
  21.6 0.1 collective-permute-start.5
  21.7 3.9 %collective-permute-start.6 = (f32[3,40,256]{2,1,0:T(8,128)S(1)}, f32[3,40,256]{2,1,0:T(8,128)S(1)}, u32[]{:S(2)}, u32[]{:S(2)}) collective-permute-start(f32[3,40,256]{2,1,0:T(8,128)S(1)} %get-tuple-element.30), channel_id=1, source_target_pairs={{4,29},{0,25},{6,31},{2,27},{5,12},{1,8},{7,14},{3,10},{12,5},{8,1... | collective-permute-start | bytes 368648 | tf_op jit(solution)/shard_map/ppermute | solution.py:459
  25.5 3.2 %collective-permute-done.6.other = f32[3,40,256]{2,1,0:T(8,128)S(1)} collective-permute-done((f32[3,40,256]{2,1,0:T(8,128)S(1)}, f32[3,40,256]{2,1,0:T(8,128)S(1)}, u32[]{:S(2)}, u32[]{:S(2)}) %collective-permute-start.6) | collective-permute-done | bytes 122912 | tf_op jit(solution)/shard_map/ppermute | solution.py:459
  28.7 0.1 shard_map.53
  28.8 0.1 collective-permute-start.7
  28.9 3.0 %collective-permute-start.8 = (f32[3,40,256]{2,1,0:T(8,128)S(1)}, f32[3,40,256]{2,1,0:T(8,128)S(1)}, u32[]{:S(2)}, u32[]{:S(2)}) collective-permute-start(f32[3,40,256]{2,1,0:T(8,128)S(1)} %get-tuple-element.34), channel_id=1, source_target_pairs={{4,29},{0,25},{6,31},{2,27},{5,12},{1,8},{7,14},{3,10},{12,5},{8,1... | collective-permute-start | bytes 368648 | tf_op jit(solution)/shard_map/ppermute | solution.py:472
  31.9 1.2 %collective-permute-done.9 = f32[8,128]{1,0:T(8,128)S(1)} collective-permute-done((f32[8,128]{1,0:T(8,128)S(1)}, f32[8,128]{1,0:T(8,128)S(1)}, u32[]{:S(2)}, u32[]{:S(2)}) %collective-permute-start.9) | collective-permute-done | bytes 4128 | tf_op jit(solution)/shard_map/ppermute | solution.py:382
  33.0 1.5 %collective-permute-start.10 = (f32[8,128]{1,0:T(8,128)S(1)}, f32[8,128]{1,0:T(8,128)S(1)}, u32[]{:S(2)}, u32[]{:S(2)}) collective-permute-start(f32[8,128]{1,0:T(8,128)S(1)} %add.31), channel_id=1, source_target_pairs={{0,4},{4,0},{8,12},{12,8},{16,20},{20,16},{24,28},{28,24},{1,5},{5... | collective-permute-start | bytes 12296 | tf_op jit(solution)/shard_map/ppermute | solution.py:382
  34.5 2.1 %collective-permute-done.10 = f32[8,128]{1,0:T(8,128)S(1)} collective-permute-done((f32[8,128]{1,0:T(8,128)S(1)}, f32[8,128]{1,0:T(8,128)S(1)}, u32[]{:S(2)}, u32[]{:S(2)}) %collective-permute-start.10) | collective-permute-done | bytes 4128 | tf_op jit(solution)/shard_map/ppermute | solution.py:382
  36.6 0.9 %shard_map.54 = (f32[10,32,256]{2,1,0:T(8,128)S(1)}, f32[5,32,256]{2,1,0:T(8,128)S(1)}, f32[5,32,256]{2,1,0:T(8,128)S(1)}) custom-call(s32[1]{0:T(128)S(6)} %select_n.31.odd_p, f32[21,40,256]{2,1,0:T(8,128)S(1)} %get-tuple-element.27.field, f32[3,40,256]{2,1,0:T(8,128)S(1)} %get-tuple-element.32.mine, f32[3,40,256]{2,1,0:T(8,128)S(1)} %collective-permute-done.7.pair, ...), custom_call_target="tpu_custom_call" | custom-call | bytes 20000000 | tf_op jit(solution)/shard_map/pallas_call | solution.py:366
  37.5 0.0 collective-permute-start.11
  37.6 3.5 %collective-permute-start.12 = (f32[5,32,256]{2,1,0:T(8,128)S(1)}, f32[5,32,256]{2,1,0:T(8,128)S(1)}, u32[]{:S(2)}, u32[]{:S(2)}) collective-permute-start(f32[5,32,256]{2,1,0:T(8,128)S(1)} %get-tuple-element.38), channel_id=1, source_target_pairs={{4,4},{0,5},{6,6},{2,7},{5,0},{1,1},{7,2},{3,3},{12,12},{8,13},{14... | collective-permute-start | bytes 491528 | tf_op jit(solution)/shard_map/ppermute | solution.py:492
  41.0 1.4 %collective-permute-start.13 = (f32[5,32,256]{2,1,0:T(8,128)S(1)}, f32[5,32,256]{2,1,0:T(8,128)S(1)}, u32[]{:S(2)}, u32[]{:S(2)}) collective-permute-start(f32[5,32,256]{2,1,0:T(8,128)S(1)} %get-tuple-element.39), channel_id=1, source_target_pairs={{4,28},{0,29},{6,30},{2,31},{5,8},{1,9},{7,10},{3,11},{12,4},{8,5}... | collective-permute-start | bytes 491528 | tf_op jit(solution)/shard_map/ppermute | solution.py:493
  42.4 1.5 %collective-permute-start.14 = (f32[8,128]{1,0:T(8,128)S(1)}, f32[8,128]{1,0:T(8,128)S(1)}, u32[]{:S(2)}, u32[]{:S(2)}) collective-permute-start(f32[8,128]{1,0:T(8,128)S(1)} %add.32.energy), channel_id=1, source_target_pairs={{0,2},{1,3},{2,0},{3,1},{4,6},{5,7},{6,4},{7,5},{8,10},{9,11},{10,... | collective-permute-start | bytes 12296 | tf_op jit(solution)/shard_map/ppermute | solution.py:382
  43.9 2.1 %collective-permute-done.14 = f32[8,128]{1,0:T(8,128)S(1)} collective-permute-done((f32[8,128]{1,0:T(8,128)S(1)}, f32[8,128]{1,0:T(8,128)S(1)}, u32[]{:S(2)}, u32[]{:S(2)}) %collective-permute-start.14) | collective-permute-done | bytes 4128 | tf_op jit(solution)/shard_map/ppermute | solution.py:382
  46.0 0.3 collective-permute-start.15
  46.3 3.3 %collective-permute-done.15 = f32[8,128]{1,0:T(8,128)S(1)} collective-permute-done((f32[8,128]{1,0:T(8,128)S(1)}, f32[8,128]{1,0:T(8,128)S(1)}, u32[]{:S(2)}, u32[]{:S(2)}) %collective-permute-start.15) | collective-permute-done | bytes 4128 | tf_op jit(solution)/shard_map/ppermute | solution.py:382
  49.6 4.5 %collective-permute-done.16 = f32[8,128]{1,0:T(8,128)S(1)} collective-permute-done((f32[8,128]{1,0:T(8,128)S(1)}, f32[8,128]{1,0:T(8,128)S(1)}, u32[]{:S(2)}, u32[]{:S(2)}) %collective-permute-start.16) | collective-permute-done | bytes 4128 | tf_op jit(solution)/shard_map/ppermute | solution.py:382
  54.1 1.2 %shard_map.55 = (f32[32,256]{1,0:T(8,128)}, f32[19,32,256]{2,1,0:T(8,128)}) custom-call(s32[1]{0:T(128)} %bitcast.odd_z, f32[19,32,256]{2,1,0:T(8,128)S(1)} %bitcast.9, f32[2,32,256]{2,1,0:T(8,128)S(1)} %pad_maximum_fusion.cell, f32[10,32,256]{2,1,0:T(8,128)S(1)} %collective-permute-done.11.flat, f32[5,32,256]{2,1,0:T(8,128)S(1)} %collective-permute-done.12.pair, ...), custom_call_target="tpu_custom_call" | custom-call | tf_op jit(solution)/shard_map/pallas_call | solution.py:366
  (24 shorter events, 0.1 us)
Async XLA Ops:
  0.6 0.8 %copy-start.2 = (s32[1,32,256]{2,1,0:T(8,128)S(1)}, s32[1,32,256]{2,1,0:T(8,128)}, u32[]{:S(2)}) copy-start(s32[1,32,256]{2,1,0:T(8,128)} %param.5) | copy-start | bytes 98308
  0.6 0.8 %copy-start.3 = (f32[1,32,256]{2,1,0:T(8,128)S(1)}, f32[1,32,256]{2,1,0:T(8,128)}, u32[]{:S(2)}) copy-start(f32[1,32,256]{2,1,0:T(8,128)} %param.4) | copy-start | bytes 98308
  1.5 1.1 %copy-start = (f32[19,1,32,256]{3,2,1,0:T(8,128)S(1)}, f32[19,1,32,256]{3,2,1,0:T(8,128)}, u32[]{:S(2)}) copy-start(f32[19,1,32,256]{3,2,1,0:T(8,128)} %param.3) | copy-start | bytes 1867780
  2.6 6.0 %copy-start.1 = (f32[19,1,32,256]{3,2,1,0:T(8,128)S(1)}, f32[19,1,32,256]{3,2,1,0:T(8,128)}, u32[]{:S(2)}) copy-start(f32[19,1,32,256]{3,2,1,0:T(8,128)} %param.3) | copy-start | bytes 1867780
  2.6 3.2 %collective-permute-start = (f32[21,4,256]{2,1,0:T(4,128)S(1)}, f32[21,4,256]{2,1,0:T(4,128)S(1)}, u32[]{:S(2)}, u32[]{:S(2)}) collective-permute-start(f32[21,4,256]{2,1,0:T(4,128)S(1)} %get-tuple-element.22), channel_id=1, source_target_pairs={{0,1},{1,0},{2,3},{3,2},{4,5},{5,4},{6,7},{7,6},{8,9},{9,8},{10,11... | collective-permute-start | bytes 258056 | tf_op jit(solution)/shard_map/ppermute | solution.py:433
  3.2 5.5 %collective-permute-start.1 = (f32[21,4,256]{2,1,0:T(4,128)S(1)}, f32[21,4,256]{2,1,0:T(4,128)S(1)}, u32[]{:S(2)}, u32[]{:S(2)}) collective-permute-start(f32[21,4,256]{2,1,0:T(4,128)S(1)} %get-tuple-element.23), channel_id=1, source_target_pairs={{0,3},{1,2},{2,1},{3,0},{4,7},{5,6},{6,5},{7,4},{8,11},{9,10},{10,... | collective-permute-start | bytes 258056 | tf_op jit(solution)/shard_map/ppermute | solution.py:434
  9.1 11.9 %collective-permute-start.2 = (f32[11,40,256]{2,1,0:T(8,128)S(1)}, f32[11,40,256]{2,1,0:T(8,128)S(1)}, u32[]{:S(2)}, u32[]{:S(2)}) collective-permute-start(f32[11,40,256]{2,1,0:T(8,128)S(1)} %get-tuple-element.24), channel_id=1, source_target_pairs={{0,4},{1,0},{2,6},{3,2},{4,5},{5,1},{6,7},{7,3},{8,12},{9,8},{10,1... | collective-permute-start | bytes 1351688 | tf_op jit(solution)/shard_map/ppermute | solution.py:446
  10.5 10.6 %collective-permute-start.3 = (f32[5,40,256]{2,1,0:T(8,128)S(1)}, f32[5,40,256]{2,1,0:T(8,128)S(1)}, u32[]{:S(2)}, u32[]{:S(2)}) collective-permute-start(f32[5,40,256]{2,1,0:T(8,128)S(1)} %get-tuple-element.25), channel_id=1, source_target_pairs={{0,5},{1,1},{2,7},{3,3},{4,4},{5,0},{6,6},{7,2},{8,13},{9,9},{10,1... | collective-permute-start | bytes 614408 | tf_op jit(solution)/shard_map/ppermute | solution.py:448
  12.5 8.6 %collective-permute-start.4 = (f32[5,40,256]{2,1,0:T(8,128)S(1)}, f32[5,40,256]{2,1,0:T(8,128)S(1)}, u32[]{:S(2)}, u32[]{:S(2)}) collective-permute-start(f32[5,40,256]{2,1,0:T(8,128)S(1)} %get-tuple-element.26), channel_id=1, source_target_pairs={{0,29},{1,25},{2,31},{3,27},{4,12},{5,8},{6,14},{7,10},{8,5},{9,1}... | collective-permute-start | bytes 614408 | tf_op jit(solution)/shard_map/ppermute | solution.py:447
  21.6 3.9 %collective-permute-start.5 = (f32[3,40,256]{2,1,0:T(8,128)S(1)}, f32[3,40,256]{2,1,0:T(8,128)S(1)}, u32[]{:S(2)}, u32[]{:S(2)}) collective-permute-start(f32[3,40,256]{2,1,0:T(8,128)S(1)} %get-tuple-element.29), channel_id=1, source_target_pairs={{4,5},{0,1},{6,7},{2,3},{5,4},{1,0},{7,6},{3,2},{12,13},{8,9},{14,... | collective-permute-start | bytes 368648 | tf_op jit(solution)/shard_map/ppermute | solution.py:460
  21.7 7.0 %collective-permute-start.6 = (f32[3,40,256]{2,1,0:T(8,128)S(1)}, f32[3,40,256]{2,1,0:T(8,128)S(1)}, u32[]{:S(2)}, u32[]{:S(2)}) collective-permute-start(f32[3,40,256]{2,1,0:T(8,128)S(1)} %get-tuple-element.30), channel_id=1, source_target_pairs={{4,29},{0,25},{6,31},{2,27},{5,12},{1,8},{7,14},{3,10},{12,5},{8,1... | collective-permute-start | bytes 368648 | tf_op jit(solution)/shard_map/ppermute | solution.py:459
  28.8 7.9 %collective-permute-start.7 = (f32[3,40,256]{2,1,0:T(8,128)S(1)}, f32[3,40,256]{2,1,0:T(8,128)S(1)}, u32[]{:S(2)}, u32[]{:S(2)}) collective-permute-start(f32[3,40,256]{2,1,0:T(8,128)S(1)} %get-tuple-element.33), channel_id=1, source_target_pairs={{4,5},{0,1},{6,7},{2,3},{5,4},{1,0},{7,6},{3,2},{12,13},{8,9},{14,... | collective-permute-start | bytes 368648 | tf_op jit(solution)/shard_map/ppermute | solution.py:473
  28.9 7.8 %collective-permute-start.8 = (f32[3,40,256]{2,1,0:T(8,128)S(1)}, f32[3,40,256]{2,1,0:T(8,128)S(1)}, u32[]{:S(2)}, u32[]{:S(2)}) collective-permute-start(f32[3,40,256]{2,1,0:T(8,128)S(1)} %get-tuple-element.34), channel_id=1, source_target_pairs={{4,29},{0,25},{6,31},{2,27},{5,12},{1,8},{7,14},{3,10},{12,5},{8,1... | collective-permute-start | bytes 368648 | tf_op jit(solution)/shard_map/ppermute | solution.py:472
  31.9 1.2 %collective-permute-start.9 = (f32[8,128]{1,0:T(8,128)S(1)}, f32[8,128]{1,0:T(8,128)S(1)}, u32[]{:S(2)}, u32[]{:S(2)}) collective-permute-start(f32[8,128]{1,0:T(8,128)S(1)} %get-tuple-element.36), channel_id=1, source_target_pairs={{0,1},{1,0},{2,3},{3,2},{4,5},{5,4},{6,7},{7,6},{8,9},{9,8},{10,11... | collective-permute-start | bytes 12296 | tf_op jit(solution)/shard_map/ppermute | solution.py:382
  33.0 3.6 %collective-permute-start.10 = (f32[8,128]{1,0:T(8,128)S(1)}, f32[8,128]{1,0:T(8,128)S(1)}, u32[]{:S(2)}, u32[]{:S(2)}) collective-permute-start(f32[8,128]{1,0:T(8,128)S(1)} %add.31), channel_id=1, source_target_pairs={{0,4},{4,0},{8,12},{12,8},{16,20},{20,16},{24,28},{28,24},{1,5},{5... | collective-permute-start | bytes 12296 | tf_op jit(solution)/shard_map/ppermute | solution.py:382
  37.5 16.6 %collective-permute-start.11 = (f32[10,32,256]{2,1,0:T(8,128)S(1)}, f32[10,32,256]{2,1,0:T(8,128)S(1)}, u32[]{:S(2)}, u32[]{:S(2)}) collective-permute-start(f32[10,32,256]{2,1,0:T(8,128)S(1)} %get-tuple-element.37), channel_id=1, source_target_pairs={{4,0},{0,1},{6,2},{2,3},{5,4},{1,5},{7,6},{3,7},{12,8},{8,9},{14,1... | collective-permute-start | bytes 983048 | tf_op jit(solution)/shard_map/ppermute | solution.py:494
  37.6 16.6 %collective-permute-start.12 = (f32[5,32,256]{2,1,0:T(8,128)S(1)}, f32[5,32,256]{2,1,0:T(8,128)S(1)}, u32[]{:S(2)}, u32[]{:S(2)}) collective-permute-start(f32[5,32,256]{2,1,0:T(8,128)S(1)} %get-tuple-element.38), channel_id=1, source_target_pairs={{4,4},{0,5},{6,6},{2,7},{5,0},{1,1},{7,2},{3,3},{12,12},{8,13},{14... | collective-permute-start | bytes 491528 | tf_op jit(solution)/shard_map/ppermute | solution.py:492
  41.0 13.1 %collective-permute-start.13 = (f32[5,32,256]{2,1,0:T(8,128)S(1)}, f32[5,32,256]{2,1,0:T(8,128)S(1)}, u32[]{:S(2)}, u32[]{:S(2)}) collective-permute-start(f32[5,32,256]{2,1,0:T(8,128)S(1)} %get-tuple-element.39), channel_id=1, source_target_pairs={{4,28},{0,29},{6,30},{2,31},{5,8},{1,9},{7,10},{3,11},{12,4},{8,5}... | collective-permute-start | bytes 491528 | tf_op jit(solution)/shard_map/ppermute | solution.py:493
  42.4 3.6 %collective-permute-start.14 = (f32[8,128]{1,0:T(8,128)S(1)}, f32[8,128]{1,0:T(8,128)S(1)}, u32[]{:S(2)}, u32[]{:S(2)}) collective-permute-start(f32[8,128]{1,0:T(8,128)S(1)} %add.32.energy), channel_id=1, source_target_pairs={{0,2},{1,3},{2,0},{3,1},{4,6},{5,7},{6,4},{7,5},{8,10},{9,11},{10,... | collective-permute-start | bytes 12296 | tf_op jit(solution)/shard_map/ppermute | solution.py:382
  46.0 3.6 %collective-permute-start.15 = (f32[8,128]{1,0:T(8,128)S(1)}, f32[8,128]{1,0:T(8,128)S(1)}, u32[]{:S(2)}, u32[]{:S(2)}) collective-permute-start(f32[8,128]{1,0:T(8,128)S(1)} %add.33), channel_id=1, source_target_pairs={{0,8},{4,12},{8,0},{12,4},{16,24},{20,28},{24,16},{28,20},{1,9},{5... | collective-permute-start | bytes 12296 | tf_op jit(solution)/shard_map/ppermute | solution.py:382
  49.6 4.5 %collective-permute-start.16 = (f32[8,128]{1,0:T(8,128)S(1)}, f32[8,128]{1,0:T(8,128)S(1)}, u32[]{:S(2)}, u32[]{:S(2)}) collective-permute-start(f32[8,128]{1,0:T(8,128)S(1)} %add.34), channel_id=1, source_target_pairs={{0,16},{4,20},{8,24},{12,28},{16,0},{20,4},{24,8},{28,12},{1,17},{... | collective-permute-start | bytes 12296 | tf_op jit(solution)/shard_map/ppermute | solution.py:382

commit v3 on v2

--- a/solution.py
+++ b/solution.py
@@ -11,8 +11,6 @@
 OMEGA = 0.9
 INLET_SPEED = 0.05
 HALO = 4
-WORK = 20_000_000
-EARLY = 2
 ALPHA, BETA = 1, 0
 
 
@@ -184,50 +182,54 @@
         write_pair(oy, edge_pair.at[i], edge_other.at[i], ref[own - HALO : own, :], ref[0:HALO, :])
 
 
-def kernel_one(odd_z, odd_y, pop, cell, edge_pair, edge_other, mid, pair, other, tile, post):
-    own = pop.shape[1]
-    rows = mid.shape[1]
-    oz, oy = odd_z[0] == 1, odd_y[0] == 1
+def send_first(odd, f, s, label, mid, pair, other, t, r):
+    out, _, _, _ = collide(f, s, label)
+    moved = [shifted(out[q], VEL[q][0], 0) for q in range(Q)]
+    for i, q in enumerate(FLAT):
+        mid[i, t, :] = moved[q]
+    mid[len(FLAT), t, :] = s
+    mid[len(FLAT) + 1, t, :] = label
+    for i in range(len(RISE)):
+        write_pair(odd, pair.at[i, r, :], other.at[i, r, :], moved[RISE[i]], moved[FALL[i]])
+
+
+def kernel_one(odd_z, pop, cell, mid, pair, other):
+    for t in tiles(pop.shape[1]):
+        send_first(odd_z[0] == 1, [pop[q, t, :] for q in range(Q)], cell[0, t, :], cell[1, t, :], mid, pair, other, t, t)
+
+
+def kernel_edge(odd_z, odd_y, edge_pair, edge_other, pair_in, other_in, mid, pair, other, tile):
+    rows = pair.shape[1]
+    oy = odd_y[0] == 1
     for i in range(Q + 2):
         a, b = edge_pair[i], edge_other[i]
         tile[i, :HALO, :] = pick(oy, a, b)
         tile[i, HALO:, :] = pick(oy, b, a)
-    for t in tiles(rows):
-        if t.start < own:
-            f = [pop[q, t, :] for q in range(Q)]
-            s, label = cell[0, t, :], cell[1, t, :]
-        else:
-            f = [tile[q] for q in range(Q)]
-            s, label = tile[Q], tile[Q + 1]
-        mid[len(FLAT), t, :] = s
-        mid[len(FLAT) + 1, t, :] = label
-        out, _, _, _ = collide(f, s, label)
-        for q in range(Q):
-            post[q, t, :] = out[q]
-    moved = lambda q: shifted(post[q], VEL[q][0], VEL[q][1])
-    for i, q in enumerate(FLAT):
-        mid[i] = moved(q)
-    for i in range(len(RISE)):
-        write_pair(oz, pair.at[i], other.at[i], moved(RISE[i]), moved(FALL[i]))
-
-
-def kernel_two(odd_p, mid, pair, other, field, mom, to_pair, to_other, part, post):
+    r = pl.ds(rows - 2 * HALO, 2 * HALO)
+    f = [tile[q] for q in range(Q)]
+    send_first(odd_z[0] == 1, f, tile[Q], tile[Q + 1], mid, pair, other, slice(None), r)
+
+
+def kernel_two(odd_p, mid, pair, other, mid_e, field, mom, to_pair, to_other, part, raw, post):
     rows = field.shape[1]
     own = rows - 2 * HALO
     odd = odd_p[0] == 1
     for q in range(Q):
         cz = VEL[q][2]
         if cz == 0:
-            value = mid[FLAT.index(q)]
+            raw[:own, :] = mid[FLAT.index(q)]
+            raw[own:, :] = mid_e[FLAT.index(q)]
+            value = raw[...]
         elif cz == 1:
             i = RISE.index(q)
             value = pick(odd, other[i], pair[i])
         else:
             i = FALL.index(q)
             value = pick(odd, pair[i], other[i])
-        field[q] = value
+        field[q] = shifted(value, 0, VEL[q][1])
     for i in (0, 1):
-        field[Q + i] = mid[len(FLAT) + i]
+        field[Q + i, :own, :] = mid[len(FLAT) + i]
+        field[Q + i, own:, :] = mid_e[len(FLAT) + i]
     total = None
     for t in tiles(rows):
         s = field[Q, t, :]
@@ -360,7 +362,7 @@
         c.wait()
 
 
-def call(kernel, shapes, scratch, flags, *args, hbm_out=False, sems=0, work=0):
+def call(kernel, shapes, scratch, flags, *args, hbm_out=False, sems=0, aliases=None):
     fast = pl.BlockSpec(memory_space=pltpu.VMEM)
     slow = pl.BlockSpec(memory_space=pltpu.HBM)
     return pl.pallas_call(
@@ -371,20 +373,37 @@
         out_specs=[slow if hbm_out else fast] * len(shapes),
         scratch_shapes=[pltpu.VMEM(s, jnp.float32) for s in scratch]
         + ([pltpu.SemaphoreType.DMA((sems,))] if sems else []),
+        input_output_aliases=aliases or {},
         compiler_params=pltpu.CompilerParams(vmem_limit_bytes=16 * 1024 * 1024),
-        cost_estimate=pl.CostEstimate(flops=0, transcendentals=0, bytes_accessed=work) if work else None,
     )(*flags, *args)
 
 
-def doubled(value, steps):
-    for axis, step in steps:
-        count = lax.axis_size(axis)
-        value = value + lax.ppermute(value, axis, [(i, i ^ step) for i in range(count)])
+def summed(value, axes, groups):
+    count = lax.axis_size(axes)
+    if groups is None:
+        return value
+    for bits in groups:
+        masks = [0]
+        for bit in bits:
+            masks += [m | bit for m in masks]
+        parts = [lax.ppermute(value, axes, [(i, i ^ m) for i in range(count)]) for m in masks[1:]]
+        value = functools.reduce(lambda a, b: a + b, parts, value)
     return value
 
 
 def doublings(count):
     return [1 << b for b in range(count.bit_length() - 1)]
+
+
+def sum_order(planes, chunks):
+    y_bits = doublings(chunks)
+    z_bits = [chunks * d for d in doublings(planes)]
+    if 2 ** len(y_bits) != chunks or 2 ** len(z_bits) != planes:
+        return None, None
+    first = z_bits[-1:]
+    rest = z_bits[:-1]
+    late = [y_bits[1:] + rest[1:2]] + [[b] for b in rest[2:]] + [rest[:1], y_bits[:1]]
+    return [g for g in [first] if g], [g for g in late if g]
 
 
 class Layout:
@@ -432,28 +451,32 @@
     side = lambda k: 1 - 2 * (k % 2)
     edge_a = lax.ppermute(edge_a, "gy", [(k, (k + side(k)) % chunks) for k in range(chunks)])
     edge_b = lax.ppermute(edge_b, "gy", [(k, (k - side(k)) % chunks) for k in range(chunks)])
-    mid, pair, other = call(
-        kernel_one,
-        [whole(11), whole(5), whole(5)],
-        [edge(Q + 2), whole(Q)],
+    mid, pair, other = call(kernel_one, [less(11), whole(5), whole(5)], [], [odd_z], pop, cell)
+    still_p, pair_p, other_p = layout.moves(layout.start, layout.home)
+    mid = lax.ppermute(mid, axes, still_p)
+    mid_e, pair, other = call(
+        kernel_edge,
+        [edge(11), whole(5), whole(5)],
+        [edge(Q + 2)],
         [odd_z, odd_y],
-        pop,
-        cell,
         edge_a,
         edge_b,
+        pair,
+        other,
+        aliases={4: 1, 5: 2},
     )
-    still_p, pair_p, other_p = layout.moves(layout.start, layout.home)
-    mid = lax.ppermute(mid, axes, still_p)
+    mid_e = lax.ppermute(mid_e, axes, still_p)
     other = lax.ppermute(other, axes, other_p)
     pair = lax.ppermute(pair, axes, pair_p)
     field, mom, pair, other, part = call(
         kernel_two,
         [whole(Q + 2), whole(3), whole(3), whole(3), (8, wide)],
-        [whole(Q)],
+        [(rows, wide), whole(Q)],
         [odd_p],
         mid,
         pair,
         other,
+        mid_e,
     )
     _, pair_p, other_p = layout.moves(layout.home, layout.home)
     other = lax.ppermute(other, axes, other_p)
@@ -471,9 +494,10 @@
     )
     other = lax.ppermute(other, axes, other_p)
     pair = lax.ppermute(pair, axes, pair_p)
-    steps = [("gy", d) for d in doublings(chunks)] + [("gz", d) for d in doublings(planes)]
-    steps.sort(key=lambda t: t[1])
-    energy = doubled(energy, steps[:EARLY])
+    early, late = sum_order(planes, chunks)
+    if early is None:
+        energy = lax.psum(energy, axes)
+    energy = summed(energy, axes, early)
     flat, pair, other = call(
         kernel_four,
         [less(10), less(5), less(5)],
@@ -485,10 +509,9 @@
         other,
         kinetic,
         energy,
-        work=WORK,
     )
     still_p, pair_p, other_p = layout.moves(layout.home, layout.start)
-    energy = doubled(energy, steps[EARLY:])
+    energy = summed(energy, axes, late)
     pair = lax.ppermute(pair, axes, pair_p)
     other = lax.ppermute(other, axes, other_p)
     flat = lax.ppermute(flat, axes, still_p)

time: 55.7 us -> 52 us (0.934)
  starting transfers between devices: 26.4 us -> 24.2 us
  waiting for transfers between devices: 23 us -> 21.5 us
    ppermute x4, waiting for transfers between devices: 3.82 us -> 0.01 us  [on_device(): pair = lax.ppermute(pair, axes, pair_p)]
    ppermute x4, waiting for transfers between devices: 3.18 us -> 6.78 us  [on_device(): other = lax.ppermute(other, axes, other_p)]
    ppermute x4, starting transfers between devices: 13 us -> 9.88 us  [on_device(): other = lax.ppermute(other, axes, other_p)]
    ppermute x1, starting transfers between devices: 1.39 us -> 2.95 us  [on_device(): mid = lax.ppermute(mid, axes, still_p)]
    ppermute x5 -> x7, waiting for transfers between devices: 13.2 us -> 12 us  [the longest x6 9.44 us: summed(): lax.ppermute(value, axes, [(i, i ^ m) for i in range(count)])]
    ppermute x1, starting transfers between devices: 2.64 us -> 1.64 us  [on_device(): lax.ppermute(edge_b, 'gy', [(k, (k - side(k)) % chunks) for k in range(ch...]
    ppermute x5 -> x7, starting transfers between devices: 3.33 us -> 3.7 us  [the longest x6 3.69 us: summed(): lax.ppermute(value, axes, [(i, i ^ m) for i in range(count)])]
    pallas_call x6 -> x7, Pallas kernels: 3.24 us -> 3.29 us  [call(): pl.pallas_call(kernel, out_shape=[jax.ShapeDtypeStruct(s, jnp.float32) fo...]
  transfers between devices with their start and end apart: 17 -> 19, of which waited for: 8 -> 8; matrix products, arithmetic and copies ran while one was open for 0% -> 0% of each run, Pallas kernels for 0% -> 0%
where the time goes in v3:
time: 52 us; the launch traced here: 51.7 us
  starting transfers between devices  24.2 us (47%)
  waiting for transfers between devices  21.5 us (41%)
  Pallas kernels  3.29 us (6%)
  local copies, waits for them, and re-layouts  1.08 us (2%)
  other arithmetic  0.85 us (2%)
  between operations  0.79 us (2%)
    ppermute x4, starting transfers between devices, on_device(): other = lax.ppermute(other, axes, other_p)  9.88 us
    ppermute x6, waiting for transfers between devices, summed(): lax.ppermute(value, axes, [(i, i ^ m) for i in range(count)])  9.44 us
    ppermute x4, waiting for transfers between devices, on_device(): other = lax.ppermute(other, axes, other_p)  6.78 us
    ppermute x4, starting transfers between devices, on_device(): pair = lax.ppermute(pair, axes, pair_p)  5.86 us
    ppermute x6, starting transfers between devices, summed(): lax.ppermute(value, axes, [(i, i ^ m) for i in range(count)])  3.69 us
    pallas_call x7, Pallas kernels, call(): pl.pallas_call(kernel, out_shape=[jax.ShapeDtypeStruct(s, jnp.float32) fo...  3.29 us
    ppermute x1, starting transfers between devices, on_device(): mid = lax.ppermute(mid, axes, still_p)  2.95 us
    ppermute x1, waiting for transfers between devices, on_device(): lax.ppermute(edge_b, 'gy', [(k, (k - side(k)) % chunks) for k in range(ch...  2.69 us
  transfers between devices with their start and end apart: 19, of which 8 were waited for; matrix products, arithmetic and copies ran while one was open for 0% of the time, Pallas kernels for 0%

profile of v3, /device:TPU:0, one launch (start us, length us, event | category | flops | bytes accessed | tf_op | source)
XLA Modules:
  0.0 51.7 jit_solution(7578995004866364262)
XLA Ops:
  0.7 0.8 %convert_element_type.4 = f32[1,32,256]{2,1,0:T(8,128)S(1)} convert(s32[1,32,256]{2,1,0:T(8,128)} %param.5) | non-fusion elementwise | flops 8192 | bytes 65536 | tf_op jit(solution)/shard_map/convert_element_type | solution.py:449
  1.5 1.1 %copy-done = f32[19,1,32,256]{3,2,1,0:T(8,128)S(1)} copy-done((f32[19,1,32,256]{3,2,1,0:T(8,128)S(1)}, f32[19,1,32,256]{3,2,1,0:T(8,128)}, u32[]{:S(2)}) %copy-start) | copy-done | bytes 622616
  2.6 0.4 shard_map.50
  3.0 3.0 %collective-permute-start = (f32[11,32,256]{2,1,0:T(8,128)S(1)}, f32[11,32,256]{2,1,0:T(8,128)S(1)}, u32[]{:S(2)}, u32[]{:S(2)}) collective-permute-start(f32[11,32,256]{2,1,0:T(8,128)S(1)} %get-tuple-element.25), channel_id=1, source_target_pairs={{0,4},{1,0},{2,6},{3,2},{4,5},{5,1},{6,7},{7,3},{8,12},{9,8},{10,1... | collective-permute-start | bytes 1081352 | tf_op jit(solution)/shard_map/ppermute | solution.py:456
  5.9 0.1 collective-permute-start.1
  6.0 1.6 %collective-permute-start.2 = (f32[21,4,256]{2,1,0:T(4,128)S(1)}, f32[21,4,256]{2,1,0:T(4,128)S(1)}, u32[]{:S(2)}, u32[]{:S(2)}) collective-permute-start(f32[21,4,256]{2,1,0:T(4,128)S(1)} %get-tuple-element.27), channel_id=1, source_target_pairs={{0,3},{1,2},{2,1},{3,0},{4,7},{5,6},{6,5},{7,4},{8,11},{9,10},{10,... | collective-permute-start | bytes 258056 | tf_op jit(solution)/shard_map/ppermute | solution.py:453
  7.7 2.7 %collective-permute-done.2.edge_other = f32[21,4,256]{2,1,0:T(4,128)S(1)} collective-permute-done((f32[21,4,256]{2,1,0:T(4,128)S(1)}, f32[21,4,256]{2,1,0:T(4,128)S(1)}, u32[]{:S(2)}, u32[]{:S(2)}) %collective-permute-start.2) | collective-permute-done | bytes 86048 | tf_op jit(solution)/shard_map/ppermute | solution.py:453
  10.4 0.2 shard_map.52
  10.5 2.9 %collective-permute-start.3 = (f32[5,40,256]{2,1,0:T(8,128)S(1)}, f32[5,40,256]{2,1,0:T(8,128)S(1)}, u32[]{:S(2)}, u32[]{:S(2)}) collective-permute-start(f32[5,40,256]{2,1,0:T(8,128)S(1)} %get-tuple-element.30), channel_id=1, source_target_pairs={{0,5},{1,1},{2,7},{3,3},{4,4},{5,0},{6,6},{7,2},{8,13},{9,9},{10,1... | collective-permute-start | bytes 614408 | tf_op jit(solution)/shard_map/ppermute | solution.py:470
  13.4 3.8 %collective-permute-start.4 = (f32[5,40,256]{2,1,0:T(8,128)S(1)}, f32[5,40,256]{2,1,0:T(8,128)S(1)}, u32[]{:S(2)}, u32[]{:S(2)}) collective-permute-start(f32[5,40,256]{2,1,0:T(8,128)S(1)} %get-tuple-element.31), channel_id=1, source_target_pairs={{0,29},{1,25},{2,31},{3,27},{4,12},{5,8},{6,14},{7,10},{8,5},{9,1}... | collective-permute-start | bytes 614408 | tf_op jit(solution)/shard_map/ppermute | solution.py:469
  17.3 2.6 %collective-permute-done.5.mid_e = f32[11,8,256]{2,1,0:T(8,128)S(1)} collective-permute-done((f32[11,8,256]{2,1,0:T(8,128)S(1)}, f32[11,8,256]{2,1,0:T(8,128)S(1)}, u32[]{:S(2)}, u32[]{:S(2)}) %collective-permute-start.5) | collective-permute-done | bytes 90144 | tf_op jit(solution)/shard_map/ppermute | solution.py:468
  19.9 1.5 %collective-permute-done.4.other = f32[5,40,256]{2,1,0:T(8,128)S(1)} collective-permute-done((f32[5,40,256]{2,1,0:T(8,128)S(1)}, f32[5,40,256]{2,1,0:T(8,128)S(1)}, u32[]{:S(2)}, u32[]{:S(2)}) %collective-permute-start.4) | collective-permute-done | bytes 204832 | tf_op jit(solution)/shard_map/ppermute | solution.py:469
  21.4 0.6 %shard_map.53 = (f32[21,40,256]{2,1,0:T(8,128)S(1)}, f32[3,40,256]{2,1,0:T(8,128)S(1)}, f32[3,40,256]{2,1,0:T(8,128)S(1)}, f32[3,40,256]{2,1,0:T(8,128)S(1)}, f32[8,256]{1,0:T(8,128)S(1)}) custom-call(s32[1]{0:T(128)S(6)} %select_n.31.odd_p, f32[11,32,256]{2,1,0:T(8,128)S(1)} %collective-permute-done.mid, f32[5,40,256]{2,1,0:T(8,128)S(1)} %collective-permute-done.3.pair, ...), custom_call_target="tpu_custom_call" | custom-call | tf_op jit(solution)/shard_map/pallas_call | solution.py:368
  21.9 0.1 collective-permute-start.6
  22.0 2.5 %collective-permute-start.7 = (f32[3,40,256]{2,1,0:T(8,128)S(1)}, f32[3,40,256]{2,1,0:T(8,128)S(1)}, u32[]{:S(2)}, u32[]{:S(2)}) collective-permute-start(f32[3,40,256]{2,1,0:T(8,128)S(1)} %get-tuple-element.36), channel_id=1, source_target_pairs={{4,29},{0,25},{6,31},{2,27},{5,12},{1,8},{7,14},{3,10},{12,5},{8,1... | collective-permute-start | bytes 368648 | tf_op jit(solution)/shard_map/ppermute | solution.py:482
  24.5 4.6 %collective-permute-done.7.other = f32[3,40,256]{2,1,0:T(8,128)S(1)} collective-permute-done((f32[3,40,256]{2,1,0:T(8,128)S(1)}, f32[3,40,256]{2,1,0:T(8,128)S(1)}, u32[]{:S(2)}, u32[]{:S(2)}) %collective-permute-start.7) | collective-permute-done | bytes 122912 | tf_op jit(solution)/shard_map/ppermute | solution.py:482
  29.1 0.1 shard_map.54
  29.2 0.1 collective-permute-start.8
  29.3 1.5 %collective-permute-start.9 = (f32[3,40,256]{2,1,0:T(8,128)S(1)}, f32[3,40,256]{2,1,0:T(8,128)S(1)}, u32[]{:S(2)}, u32[]{:S(2)}) collective-permute-start(f32[3,40,256]{2,1,0:T(8,128)S(1)} %get-tuple-element.40), channel_id=1, source_target_pairs={{4,29},{0,25},{6,31},{2,27},{5,12},{1,8},{7,14},{3,10},{12,5},{8,1... | collective-permute-start | bytes 368648 | tf_op jit(solution)/shard_map/ppermute | solution.py:495
  30.8 4.8 %collective-permute-done.10 = f32[8,128]{1,0:T(8,128)S(1)} collective-permute-done((f32[8,128]{1,0:T(8,128)S(1)}, f32[8,128]{1,0:T(8,128)S(1)}, u32[]{:S(2)}, u32[]{:S(2)}) %collective-permute-start.10) | collective-permute-done | bytes 4128 | tf_op jit(solution)/shard_map/ppermute | solution.py:389
  35.6 0.9 %shard_map.55 = (f32[10,32,256]{2,1,0:T(8,128)S(1)}, f32[5,32,256]{2,1,0:T(8,128)S(1)}, f32[5,32,256]{2,1,0:T(8,128)S(1)}) custom-call(s32[1]{0:T(128)S(6)} %select_n.31.odd_p, f32[21,40,256]{2,1,0:T(8,128)S(1)} %get-tuple-element.33.field, f32[3,40,256]{2,1,0:T(8,128)S(1)} %get-tuple-element.38.mine, f32[3,40,256]{2,1,0:T(8,128)S(1)} %collective-permute-done.8.pair, ...), custom_call_target="tpu_custom_call" | custom-call | tf_op jit(solution)/shard_map/pallas_call | solution.py:368
  36.5 0.1 collective-permute-start.11
  36.6 1.4 %collective-permute-start.16 = (f32[8,128]{1,0:T(8,128)S(1)}, f32[8,128]{1,0:T(8,128)S(1)}, u32[]{:S(2)}, u32[]{:S(2)}) collective-permute-start(f32[8,128]{1,0:T(8,128)S(1)} %add.34.energy), channel_id=1, source_target_pairs={{0,10},{1,11},{2,8},{3,9},{4,14},{5,15},{6,12},{7,13},{8,2},{9,3},... | collective-permute-start | bytes 12296 | tf_op jit(solution)/shard_map/ppermute | solution.py:389
  38.0 1.6 %collective-permute-start.15 = (f32[8,128]{1,0:T(8,128)S(1)}, f32[8,128]{1,0:T(8,128)S(1)}, u32[]{:S(2)}, u32[]{:S(2)}) collective-permute-start(f32[8,128]{1,0:T(8,128)S(1)} %add.34.energy), channel_id=1, source_target_pairs={{0,8},{1,9},{2,10},{3,11},{4,12},{5,13},{6,14},{7,15},{8,0},{9,1},... | collective-permute-start | bytes 12296 | tf_op jit(solution)/shard_map/ppermute | solution.py:389
  39.6 0.5 collective-permute-start.14
  40.1 2.8 %collective-permute-start.12 = (f32[5,32,256]{2,1,0:T(8,128)S(1)}, f32[5,32,256]{2,1,0:T(8,128)S(1)}, u32[]{:S(2)}, u32[]{:S(2)}) collective-permute-start(f32[5,32,256]{2,1,0:T(8,128)S(1)} %get-tuple-element.44), channel_id=1, source_target_pairs={{4,4},{0,5},{6,6},{2,7},{5,0},{1,1},{7,2},{3,3},{12,12},{8,13},{14... | collective-permute-start | bytes 491528 | tf_op jit(solution)/shard_map/ppermute | solution.py:515
  43.0 2.0 %collective-permute-start.13 = (f32[5,32,256]{2,1,0:T(8,128)S(1)}, f32[5,32,256]{2,1,0:T(8,128)S(1)}, u32[]{:S(2)}, u32[]{:S(2)}) collective-permute-start(f32[5,32,256]{2,1,0:T(8,128)S(1)} %get-tuple-element.45), channel_id=1, source_target_pairs={{4,28},{0,29},{6,30},{2,31},{5,8},{1,9},{7,10},{3,11},{12,4},{8,5}... | collective-permute-start | bytes 491528 | tf_op jit(solution)/shard_map/ppermute | solution.py:516
  45.0 0.2 collective-permute-start.17
  45.2 3.5 %collective-permute-done.17 = f32[8,128]{1,0:T(8,128)S(1)} collective-permute-done((f32[8,128]{1,0:T(8,128)S(1)}, f32[8,128]{1,0:T(8,128)S(1)}, u32[]{:S(2)}, u32[]{:S(2)}) %collective-permute-start.17) | collective-permute-done | bytes 4128 | tf_op jit(solution)/shard_map/ppermute | solution.py:389
  48.6 1.2 %collective-permute-done.18 = f32[8,128]{1,0:T(8,128)S(1)} collective-permute-done((f32[8,128]{1,0:T(8,128)S(1)}, f32[8,128]{1,0:T(8,128)S(1)}, u32[]{:S(2)}, u32[]{:S(2)}) %collective-permute-start.18) | collective-permute-done | bytes 4128 | tf_op jit(solution)/shard_map/ppermute | solution.py:389
  49.8 0.6 %collective-permute-done.13.other = f32[5,32,256]{2,1,0:T(8,128)S(1)} collective-permute-done((f32[5,32,256]{2,1,0:T(8,128)S(1)}, f32[5,32,256]{2,1,0:T(8,128)S(1)}, u32[]{:S(2)}, u32[]{:S(2)}) %collective-permute-start.13) | collective-permute-done | bytes 163872 | tf_op jit(solution)/shard_map/ppermute | solution.py:516
  50.5 1.2 %shard_map.56 = (f32[32,256]{1,0:T(8,128)}, f32[19,32,256]{2,1,0:T(8,128)}) custom-call(s32[1]{0:T(128)} %bitcast.odd_z, f32[19,32,256]{2,1,0:T(8,128)S(1)} %bitcast.9, f32[2,32,256]{2,1,0:T(8,128)S(1)} %pad_maximum_fusion.cell, f32[10,32,256]{2,1,0:T(8,128)S(1)} %collective-permute-done.11.flat, f32[5,32,256]{2,1,0:T(8,128)S(1)} %collective-permute-done.12.pair, ...), custom_call_target="tpu_custom_call" | custom-call | tf_op jit(solution)/shard_map/pallas_call | solution.py:368
  (28 shorter events, 0.1 us)
Async XLA Ops:
  0.6 0.8 %copy-start.2 = (s32[1,32,256]{2,1,0:T(8,128)S(1)}, s32[1,32,256]{2,1,0:T(8,128)}, u32[]{:S(2)}) copy-start(s32[1,32,256]{2,1,0:T(8,128)} %param.5) | copy-start | bytes 98308
  0.6 0.8 %copy-start.3 = (f32[1,32,256]{2,1,0:T(8,128)S(1)}, f32[1,32,256]{2,1,0:T(8,128)}, u32[]{:S(2)}) copy-start(f32[1,32,256]{2,1,0:T(8,128)} %param.4) | copy-start | bytes 98308
  1.5 1.1 %copy-start = (f32[19,1,32,256]{3,2,1,0:T(8,128)S(1)}, f32[19,1,32,256]{3,2,1,0:T(8,128)}, u32[]{:S(2)}) copy-start(f32[19,1,32,256]{3,2,1,0:T(8,128)} %param.3) | copy-start | bytes 1867780
  2.6 3.3 %copy-start.1 = (f32[19,1,32,256]{3,2,1,0:T(8,128)S(1)}, f32[19,1,32,256]{3,2,1,0:T(8,128)}, u32[]{:S(2)}) copy-start(f32[19,1,32,256]{3,2,1,0:T(8,128)} %param.3) | copy-start | bytes 1867780
  3.0 18.4 %collective-permute-start = (f32[11,32,256]{2,1,0:T(8,128)S(1)}, f32[11,32,256]{2,1,0:T(8,128)S(1)}, u32[]{:S(2)}, u32[]{:S(2)}) collective-permute-start(f32[11,32,256]{2,1,0:T(8,128)S(1)} %get-tuple-element.25), channel_id=1, source_target_pairs={{0,4},{1,0},{2,6},{3,2},{4,5},{5,1},{6,7},{7,3},{8,12},{9,8},{10,1... | collective-permute-start | bytes 1081352 | tf_op jit(solution)/shard_map/ppermute | solution.py:456
  5.9 1.7 %collective-permute-start.1 = (f32[21,4,256]{2,1,0:T(4,128)S(1)}, f32[21,4,256]{2,1,0:T(4,128)S(1)}, u32[]{:S(2)}, u32[]{:S(2)}) collective-permute-start(f32[21,4,256]{2,1,0:T(4,128)S(1)} %get-tuple-element.26), channel_id=1, source_target_pairs={{0,1},{1,0},{2,3},{3,2},{4,5},{5,4},{6,7},{7,6},{8,9},{9,8},{10,11... | collective-permute-start | bytes 258056 | tf_op jit(solution)/shard_map/ppermute | solution.py:452
  6.0 4.3 %collective-permute-start.2 = (f32[21,4,256]{2,1,0:T(4,128)S(1)}, f32[21,4,256]{2,1,0:T(4,128)S(1)}, u32[]{:S(2)}, u32[]{:S(2)}) collective-permute-start(f32[21,4,256]{2,1,0:T(4,128)S(1)} %get-tuple-element.27), channel_id=1, source_target_pairs={{0,3},{1,2},{2,1},{3,0},{4,7},{5,6},{6,5},{7,4},{8,11},{9,10},{10,... | collective-permute-start | bytes 258056 | tf_op jit(solution)/shard_map/ppermute | solution.py:453
  10.5 9.3 %collective-permute-start.3 = (f32[5,40,256]{2,1,0:T(8,128)S(1)}, f32[5,40,256]{2,1,0:T(8,128)S(1)}, u32[]{:S(2)}, u32[]{:S(2)}) collective-permute-start(f32[5,40,256]{2,1,0:T(8,128)S(1)} %get-tuple-element.30), channel_id=1, source_target_pairs={{0,5},{1,1},{2,7},{3,3},{4,4},{5,0},{6,6},{7,2},{8,13},{9,9},{10,1... | collective-permute-start | bytes 614408 | tf_op jit(solution)/shard_map/ppermute | solution.py:470
  13.4 7.9 %collective-permute-start.4 = (f32[5,40,256]{2,1,0:T(8,128)S(1)}, f32[5,40,256]{2,1,0:T(8,128)S(1)}, u32[]{:S(2)}, u32[]{:S(2)}) collective-permute-start(f32[5,40,256]{2,1,0:T(8,128)S(1)} %get-tuple-element.31), channel_id=1, source_target_pairs={{0,29},{1,25},{2,31},{3,27},{4,12},{5,8},{6,14},{7,10},{8,5},{9,1}... | collective-permute-start | bytes 614408 | tf_op jit(solution)/shard_map/ppermute | solution.py:469
  17.3 2.6 %collective-permute-start.5 = (f32[11,8,256]{2,1,0:T(8,128)S(1)}, f32[11,8,256]{2,1,0:T(8,128)S(1)}, u32[]{:S(2)}, u32[]{:S(2)}) collective-permute-start(f32[11,8,256]{2,1,0:T(8,128)S(1)} %get-tuple-element.32), channel_id=1, source_target_pairs={{0,4},{1,0},{2,6},{3,2},{4,5},{5,1},{6,7},{7,3},{8,12},{9,8},{10,1... | collective-permute-start | bytes 270344 | tf_op jit(solution)/shard_map/ppermute | solution.py:468
  21.9 2.6 %collective-permute-start.6 = (f32[3,40,256]{2,1,0:T(8,128)S(1)}, f32[3,40,256]{2,1,0:T(8,128)S(1)}, u32[]{:S(2)}, u32[]{:S(2)}) collective-permute-start(f32[3,40,256]{2,1,0:T(8,128)S(1)} %get-tuple-element.35), channel_id=1, source_target_pairs={{4,5},{0,1},{6,7},{2,3},{5,4},{1,0},{7,6},{3,2},{12,13},{8,9},{14,... | collective-permute-start | bytes 368648 | tf_op jit(solution)/shard_map/ppermute | solution.py:483
  22.0 7.1 %collective-permute-start.7 = (f32[3,40,256]{2,1,0:T(8,128)S(1)}, f32[3,40,256]{2,1,0:T(8,128)S(1)}, u32[]{:S(2)}, u32[]{:S(2)}) collective-permute-start(f32[3,40,256]{2,1,0:T(8,128)S(1)} %get-tuple-element.36), channel_id=1, source_target_pairs={{4,29},{0,25},{6,31},{2,27},{5,12},{1,8},{7,14},{3,10},{12,5},{8,1... | collective-permute-start | bytes 368648 | tf_op jit(solution)/shard_map/ppermute | solution.py:482
  29.2 6.4 %collective-permute-start.8 = (f32[3,40,256]{2,1,0:T(8,128)S(1)}, f32[3,40,256]{2,1,0:T(8,128)S(1)}, u32[]{:S(2)}, u32[]{:S(2)}) collective-permute-start(f32[3,40,256]{2,1,0:T(8,128)S(1)} %get-tuple-element.39), channel_id=1, source_target_pairs={{4,5},{0,1},{6,7},{2,3},{5,4},{1,0},{7,6},{3,2},{12,13},{8,9},{14,... | collective-permute-start | bytes 368648 | tf_op jit(solution)/shard_map/ppermute | solution.py:496
  29.3 6.4 %collective-permute-start.9 = (f32[3,40,256]{2,1,0:T(8,128)S(1)}, f32[3,40,256]{2,1,0:T(8,128)S(1)}, u32[]{:S(2)}, u32[]{:S(2)}) collective-permute-start(f32[3,40,256]{2,1,0:T(8,128)S(1)} %get-tuple-element.40), channel_id=1, source_target_pairs={{4,29},{0,25},{6,31},{2,27},{5,12},{1,8},{7,14},{3,10},{12,5},{8,1... | collective-permute-start | bytes 368648 | tf_op jit(solution)/shard_map/ppermute | solution.py:495
  30.8 4.8 %collective-permute-start.10 = (f32[8,128]{1,0:T(8,128)S(1)}, f32[8,128]{1,0:T(8,128)S(1)}, u32[]{:S(2)}, u32[]{:S(2)}) collective-permute-start(f32[8,128]{1,0:T(8,128)S(1)} %get-tuple-element.42), channel_id=1, source_target_pairs={{0,16},{1,17},{2,18},{3,19},{4,20},{5,21},{6,22},{7,23},{8,24},{9,... | collective-permute-start | bytes 12296 | tf_op jit(solution)/shard_map/ppermute | solution.py:389
  36.5 13.9 %collective-permute-start.11 = (f32[10,32,256]{2,1,0:T(8,128)S(1)}, f32[10,32,256]{2,1,0:T(8,128)S(1)}, u32[]{:S(2)}, u32[]{:S(2)}) collective-permute-start(f32[10,32,256]{2,1,0:T(8,128)S(1)} %get-tuple-element.43), channel_id=1, source_target_pairs={{4,0},{0,1},{6,2},{2,3},{5,4},{1,5},{7,6},{3,7},{12,8},{8,9},{14,1... | collective-permute-start | bytes 983048 | tf_op jit(solution)/shard_map/ppermute | solution.py:517
  36.6 6.3 %collective-permute-start.16 = (f32[8,128]{1,0:T(8,128)S(1)}, f32[8,128]{1,0:T(8,128)S(1)}, u32[]{:S(2)}, u32[]{:S(2)}) collective-permute-start(f32[8,128]{1,0:T(8,128)S(1)} %add.34.energy), channel_id=1, source_target_pairs={{0,10},{1,11},{2,8},{3,9},{4,14},{5,15},{6,12},{7,13},{8,2},{9,3},... | collective-permute-start | bytes 12296 | tf_op jit(solution)/shard_map/ppermute | solution.py:389
  38.0 7.0 %collective-permute-start.15 = (f32[8,128]{1,0:T(8,128)S(1)}, f32[8,128]{1,0:T(8,128)S(1)}, u32[]{:S(2)}, u32[]{:S(2)}) collective-permute-start(f32[8,128]{1,0:T(8,128)S(1)} %add.34.energy), channel_id=1, source_target_pairs={{0,8},{1,9},{2,10},{3,11},{4,12},{5,13},{6,14},{7,15},{8,0},{9,1},... | collective-permute-start | bytes 12296 | tf_op jit(solution)/shard_map/ppermute | solution.py:389
  39.6 5.3 %collective-permute-start.14 = (f32[8,128]{1,0:T(8,128)S(1)}, f32[8,128]{1,0:T(8,128)S(1)}, u32[]{:S(2)}, u32[]{:S(2)}) collective-permute-start(f32[8,128]{1,0:T(8,128)S(1)} %add.34.energy), channel_id=1, source_target_pairs={{0,2},{1,3},{2,0},{3,1},{4,6},{5,7},{6,4},{7,5},{8,10},{9,11},{10,... | collective-permute-start | bytes 12296 | tf_op jit(solution)/shard_map/ppermute | solution.py:389
  40.1 9.7 %collective-permute-start.12 = (f32[5,32,256]{2,1,0:T(8,128)S(1)}, f32[5,32,256]{2,1,0:T(8,128)S(1)}, u32[]{:S(2)}, u32[]{:S(2)}) collective-permute-start(f32[5,32,256]{2,1,0:T(8,128)S(1)} %get-tuple-element.44), channel_id=1, source_target_pairs={{4,4},{0,5},{6,6},{2,7},{5,0},{1,1},{7,2},{3,3},{12,12},{8,13},{14... | collective-permute-start | bytes 491528 | tf_op jit(solution)/shard_map/ppermute | solution.py:515
  43.0 7.5 %collective-permute-start.13 = (f32[5,32,256]{2,1,0:T(8,128)S(1)}, f32[5,32,256]{2,1,0:T(8,128)S(1)}, u32[]{:S(2)}, u32[]{:S(2)}) collective-permute-start(f32[5,32,256]{2,1,0:T(8,128)S(1)} %get-tuple-element.45), channel_id=1, source_target_pairs={{4,28},{0,29},{6,30},{2,31},{5,8},{1,9},{7,10},{3,11},{12,4},{8,5}... | collective-permute-start | bytes 491528 | tf_op jit(solution)/shard_map/ppermute | solution.py:516
  45.0 3.7 %collective-permute-start.17 = (f32[8,128]{1,0:T(8,128)S(1)}, f32[8,128]{1,0:T(8,128)S(1)}, u32[]{:S(2)}, u32[]{:S(2)}) collective-permute-start(f32[8,128]{1,0:T(8,128)S(1)} %add_add_fusion), channel_id=1, source_target_pairs={{0,4},{1,5},{2,6},{3,7},{4,0},{5,1},{6,2},{7,3},{8,12},{9,13},{10,... | collective-permute-start | bytes 12296 | tf_op jit(solution)/shard_map/ppermute | solution.py:389
  48.6 1.2 %collective-permute-start.18 = (f32[8,128]{1,0:T(8,128)S(1)}, f32[8,128]{1,0:T(8,128)S(1)}, u32[]{:S(2)}, u32[]{:S(2)}) collective-permute-start(f32[8,128]{1,0:T(8,128)S(1)} %add.38), channel_id=1, source_target_pairs={{0,1},{1,0},{2,3},{3,2},{4,5},{5,4},{6,7},{7,6},{8,9},{9,8},{10,11... | collective-permute-start | bytes 12296 | tf_op jit(solution)/shard_map/ppermute | solution.py:389

commit v4 on v3

--- a/solution.py
+++ b/solution.py
@@ -11,7 +11,7 @@
 OMEGA = 0.9
 INLET_SPEED = 0.05
 HALO = 4
-ALPHA, BETA = 1, 0
+ALPHA, BETA = 0, 1
 
 
 def velocity_table():
@@ -101,56 +101,82 @@
     return [jnp.where(inlet, inlet_value(q), post[q]) for q in range(Q)], rho, u, speed
 
 
-def pull_back(lam, f, s, lab):
+def total(terms):
+    return functools.reduce(lambda a, b: a + b, terms)
+
+
+def by_moments(lam, group, u, speed):
+    near = [q for q in group if 0 < q < 7]
+    far = [q for q in group if q >= 7]
+
+    def weighted(sign):
+        out = None
+        for weight, part in ((WEIGHT[1], near), (WEIGHT[7], far)):
+            terms = sorted(((sign(VEL[q]), lam[q]) for q in part if sign(VEL[q])), key=lambda t: -t[0])
+            if terms:
+                term = weight * signed_sum(terms)
+                out = term if out is None else out + term
+        return out
+
+    s0 = weighted(lambda c: 1)
+    if 0 in group:
+        s0 = s0 + WEIGHT[0] * lam[0]
+    s1 = [weighted(lambda c: c[a]) for a in range(3)]
+    tens = {(a, b): weighted(lambda c: c[a] * c[b]) for a in range(3) for b in range(3)}
+    plus = lambda terms: total(terms) if terms else None
+    tu = [plus([tens[a, b] * u[b] for b in range(3) if tens[a, b] is not None]) for a in range(3)]
+    utu = total([tu[a] * u[a] for a in range(3) if tu[a] is not None])
+    by_rho = s0 * (1.0 + 1.5 * speed) - 4.5 * utu
+    by_mom = []
+    for a in range(3):
+        value = -3.0 * u[a] * s0
+        if tu[a] is not None:
+            value = value + 9.0 * tu[a]
+        if s1[a] is not None:
+            value = value + 3.0 * s1[a]
+        by_mom.append(value)
+    s1u = total([s1[a] * u[a] for a in range(3) if s1[a] is not None])
+    along = s0 * (1.0 - 1.5 * speed) + 3.0 * s1u + 4.5 * utu
+    return by_rho, by_mom, along
+
+
+def rates(s, lab):
+    rate = jnp.where(lab == 4.0, 1.0, OMEGA)
+    free = 1.0 - s
+    return rate, free * (1.0 - rate), free * rate
+
+
+def spread(lam, group, s, keep, g0, gm):
+    out = {}
+    for q in group:
+        o = OPP[q]
+        if q == 0:
+            out[0] = (keep + s) * lam[0] + g0
+        elif q < o:
+            along = dot_c(q, gm)
+            out[q] = keep * lam[q] + s * lam[o] + (g0 + along)
+            out[o] = keep * lam[o] + s * lam[q] + (g0 - along)
+    return out
+
+
+def pull_back(lam, f, s, lab, group):
     rho, u, speed = macroscopic(f)
-    rate = jnp.where(lab == 4.0, 1.0, OMEGA)
+    rate, keep, gain = rates(s, lab)
     inlet = lab == 3.0
     lam = [jnp.where(inlet, 0.0, v) for v in lam]
-    wsum = [None] * Q
-    s0 = WEIGHT[0] * lam[0]
-    axis_sum = functools.reduce(lambda a, b: a + b, [lam[q] for q in range(1, 7)])
-    diag_sum = functools.reduce(lambda a, b: a + b, [lam[q] for q in range(7, Q)])
-    s0 = s0 + WEIGHT[1] * axis_sum + WEIGHT[7] * diag_sum
-    s1, tens = [], {}
-    for a in range(3):
-        near = signed_sum(sorted(((VEL[q][a], lam[q]) for q in range(1, 7) if VEL[q][a]), key=lambda t: -t[0]))
-        far = signed_sum(sorted(((VEL[q][a], lam[q]) for q in range(7, Q) if VEL[q][a]), key=lambda t: -t[0]))
-        s1.append(WEIGHT[1] * near + WEIGHT[7] * far)
-        near = functools.reduce(lambda x, y: x + y, [lam[q] for q in range(1, 7) if VEL[q][a]])
-        far = functools.reduce(lambda x, y: x + y, [lam[q] for q in range(7, Q) if VEL[q][a]])
-        tens[a, a] = WEIGHT[1] * near + WEIGHT[7] * far
-    for a in range(3):
-        for b in range(a + 1, 3):
-            cross = signed_sum(sorted(((VEL[q][a] * VEL[q][b], lam[q]) for q in range(7, Q) if VEL[q][a] * VEL[q][b]), key=lambda t: -t[0]))
-            tens[a, b] = tens[b, a] = WEIGHT[7] * cross
-    tu = [tens[a, 0] * u[0] + tens[a, 1] * u[1] + tens[a, 2] * u[2] for a in range(3)]
-    utu = tu[0] * u[0] + tu[1] * u[1] + tu[2] * u[2]
-    free = 1.0 - s
-    by_rho = s0 * (1.0 + 1.5 * speed) - 4.5 * utu
-    by_mom = [3.0 * s1[a] + 9.0 * tu[a] - 3.0 * u[a] * s0 for a in range(3)]
-    keep = free * (1.0 - rate)
-    gain = free * rate
+    by_rho, by_mom, along = by_moments(lam, range(Q), u, speed)
     g0 = gain * by_rho
     gm = [gain * by_mom[a] for a in range(3)]
-    out = [None] * Q
+    out = spread(lam, group, s, keep, g0, gm)
     bounce = lam[0] * f[0]
     plain = lam[0] * f[0]
-    for q in range(Q):
+    for q in range(1, Q):
         o = OPP[q]
-        if o < q:
-            continue
-        if q == 0:
-            out[0] = (keep + s) * lam[0] + g0
-            continue
-        along = dot_c(q, gm)
-        out[q] = keep * lam[q] + s * lam[o] + (g0 + along)
-        out[o] = keep * lam[o] + s * lam[q] + (g0 - along)
-        bounce = bounce + (lam[q] * f[o] + lam[o] * f[q])
-        plain = plain + (lam[q] * f[q] + lam[o] * f[o])
-    s1u = s1[0] * u[0] + s1[1] * u[1] + s1[2] * u[2]
-    at_eq = rho * (s0 * (1.0 - 1.5 * speed) + 3.0 * s1u + 4.5 * utu)
-    by_s = bounce - (1.0 - rate) * plain - rate * at_eq
-    return out, by_s, rho, u, speed
+        if q < o:
+            bounce = bounce + (lam[q] * f[o] + lam[o] * f[q])
+            plain = plain + (lam[q] * f[q] + lam[o] * f[o])
+    by_s = bounce - (1.0 - rate) * plain - rate * (rho * along)
+    return out, by_s, rho, u, speed, (g0, gm[0], gm[1])
 
 
 def shifted(value, dx, dy):
@@ -291,15 +317,10 @@
     out[...] = total[:, :half] + total[:, half:]
 
 
-def kernel_four(odd_p, field, mine, pair, other, kinetic, energy, flat, to_pair, to_other, lam, adj):
-    rows = field.shape[1]
-    own = rows - 2 * HALO
-    odd = odd_p[0] == 1
-    low = [pick(odd, other[k], pair[k]) for k in range(3)]
-    high = [pick(odd, pair[k], other[k]) for k in range(3)]
-    for q in range(Q):
+def fill_adjoint(lam, group, sources):
+    for q in group:
         cx, cy, cz = VEL[q]
-        ref = {0: mine, 1: high, -1: low}[cz]
+        ref = sources[cz]
         value = ref[2]
         if cz == 0:
             value = -value
@@ -308,51 +329,104 @@
         if cy:
             value = value + ref[1] if cy > 0 else value - ref[1]
         lam[q] = shifted(value, -cx, -cy)
+
+
+def energy_part(q, out, two, less):
+    e = out - less
+    return e + dot_c(q, two) if q else e
+
+
+def kernel_near(field, mine, flat, near, lam, adj):
+    rows = field.shape[1]
+    own = rows - 2 * HALO
+    fill_adjoint(lam, FLAT, {0: mine})
+    for t in tiles(rows):
+        s, label = field[Q, t, :], field[Q + 1, t, :]
+        rho, u, speed = macroscopic([field[q, t, :] for q in range(Q)])
+        rate, keep, gain = rates(s, label)
+        inlet = label == 3.0
+        here = {q: jnp.where(inlet, 0.0, lam[q, t, :]) for q in FLAT}
+        by_rho, by_mom, _ = by_moments(here, FLAT, u, speed)
+        g0 = gain * by_rho
+        gm = [gain * by_mom[a] for a in range(2)]
+        near[0, t, :] = g0
+        near[1, t, :] = gm[0]
+        near[2, t, :] = gm[1]
+        out = spread(here, FLAT, s, keep, g0, gm + [None])
+        free = 1.0 - s
+        two = [2.0 * free * u[a] for a in range(3)]
+        less = free * speed
+        for i, q in enumerate(FLAT):
+            adj[i, t, :] = energy_part(q, out[q], two, less)
+    for i, q in enumerate(FLAT):
+        flat[i] = shifted(adj[i], -VEL[q][0], -VEL[q][1])[:own]
+
+
+def kernel_four(odd_p, field, mine, pair, other, kinetic, near, late, to_pair, to_other, lam, adj):
+    rows = field.shape[1]
+    own = rows - 2 * HALO
+    odd = odd_p[0] == 1
+    low = [pick(odd, other[k], pair[k]) for k in range(3)]
+    high = [pick(odd, pair[k], other[k]) for k in range(3)]
+    fill_adjoint(lam, range(Q), {0: mine, 1: high, -1: low})
     for t in tiles(rows):
         s = field[Q, t, :]
-        out, by_s, rho, u, speed = pull_back(
-            [lam[q, t, :] for q in range(Q)], [field[q, t, :] for q in range(Q)], s, field[Q + 1, t, :]
+        out, by_s, rho, u, speed, through = pull_back(
+            [lam[q, t, :] for q in range(Q)],
+            [field[q, t, :] for q in range(Q)],
+            s,
+            field[Q + 1, t, :],
+            sorted(RISE + FALL),
         )
         free = 1.0 - s
         two = [2.0 * free * u[a] for a in range(3)]
         less = free * speed
-        for q in range(Q):
-            e = out[q] - less
-            adj[q, t, :] = e + dot_c(q, two) if q else e
+        for q in RISE + FALL:
+            adj[q, t, :] = energy_part(q, out[q], two, less)
+        for k in range(3):
+            late[k, t, :] = through[k] - near[k, t, :]
         if t.start < own:
-            flat[len(FLAT), t, :] = by_s - rho * speed - kinetic[t, :]
+            late[3, t, :] = by_s - rho * speed - kinetic[t, :]
+        else:
+            late[3, t, :] = jnp.zeros_like(s)
 
     def pulled(q):
         return shifted(adj[q], -VEL[q][0], -VEL[q][1])[:own]
 
-    for i, q in enumerate(FLAT):
-        flat[i] = pulled(q)
     for i in range(len(RISE)):
         write_pair(odd, to_pair.at[i], to_other.at[i], pulled(FALL[i]), pulled(RISE[i]))
 
 
-def kernel_five(cells, odd_z, pop, cell, flat, pair, other, energy, sens_h, out_h, sens, out, sems):
+def kernel_five(cells, odd_z, pop, cell, flat, late, pair, other, energy, sens_h, out_h, sens, out, level, sems):
     own = pop.shape[1]
     odd = odd_z[0] == 1
     copies = []
-    scale = cells / jnp.sum(energy[...], keepdims=True)
+    for i, q in enumerate(FLAT):
+        cx, cy, _ = VEL[q]
+        value = late[0]
+        if cx:
+            value = value + late[1] if cx > 0 else value - late[1]
+        if cy:
+            value = value + late[2] if cy > 0 else value - late[2]
+        level[i] = flat[i] + shifted(value, -cx, -cy)[:own]
+    scale = cells / jnp.sum(jnp.sum(energy[...], axis=0), keepdims=True)
     scale = jnp.broadcast_to(scale, (8, pop.shape[2]))
     for t in tiles(own):
         s, label = cell[0, t, :], cell[1, t, :]
         lam = []
         for q in range(Q):
             if VEL[q][2] == 0:
-                lam.append(flat[FLAT.index(q), t, :])
+                lam.append(level[FLAT.index(q), t, :])
             elif VEL[q][2] == 1:
                 i = RISE.index(q)
                 lam.append(pick(odd, pair[i, t, :], other[i, t, :]))
             else:
                 i = FALL.index(q)
                 lam.append(pick(odd, other[i, t, :], pair[i, t, :]))
-        grads, by_s, _, _, _ = pull_back(lam, [pop[q, t, :] for q in range(Q)], s, label)
+        grads, by_s, _, _, _, _ = pull_back(lam, [pop[q, t, :] for q in range(Q)], s, label, range(Q))
         for q in range(Q):
             out[q, t, :] = grads[q] * scale
-        sens[t, :] = jnp.where(label == 1.0, (by_s + flat[len(FLAT), t, :]) * scale, 0.0)
+        sens[t, :] = jnp.where(label == 1.0, (by_s + late[3, t, :]) * scale, 0.0)
         n = t.start // 8
         copies.append(pltpu.make_async_copy(out.at[:, t, :], out_h.at[:, t, :], sems.at[n]))
         copies[-1].start()
@@ -376,34 +450,6 @@
         input_output_aliases=aliases or {},
         compiler_params=pltpu.CompilerParams(vmem_limit_bytes=16 * 1024 * 1024),
     )(*flags, *args)
-
-
-def summed(value, axes, groups):
-    count = lax.axis_size(axes)
-    if groups is None:
-        return value
-    for bits in groups:
-        masks = [0]
-        for bit in bits:
-            masks += [m | bit for m in masks]
-        parts = [lax.ppermute(value, axes, [(i, i ^ m) for i in range(count)]) for m in masks[1:]]
-        value = functools.reduce(lambda a, b: a + b, parts, value)
-    return value
-
-
-def doublings(count):
-    return [1 << b for b in range(count.bit_length() - 1)]
-
-
-def sum_order(planes, chunks):
-    y_bits = doublings(chunks)
-    z_bits = [chunks * d for d in doublings(planes)]
-    if 2 ** len(y_bits) != chunks or 2 ** len(z_bits) != planes:
-        return None, None
-    first = z_bits[-1:]
-    rest = z_bits[:-1]
-    late = [y_bits[1:] + rest[1:2]] + [[b] for b in rest[2:]] + [rest[:1], y_bits[:1]]
-    return [g for g in [first] if g], [g for g in late if g]
 
 
 class Layout:
@@ -494,13 +540,12 @@
     )
     other = lax.ppermute(other, axes, other_p)
     pair = lax.ppermute(pair, axes, pair_p)
-    early, late = sum_order(planes, chunks)
-    if early is None:
-        energy = lax.psum(energy, axes)
-    energy = summed(energy, axes, early)
-    flat, pair, other = call(
+    energy = jnp.broadcast_to(energy, (planes * chunks,) + energy.shape)
+    energy = lax.all_to_all(energy, axes, 0, 0, tiled=True)
+    flat, near = call(kernel_near, [less(9), whole(3)], [whole(Q), whole(9)], [], field, mine)
+    late, pair, other = call(
         kernel_four,
-        [less(10), less(5), less(5)],
+        [whole(4), less(5), less(5)],
         [whole(Q), whole(Q)],
         [odd_p],
         field,
@@ -508,22 +553,23 @@
         pair,
         other,
         kinetic,
-        energy,
+        near,
     )
     still_p, pair_p, other_p = layout.moves(layout.home, layout.start)
-    energy = summed(energy, axes, late)
+    flat = lax.ppermute(flat, axes, still_p)
     pair = lax.ppermute(pair, axes, pair_p)
     other = lax.ppermute(other, axes, other_p)
-    flat = lax.ppermute(flat, axes, still_p)
+    late = lax.ppermute(late, axes, still_p)
     cells = float(STEPS * own * wide * populations.shape[1] * planes * chunks)
     sens, out = call(
         functools.partial(kernel_five, cells),
         [(own, wide), less(Q)],
-        [(own, wide), less(Q)],
+        [(own, wide), less(Q), less(9)],
         [odd_z],
         pop,
         cell,
         flat,
+        late,
         pair,
         other,
         energy,

time: 52 us -> 50 us (0.962)
  waiting for transfers between devices: 21.5 us -> 14.3 us
  starting transfers between devices: 24.2 us -> 27.6 us
  local copies, waits for them, and re-layouts: 1.08 us -> 2 us
    ppermute x6 -> x1, waiting for transfers between devices: 9.44 us -> 0.01 us  [on_device(): late = lax.ppermute(late, axes, still_p)]
    all_to_all x0 -> x1, starting transfers between devices: none -> 5.85 us  [on_device(): energy = lax.all_to_all(energy, axes, 0, 0, tiled=True)]
    all_to_all x0 -> x1, waiting for transfers between devices: none -> 3.52 us  [on_device(): energy = lax.all_to_all(energy, axes, 0, 0, tiled=True)]
    ppermute x4, starting transfers between devices: 9.88 us -> 6.71 us  [on_device(): other = lax.ppermute(other, axes, other_p)]
    ppermute x1, starting transfers between devices: 0.01 us -> 2.88 us  [on_device(): mid_e = lax.ppermute(mid_e, axes, still_p)]
    ppermute x1, starting transfers between devices: 2.95 us -> 0.47 us  [on_device(): mid = lax.ppermute(mid, axes, still_p)]
    ppermute x6 -> x1, starting transfers between devices: 3.69 us -> 1.78 us  [on_device(): late = lax.ppermute(late, axes, still_p)]
    ppermute x1, starting transfers between devices: 0.07 us -> 1.86 us  [on_device(): lax.ppermute(edge_a, 'gy', [(k, (k + side(k)) % chunks) for k in range(ch...]
  transfers between devices with their start and end apart: 19 -> 15, of which waited for: 8 -> 5; matrix products, arithmetic and copies ran while one was open for 0% -> 1% of each run, Pallas kernels for 0% -> 2%
where the time goes in v4:
time: 50 us; the launch traced here: 49.2 us
  starting transfers between devices  27.6 us (55%)
  waiting for transfers between devices  14.3 us (29%)
  Pallas kernels  3.76 us (8%)
  local copies, waits for them, and re-layouts  2 us (4%)
  other arithmetic  0.83 us (2%)
  between operations  0.78 us (2%)
    ppermute x4, starting transfers between devices, on_device(): other = lax.ppermute(other, axes, other_p)  6.71 us
    ppermute x4, starting transfers between devices, on_device(): pair = lax.ppermute(pair, axes, pair_p)  6.62 us
    all_to_all x1, starting transfers between devices, on_device(): energy = lax.all_to_all(energy, axes, 0, 0, tiled=True)  5.85 us
    ppermute x4, waiting for transfers between devices, on_device(): other = lax.ppermute(other, axes, other_p)  5.82 us
    pallas_call x8, Pallas kernels, call(): pl.pallas_call(kernel, out_shape=[jax.ShapeDtypeStruct(s, jnp.float32) fo...  3.76 us
    all_to_all x1, waiting for transfers between devices, on_device(): energy = lax.all_to_all(energy, axes, 0, 0, tiled=True)  3.52 us
    ppermute x1, waiting for transfers between devices, on_device(): lax.ppermute(edge_b, 'gy', [(k, (k - side(k)) % chunks) for k in range(ch...  3.28 us
    ppermute x1, starting transfers between devices, on_device(): mid_e = lax.ppermute(mid_e, axes, still_p)  2.88 us
  transfers between devices with their start and end apart: 15, of which 5 were waited for; matrix products, arithmetic and copies ran while one was open for 1% of the time, Pallas kernels for 2%

profile of v4, /device:TPU:0, one launch (start us, length us, event | category | flops | bytes accessed | tf_op | source)
XLA Modules:
  0.0 49.2 jit_solution(3362427284048293468)
XLA Ops:
  0.7 0.8 %convert_element_type.4 = f32[1,32,256]{2,1,0:T(8,128)S(1)} convert(s32[1,32,256]{2,1,0:T(8,128)} %param.5) | non-fusion elementwise | flops 8192 | bytes 65536 | tf_op jit(solution)/shard_map/convert_element_type | solution.py:495
  1.5 0.0 copy-start
  1.5 1.1 %copy-done = f32[19,1,32,256]{3,2,1,0:T(8,128)S(1)} copy-done((f32[19,1,32,256]{3,2,1,0:T(8,128)S(1)}, f32[19,1,32,256]{3,2,1,0:T(8,128)}, u32[]{:S(2)}) %copy-start) | copy-done | bytes 622616
  2.6 0.4 shard_map.50
  3.0 0.5 collective-permute-start
  3.4 0.2 copy-done.1
  3.7 1.9 %collective-permute-start.1 = (f32[21,4,256]{2,1,0:T(4,128)S(1)}, f32[21,4,256]{2,1,0:T(4,128)S(1)}, u32[]{:S(2)}, u32[]{:S(2)}) collective-permute-start(f32[21,4,256]{2,1,0:T(4,128)S(1)} %get-tuple-element.28), channel_id=1, source_target_pairs={{0,1},{1,0},{2,3},{3,2},{4,5},{5,4},{6,7},{7,6},{8,9},{9,8},{10,11... | collective-permute-start | bytes 258056 | tf_op jit(solution)/shard_map/ppermute | solution.py:498
  5.6 1.3 %collective-permute-start.2 = (f32[21,4,256]{2,1,0:T(4,128)S(1)}, f32[21,4,256]{2,1,0:T(4,128)S(1)}, u32[]{:S(2)}, u32[]{:S(2)}) collective-permute-start(f32[21,4,256]{2,1,0:T(4,128)S(1)} %get-tuple-element.29), channel_id=1, source_target_pairs={{0,3},{1,2},{2,1},{3,0},{4,7},{5,6},{6,5},{7,4},{8,11},{9,10},{10,... | collective-permute-start | bytes 258056 | tf_op jit(solution)/shard_map/ppermute | solution.py:499
  6.9 0.0 collective-permute-done.1.edge_pair
  6.9 3.3 %collective-permute-done.2.edge_other = f32[21,4,256]{2,1,0:T(4,128)S(1)} collective-permute-done((f32[21,4,256]{2,1,0:T(4,128)S(1)}, f32[21,4,256]{2,1,0:T(4,128)S(1)}, u32[]{:S(2)}, u32[]{:S(2)}) %collective-permute-start.2) | collective-permute-done | bytes 86048 | tf_op jit(solution)/shard_map/ppermute | solution.py:499
  10.1 0.2 shard_map.52
  10.3 0.7 %collective-permute-start.3 = (f32[5,40,256]{2,1,0:T(8,128)S(1)}, f32[5,40,256]{2,1,0:T(8,128)S(1)}, u32[]{:S(2)}, u32[]{:S(2)}) collective-permute-start(f32[5,40,256]{2,1,0:T(8,128)S(1)} %get-tuple-element.32), channel_id=1, source_target_pairs={{0,0},{1,4},{2,2},{3,6},{4,1},{5,5},{6,3},{7,7},{8,8},{9,12},{10,1... | collective-permute-start | bytes 614408 | tf_op jit(solution)/shard_map/ppermute | solution.py:516
  11.0 3.6 %collective-permute-start.4 = (f32[5,40,256]{2,1,0:T(8,128)S(1)}, f32[5,40,256]{2,1,0:T(8,128)S(1)}, u32[]{:S(2)}, u32[]{:S(2)}) collective-permute-start(f32[5,40,256]{2,1,0:T(8,128)S(1)} %get-tuple-element.33), channel_id=1, source_target_pairs={{0,24},{1,28},{2,26},{3,30},{4,9},{5,13},{6,11},{7,15},{8,0},{9,4}... | collective-permute-start | bytes 614408 | tf_op jit(solution)/shard_map/ppermute | solution.py:515
  14.6 2.9 %collective-permute-start.5 = (f32[11,8,256]{2,1,0:T(8,128)S(1)}, f32[11,8,256]{2,1,0:T(8,128)S(1)}, u32[]{:S(2)}, u32[]{:S(2)}) collective-permute-start(f32[11,8,256]{2,1,0:T(8,128)S(1)} %get-tuple-element.34), channel_id=1, source_target_pairs={{0,1},{1,5},{2,3},{3,7},{4,0},{5,4},{6,2},{7,6},{8,9},{9,13},{10,1... | collective-permute-start | bytes 270344 | tf_op jit(solution)/shard_map/ppermute | solution.py:514
  17.4 1.7 %collective-permute-done.5.mid_e = f32[11,8,256]{2,1,0:T(8,128)S(1)} collective-permute-done((f32[11,8,256]{2,1,0:T(8,128)S(1)}, f32[11,8,256]{2,1,0:T(8,128)S(1)}, u32[]{:S(2)}, u32[]{:S(2)}) %collective-permute-start.5) | collective-permute-done | bytes 90144 | tf_op jit(solution)/shard_map/ppermute | solution.py:514
  19.1 0.5 %shard_map.53 = (f32[21,40,256]{2,1,0:T(8,128)S(1)}, f32[3,40,256]{2,1,0:T(8,128)S(1)}, f32[3,40,256]{2,1,0:T(8,128)S(1)}, f32[3,40,256]{2,1,0:T(8,128)S(1)}, f32[8,256]{1,0:T(8,128)S(1)}) custom-call(s32[1]{0:T(128)S(6)} %select_n.31.odd_p, f32[11,32,256]{2,1,0:T(8,128)S(1)} %collective-permute-done.mid, f32[5,40,256]{2,1,0:T(8,128)S(1)} %collective-permute-done.3.pair, ...), custom_call_target="tpu_custom_call" | custom-call | tf_op jit(solution)/shard_map/pallas_call | solution.py:442
  19.6 2.1 %collective-permute-start.6 = (f32[3,40,256]{2,1,0:T(8,128)S(1)}, f32[3,40,256]{2,1,0:T(8,128)S(1)}, u32[]{:S(2)}, u32[]{:S(2)}) collective-permute-start(f32[3,40,256]{2,1,0:T(8,128)S(1)} %get-tuple-element.37), channel_id=1, source_target_pairs={{1,0},{5,4},{3,2},{7,6},{0,1},{4,5},{2,3},{6,7},{9,8},{13,12},{11,... | collective-permute-start | bytes 368648 | tf_op jit(solution)/shard_map/ppermute | solution.py:529
  21.8 1.6 %collective-permute-start.7 = (f32[3,40,256]{2,1,0:T(8,128)S(1)}, f32[3,40,256]{2,1,0:T(8,128)S(1)}, u32[]{:S(2)}, u32[]{:S(2)}) collective-permute-start(f32[3,40,256]{2,1,0:T(8,128)S(1)} %get-tuple-element.38), channel_id=1, source_target_pairs={{1,24},{5,28},{3,26},{7,30},{0,9},{4,13},{2,11},{6,15},{9,0},{13,4... | collective-permute-start | bytes 368648 | tf_op jit(solution)/shard_map/ppermute | solution.py:528
  23.4 2.7 %collective-permute-done.7.other = f32[3,40,256]{2,1,0:T(8,128)S(1)} collective-permute-done((f32[3,40,256]{2,1,0:T(8,128)S(1)}, f32[3,40,256]{2,1,0:T(8,128)S(1)}, u32[]{:S(2)}, u32[]{:S(2)}) %collective-permute-start.7) | collective-permute-done | bytes 122912 | tf_op jit(solution)/shard_map/ppermute | solution.py:528
  26.1 0.1 shard_map.54
  26.2 0.4 shard_map.55
  26.6 0.1 collective-permute-start.8
  26.7 3.1 %collective-permute-start.9 = (f32[3,40,256]{2,1,0:T(8,128)S(1)}, f32[3,40,256]{2,1,0:T(8,128)S(1)}, u32[]{:S(2)}, u32[]{:S(2)}) collective-permute-start(f32[3,40,256]{2,1,0:T(8,128)S(1)} %get-tuple-element.42), channel_id=1, source_target_pairs={{1,0},{5,4},{3,2},{7,6},{0,1},{4,5},{2,3},{6,7},{9,8},{13,12},{11,... | collective-permute-start | bytes 368648 | tf_op jit(solution)/shard_map/ppermute | solution.py:542
  29.9 0.7 %broadcast_in_dim.13 = f32[32,8,128]{2,1,0:T(8,128)} broadcast(f32[8,128]{1,0:T(8,128)S(1)} %get-tuple-element.49), dimensions={1,2} | broadcast | bytes 135168 | tf_op jit(solution)/shard_map/broadcast_in_dim | solution.py:543
  30.5 5.9 %all-to-all-start = ((f32[32,8,128]{2,1,0:T(8,128)}), f32[32,8,128]{2,1,0:T(8,128)S(1)}, u32[]{:S(2)}, u32[]{:S(2)}) async-start(f32[32,8,128]{2,1,0:T(8,128)} %broadcast_in_dim.13), calls=%async_computation | async-start | bytes 262144 | tf_op jit(solution)/shard_map/all_to_all | solution.py:544
  36.4 0.7 %shard_map.56 = (f32[4,40,256]{2,1,0:T(8,128)S(1)}, f32[5,32,256]{2,1,0:T(8,128)S(1)}, f32[5,32,256]{2,1,0:T(8,128)S(1)}) custom-call(s32[1]{0:T(128)S(6)} %select_n.31.odd_p, f32[21,40,256]{2,1,0:T(8,128)S(1)} %get-tuple-element.35.field, f32[3,40,256]{2,1,0:T(8,128)S(1)} %get-tuple-element.40.mine, f32[3,40,256]{2,1,0:T(8,128)S(1)} %collective-permute-done.9.pair, ...), custom_call_target="tpu_custom_call" | custom-call | tf_op jit(solution)/shard_map/pallas_call | solution.py:442
  37.1 1.8 %collective-permute-start.11 = (f32[4,40,256]{2,1,0:T(8,128)S(1)}, f32[4,40,256]{2,1,0:T(8,128)S(1)}, u32[]{:S(2)}, u32[]{:S(2)}) collective-permute-start(f32[4,40,256]{2,1,0:T(8,128)S(1)} %get-tuple-element.46), channel_id=1, source_target_pairs={{1,0},{5,1},{3,2},{7,3},{0,4},{4,5},{2,6},{6,7},{9,8},{13,9},{11,1... | collective-permute-start | bytes 491528 | tf_op jit(solution)/shard_map/ppermute | solution.py:562
  38.9 0.7 %collective-permute-start.12 = (f32[5,32,256]{2,1,0:T(8,128)S(1)}, f32[5,32,256]{2,1,0:T(8,128)S(1)}, u32[]{:S(2)}, u32[]{:S(2)}) collective-permute-start(f32[5,32,256]{2,1,0:T(8,128)S(1)} %get-tuple-element.47), channel_id=1, source_target_pairs={{1,4},{5,5},{3,6},{7,7},{0,0},{4,1},{2,2},{6,3},{9,12},{13,13},{11... | collective-permute-start | bytes 491528 | tf_op jit(solution)/shard_map/ppermute | solution.py:560
  39.6 1.5 %collective-permute-start.13 = (f32[5,32,256]{2,1,0:T(8,128)S(1)}, f32[5,32,256]{2,1,0:T(8,128)S(1)}, u32[]{:S(2)}, u32[]{:S(2)}) collective-permute-start(f32[5,32,256]{2,1,0:T(8,128)S(1)} %get-tuple-element.48), channel_id=1, source_target_pairs={{1,28},{5,29},{3,30},{7,31},{0,8},{4,9},{2,10},{6,11},{9,4},{13,5}... | collective-permute-start | bytes 491528 | tf_op jit(solution)/shard_map/ppermute | solution.py:561
  41.1 3.5 %all-to-all-done.energy = f32[32,8,128]{2,1,0:T(8,128)S(1)} async-done(((f32[32,8,128]{2,1,0:T(8,128)}), f32[32,8,128]{2,1,0:T(8,128)S(1)}, u32[]{:S(2)}, u32[]{:S(2)}) %all-to-all-start) | async-done | bytes 131104 | tf_op jit(solution)/shard_map/all_to_all | solution.py:544
  44.6 3.1 %collective-permute-done.13.other = f32[5,32,256]{2,1,0:T(8,128)S(1)} collective-permute-done((f32[5,32,256]{2,1,0:T(8,128)S(1)}, f32[5,32,256]{2,1,0:T(8,128)S(1)}, u32[]{:S(2)}, u32[]{:S(2)}) %collective-permute-start.13) | collective-permute-done | bytes 163872 | tf_op jit(solution)/shard_map/ppermute | solution.py:561
  47.8 1.5 %shard_map.57 = (f32[32,256]{1,0:T(8,128)}, f32[19,32,256]{2,1,0:T(8,128)}) custom-call(s32[1]{0:T(128)} %bitcast.odd_z, f32[19,32,256]{2,1,0:T(8,128)S(1)} %bitcast.9, f32[2,32,256]{2,1,0:T(8,128)S(1)} %pad_maximum_fusion.cell, f32[9,32,256]{2,1,0:T(8,128)S(1)} %collective-permute-done.8.flat, f32[4,40,256]{2,1,0:T(8,128)S(1)} %collective-permute-done.11.late, ...), custom_call_target="tpu_custom_call" | custom-call | tf_op jit(solution)/shard_map/pallas_call | solution.py:442
  (18 shorter events, 0.1 us)
Async XLA Ops:
  0.6 0.8 %copy-start.2 = (s32[1,32,256]{2,1,0:T(8,128)S(1)}, s32[1,32,256]{2,1,0:T(8,128)}, u32[]{:S(2)}) copy-start(s32[1,32,256]{2,1,0:T(8,128)} %param.5) | copy-start | bytes 98308
  0.6 0.8 %copy-start.3 = (f32[1,32,256]{2,1,0:T(8,128)S(1)}, f32[1,32,256]{2,1,0:T(8,128)}, u32[]{:S(2)}) copy-start(f32[1,32,256]{2,1,0:T(8,128)} %param.4) | copy-start | bytes 98308
  1.5 1.1 %copy-start = (f32[19,1,32,256]{3,2,1,0:T(8,128)S(1)}, f32[19,1,32,256]{3,2,1,0:T(8,128)}, u32[]{:S(2)}) copy-start(f32[19,1,32,256]{3,2,1,0:T(8,128)} %param.3) | copy-start | bytes 1867780
  2.6 1.1 %copy-start.1 = (f32[19,1,32,256]{3,2,1,0:T(8,128)S(1)}, f32[19,1,32,256]{3,2,1,0:T(8,128)}, u32[]{:S(2)}) copy-start(f32[19,1,32,256]{3,2,1,0:T(8,128)} %param.3) | copy-start | bytes 1867780
  3.0 16.1 %collective-permute-start = (f32[11,32,256]{2,1,0:T(8,128)S(1)}, f32[11,32,256]{2,1,0:T(8,128)S(1)}, u32[]{:S(2)}, u32[]{:S(2)}) collective-permute-start(f32[11,32,256]{2,1,0:T(8,128)S(1)} %get-tuple-element.27), channel_id=1, source_target_pairs={{0,1},{1,5},{2,3},{3,7},{4,0},{5,4},{6,2},{7,6},{8,9},{9,13},{10,1... | collective-permute-start | bytes 1081352 | tf_op jit(solution)/shard_map/ppermute | solution.py:502
  3.7 3.2 %collective-permute-start.1 = (f32[21,4,256]{2,1,0:T(4,128)S(1)}, f32[21,4,256]{2,1,0:T(4,128)S(1)}, u32[]{:S(2)}, u32[]{:S(2)}) collective-permute-start(f32[21,4,256]{2,1,0:T(4,128)S(1)} %get-tuple-element.28), channel_id=1, source_target_pairs={{0,1},{1,0},{2,3},{3,2},{4,5},{5,4},{6,7},{7,6},{8,9},{9,8},{10,11... | collective-permute-start | bytes 258056 | tf_op jit(solution)/shard_map/ppermute | solution.py:498
  5.6 4.6 %collective-permute-start.2 = (f32[21,4,256]{2,1,0:T(4,128)S(1)}, f32[21,4,256]{2,1,0:T(4,128)S(1)}, u32[]{:S(2)}, u32[]{:S(2)}) collective-permute-start(f32[21,4,256]{2,1,0:T(4,128)S(1)} %get-tuple-element.29), channel_id=1, source_target_pairs={{0,3},{1,2},{2,1},{3,0},{4,7},{5,6},{6,5},{7,4},{8,11},{9,10},{10,... | collective-permute-start | bytes 258056 | tf_op jit(solution)/shard_map/ppermute | solution.py:499
  10.3 8.8 %collective-permute-start.3 = (f32[5,40,256]{2,1,0:T(8,128)S(1)}, f32[5,40,256]{2,1,0:T(8,128)S(1)}, u32[]{:S(2)}, u32[]{:S(2)}) collective-permute-start(f32[5,40,256]{2,1,0:T(8,128)S(1)} %get-tuple-element.32), channel_id=1, source_target_pairs={{0,0},{1,4},{2,2},{3,6},{4,1},{5,5},{6,3},{7,7},{8,8},{9,12},{10,1... | collective-permute-start | bytes 614408 | tf_op jit(solution)/shard_map/ppermute | solution.py:516
  11.0 8.1 %collective-permute-start.4 = (f32[5,40,256]{2,1,0:T(8,128)S(1)}, f32[5,40,256]{2,1,0:T(8,128)S(1)}, u32[]{:S(2)}, u32[]{:S(2)}) collective-permute-start(f32[5,40,256]{2,1,0:T(8,128)S(1)} %get-tuple-element.33), channel_id=1, source_target_pairs={{0,24},{1,28},{2,26},{3,30},{4,9},{5,13},{6,11},{7,15},{8,0},{9,4}... | collective-permute-start | bytes 614408 | tf_op jit(solution)/shard_map/ppermute | solution.py:515
  14.6 4.5 %collective-permute-start.5 = (f32[11,8,256]{2,1,0:T(8,128)S(1)}, f32[11,8,256]{2,1,0:T(8,128)S(1)}, u32[]{:S(2)}, u32[]{:S(2)}) collective-permute-start(f32[11,8,256]{2,1,0:T(8,128)S(1)} %get-tuple-element.34), channel_id=1, source_target_pairs={{0,1},{1,5},{2,3},{3,7},{4,0},{5,4},{6,2},{7,6},{8,9},{9,13},{10,1... | collective-permute-start | bytes 270344 | tf_op jit(solution)/shard_map/ppermute | solution.py:514
  19.6 3.8 %collective-permute-start.6 = (f32[3,40,256]{2,1,0:T(8,128)S(1)}, f32[3,40,256]{2,1,0:T(8,128)S(1)}, u32[]{:S(2)}, u32[]{:S(2)}) collective-permute-start(f32[3,40,256]{2,1,0:T(8,128)S(1)} %get-tuple-element.37), channel_id=1, source_target_pairs={{1,0},{5,4},{3,2},{7,6},{0,1},{4,5},{2,3},{6,7},{9,8},{13,12},{11,... | collective-permute-start | bytes 368648 | tf_op jit(solution)/shard_map/ppermute | solution.py:529
  21.8 4.3 %collective-permute-start.7 = (f32[3,40,256]{2,1,0:T(8,128)S(1)}, f32[3,40,256]{2,1,0:T(8,128)S(1)}, u32[]{:S(2)}, u32[]{:S(2)}) collective-permute-start(f32[3,40,256]{2,1,0:T(8,128)S(1)} %get-tuple-element.38), channel_id=1, source_target_pairs={{1,24},{5,28},{3,26},{7,30},{0,9},{4,13},{2,11},{6,15},{9,0},{13,4... | collective-permute-start | bytes 368648 | tf_op jit(solution)/shard_map/ppermute | solution.py:528
  26.6 21.2 %collective-permute-start.8 = (f32[9,32,256]{2,1,0:T(8,128)S(1)}, f32[9,32,256]{2,1,0:T(8,128)S(1)}, u32[]{:S(2)}, u32[]{:S(2)}) collective-permute-start(f32[9,32,256]{2,1,0:T(8,128)S(1)} %get-tuple-element.41), channel_id=1, source_target_pairs={{1,0},{5,1},{3,2},{7,3},{0,4},{4,5},{2,6},{6,7},{9,8},{13,9},{11,1... | collective-permute-start | bytes 884744 | tf_op jit(solution)/shard_map/ppermute | solution.py:559
  26.7 9.7 %collective-permute-start.9 = (f32[3,40,256]{2,1,0:T(8,128)S(1)}, f32[3,40,256]{2,1,0:T(8,128)S(1)}, u32[]{:S(2)}, u32[]{:S(2)}) collective-permute-start(f32[3,40,256]{2,1,0:T(8,128)S(1)} %get-tuple-element.42), channel_id=1, source_target_pairs={{1,0},{5,4},{3,2},{7,6},{0,1},{4,5},{2,3},{6,7},{9,8},{13,12},{11,... | collective-permute-start | bytes 368648 | tf_op jit(solution)/shard_map/ppermute | solution.py:542
  29.9 6.5 %collective-permute-start.10 = (f32[3,40,256]{2,1,0:T(8,128)S(1)}, f32[3,40,256]{2,1,0:T(8,128)S(1)}, u32[]{:S(2)}, u32[]{:S(2)}) collective-permute-start(f32[3,40,256]{2,1,0:T(8,128)S(1)} %get-tuple-element.43), channel_id=1, source_target_pairs={{1,24},{5,28},{3,26},{7,30},{0,9},{4,13},{2,11},{6,15},{9,0},{13,4... | collective-permute-start | bytes 368648 | tf_op jit(solution)/shard_map/ppermute | solution.py:541
  30.5 14.1 %all-to-all-start = ((f32[32,8,128]{2,1,0:T(8,128)}), f32[32,8,128]{2,1,0:T(8,128)S(1)}, u32[]{:S(2)}, u32[]{:S(2)}) async-start(f32[32,8,128]{2,1,0:T(8,128)} %broadcast_in_dim.13), calls=%async_computation | async-start | bytes 262144 | tf_op jit(solution)/shard_map/all_to_all | solution.py:544
  37.1 7.5 %collective-permute-start.11 = (f32[4,40,256]{2,1,0:T(8,128)S(1)}, f32[4,40,256]{2,1,0:T(8,128)S(1)}, u32[]{:S(2)}, u32[]{:S(2)}) collective-permute-start(f32[4,40,256]{2,1,0:T(8,128)S(1)} %get-tuple-element.46), channel_id=1, source_target_pairs={{1,0},{5,1},{3,2},{7,3},{0,4},{4,5},{2,6},{6,7},{9,8},{13,9},{11,1... | collective-permute-start | bytes 491528 | tf_op jit(solution)/shard_map/ppermute | solution.py:562
  38.9 5.7 %collective-permute-start.12 = (f32[5,32,256]{2,1,0:T(8,128)S(1)}, f32[5,32,256]{2,1,0:T(8,128)S(1)}, u32[]{:S(2)}, u32[]{:S(2)}) collective-permute-start(f32[5,32,256]{2,1,0:T(8,128)S(1)} %get-tuple-element.47), channel_id=1, source_target_pairs={{1,4},{5,5},{3,6},{7,7},{0,0},{4,1},{2,2},{6,3},{9,12},{13,13},{11... | collective-permute-start | bytes 491528 | tf_op jit(solution)/shard_map/ppermute | solution.py:560
  39.6 8.2 %collective-permute-start.13 = (f32[5,32,256]{2,1,0:T(8,128)S(1)}, f32[5,32,256]{2,1,0:T(8,128)S(1)}, u32[]{:S(2)}, u32[]{:S(2)}) collective-permute-start(f32[5,32,256]{2,1,0:T(8,128)S(1)} %get-tuple-element.48), channel_id=1, source_target_pairs={{1,28},{5,29},{3,30},{7,31},{0,8},{4,9},{2,10},{6,11},{9,4},{13,5}... | collective-permute-start | bytes 491528 | tf_op jit(solution)/shard_map/ppermute | solution.py:561

commit v5 on v4

--- a/solution.py
+++ b/solution.py
@@ -140,6 +140,10 @@
     return by_rho, by_mom, along
 
 
+def stored(field, t):
+    return field[Q + 2, t, :], [field[Q + 3 + a, t, :] for a in range(3)], field[Q + 6, t, :]
+
+
 def rates(s, lab):
     rate = jnp.where(lab == 4.0, 1.0, OMEGA)
     free = 1.0 - s
@@ -159,8 +163,8 @@
     return out
 
 
-def pull_back(lam, f, s, lab, group):
-    rho, u, speed = macroscopic(f)
+def pull_back(lam, f, s, lab, group, known=None):
+    rho, u, speed = known or macroscopic(f)
     rate, keep, gain = rates(s, lab)
     inlet = lab == 3.0
     lam = [jnp.where(inlet, 0.0, v) for v in lam]
@@ -200,40 +204,85 @@
     to_other[...] = pick(odd, falling, rising)
 
 
-def kernel_pack(odd_y, pop, cell, edge_pair, edge_other):
+def edge_rows(q, high):
+    if q >= Q:
+        return HALO - 1
+    cy = VEL[q][1] if high else -VEL[q][1]
+    return {0: HALO - 1, 1: HALO - 2, -1: HALO}[cy]
+
+
+def edge_slots(high):
+    slots, at = {}, 0
+    for q in range(Q + 2):
+        n = edge_rows(q, high)
+        slots[q] = (at, n)
+        at += n
+    return slots, at
+
+
+def kernel_one(odd_z, odd_y, pop, cell, edge_pair, edge_other, mid, pair, other, post):
     own = pop.shape[1]
-    oy = odd_y[0] == 1
-    for i in range(Q + 2):
-        ref = pop.at[i] if i < Q else cell.at[i - Q]
-        write_pair(oy, edge_pair.at[i], edge_other.at[i], ref[own - HALO : own, :], ref[0:HALO, :])
-
-
-def send_first(odd, f, s, label, mid, pair, other, t, r):
-    out, _, _, _ = collide(f, s, label)
-    moved = [shifted(out[q], VEL[q][0], 0) for q in range(Q)]
+    odd, oy = odd_z[0] == 1, odd_y[0] == 1
+    for t in tiles(own):
+        s, label = cell[0, t, :], cell[1, t, :]
+        out, _, _, _ = collide([pop[q, t, :] for q in range(Q)], s, label)
+        for q in range(Q):
+            post[q, t, :] = shifted(out[q], VEL[q][0], 0)
+        mid[len(FLAT), t, :] = s
+        mid[len(FLAT) + 1, t, :] = label
+    low_slots, size = edge_slots(True)
+    high_slots, _ = edge_slots(False)
+    field = lambda q: post.at[q] if q < Q else cell.at[q - Q]
+
+    def fill(to_high, to_low):
+        for q in range(Q + 2):
+            at, n = low_slots[q]
+            to_low[at : at + n, :] = field(q)[:n, :]
+            at, n = high_slots[q]
+            to_high[at : at + n, :] = field(q)[own - n : own, :]
+
+    @pl.when(oy)
+    def _():
+        fill(edge_other, edge_pair)
+
+    @pl.when(jnp.logical_not(oy))
+    def _():
+        fill(edge_pair, edge_other)
+
     for i, q in enumerate(FLAT):
-        mid[i, t, :] = moved[q]
-    mid[len(FLAT), t, :] = s
-    mid[len(FLAT) + 1, t, :] = label
+        mid[i] = post[q]
     for i in range(len(RISE)):
-        write_pair(odd, pair.at[i, r, :], other.at[i, r, :], moved[RISE[i]], moved[FALL[i]])
-
-
-def kernel_one(odd_z, pop, cell, mid, pair, other):
-    for t in tiles(pop.shape[1]):
-        send_first(odd_z[0] == 1, [pop[q, t, :] for q in range(Q)], cell[0, t, :], cell[1, t, :], mid, pair, other, t, t)
-
-
-def kernel_edge(odd_z, odd_y, edge_pair, edge_other, pair_in, other_in, mid, pair, other, tile):
+        for t in tiles(own):
+            write_pair(odd, pair.at[i, t, :], other.at[i, t, :], post[RISE[i], t, :], post[FALL[i], t, :])
+
+
+def kernel_edge(odd_z, odd_y, edge_pair, edge_other, pair_in, other_in, mid, pair, other):
     rows = pair.shape[1]
-    oy = odd_y[0] == 1
-    for i in range(Q + 2):
-        a, b = edge_pair[i], edge_other[i]
-        tile[i, :HALO, :] = pick(oy, a, b)
-        tile[i, HALO:, :] = pick(oy, b, a)
-    r = pl.ds(rows - 2 * HALO, 2 * HALO)
-    f = [tile[q] for q in range(Q)]
-    send_first(odd_z[0] == 1, f, tile[Q], tile[Q + 1], mid, pair, other, slice(None), r)
+    odd, oy = odd_z[0] == 1, odd_y[0] == 1
+    from_high, size = edge_slots(True)
+    from_low, _ = edge_slots(False)
+    zeros = lambda n: [jnp.zeros((n, pair.shape[2]), jnp.float32)] if n else []
+
+    def tile(q, high, low):
+        at, n = from_high[q]
+        top = [high[at : at + n, :]] + zeros(HALO - n)
+        at, n = from_low[q]
+        return jnp.concatenate(top + zeros(HALO - n) + [low[at : at + n, :]], axis=0)
+
+    def build(high, low):
+        for i, q in enumerate(FLAT + [Q, Q + 1]):
+            mid[i] = tile(q, high, low)
+        r = pl.ds(rows - 2 * HALO, 2 * HALO)
+        for i in range(len(RISE)):
+            write_pair(odd, pair.at[i, r, :], other.at[i, r, :], tile(RISE[i], high, low), tile(FALL[i], high, low))
+
+    @pl.when(oy)
+    def _():
+        build(edge_other, edge_pair)
+
+    @pl.when(jnp.logical_not(oy))
+    def _():
+        build(edge_pair, edge_other)
 
 
 def kernel_two(odd_p, mid, pair, other, mid_e, field, mom, to_pair, to_other, part, raw, post):
@@ -262,6 +311,8 @@
         out, rho, u, speed = collide([field[q, t, :] for q in range(Q)], s, field[Q + 1, t, :])
         for q in range(Q):
             post[q, t, :] = out[q]
+        for i, value in enumerate([rho] + u + [speed]):
+            field[Q + 2 + i, t, :] = value
         if t.start < own:
             e = (1.0 - s) * (rho * speed)
             total = e if total is None else total + e
@@ -336,13 +387,17 @@
     return e + dot_c(q, two) if q else e
 
 
-def kernel_near(field, mine, flat, near, lam, adj):
+def kernel_near(field, mine, energy, flat, near, shares, lam, adj, block, sems):
+    for i in range(block.shape[0]):
+        block[i] = energy[...]
+    copy = pltpu.make_async_copy(block, shares, sems.at[0])
+    copy.start()
     rows = field.shape[1]
     own = rows - 2 * HALO
     fill_adjoint(lam, FLAT, {0: mine})
     for t in tiles(rows):
         s, label = field[Q, t, :], field[Q + 1, t, :]
-        rho, u, speed = macroscopic([field[q, t, :] for q in range(Q)])
+        rho, u, speed = stored(field, t)
         rate, keep, gain = rates(s, label)
         inlet = label == 3.0
         here = {q: jnp.where(inlet, 0.0, lam[q, t, :]) for q in FLAT}
@@ -360,6 +415,7 @@
             adj[i, t, :] = energy_part(q, out[q], two, less)
     for i, q in enumerate(FLAT):
         flat[i] = shifted(adj[i], -VEL[q][0], -VEL[q][1])[:own]
+    copy.wait()
 
 
 def kernel_four(odd_p, field, mine, pair, other, kinetic, near, late, to_pair, to_other, lam, adj):
@@ -377,6 +433,7 @@
             s,
             field[Q + 1, t, :],
             sorted(RISE + FALL),
+            stored(field, t),
         )
         free = 1.0 - s
         two = [2.0 * free * u[a] for a in range(3)]
@@ -436,7 +493,7 @@
         c.wait()
 
 
-def call(kernel, shapes, scratch, flags, *args, hbm_out=False, sems=0, aliases=None):
+def call(kernel, shapes, scratch, flags, *args, hbm_out=0, sems=0, aliases=None):
     fast = pl.BlockSpec(memory_space=pltpu.VMEM)
     slow = pl.BlockSpec(memory_space=pltpu.HBM)
     return pl.pallas_call(
@@ -444,7 +501,7 @@
         out_shape=[jax.ShapeDtypeStruct(s, jnp.float32) for s in shapes],
         in_specs=[pl.BlockSpec(memory_space=pltpu.SMEM)] * len(flags)
         + [fast] * len(args),
-        out_specs=[slow if hbm_out else fast] * len(shapes),
+        out_specs=[fast] * (len(shapes) - hbm_out) + [slow] * hbm_out,
         scratch_shapes=[pltpu.VMEM(s, jnp.float32) for s in scratch]
         + ([pltpu.SemaphoreType.DMA((sems,))] if sems else []),
         input_output_aliases=aliases or {},
@@ -491,19 +548,27 @@
     less = lambda n: (n, own, wide)
     edge = lambda n: (n, 2 * HALO, wide)
 
-    mixed = jnp.where(lab == 1, frac, jnp.where(lab == 2, jnp.float32(1.0), jnp.float32(0.0)))
-    cell = jnp.stack([mixed, lab.astype(jnp.float32)])
-    edge_a, edge_b = call(kernel_pack, [(Q + 2, HALO, wide)] * 2, [], [odd_y], pop, cell)
+    marks = lax.optimization_barrier(lab.astype(jnp.float32))
+    mixed = jnp.where(marks == 1.0, frac, jnp.where(marks == 2.0, jnp.float32(1.0), jnp.float32(0.0)))
+    cell = jnp.stack([mixed, marks])
+    size = edge_slots(True)[1]
+    edge_a, edge_b, mid, pair, other = call(
+        kernel_one,
+        [(size, wide)] * 2 + [less(11), whole(5), whole(5)],
+        [less(Q)],
+        [odd_z, odd_y],
+        pop,
+        cell,
+    )
     side = lambda k: 1 - 2 * (k % 2)
     edge_a = lax.ppermute(edge_a, "gy", [(k, (k + side(k)) % chunks) for k in range(chunks)])
     edge_b = lax.ppermute(edge_b, "gy", [(k, (k - side(k)) % chunks) for k in range(chunks)])
-    mid, pair, other = call(kernel_one, [less(11), whole(5), whole(5)], [], [odd_z], pop, cell)
     still_p, pair_p, other_p = layout.moves(layout.start, layout.home)
     mid = lax.ppermute(mid, axes, still_p)
     mid_e, pair, other = call(
         kernel_edge,
         [edge(11), whole(5), whole(5)],
-        [edge(Q + 2)],
+        [],
         [odd_z, odd_y],
         edge_a,
         edge_b,
@@ -516,7 +581,7 @@
     pair = lax.ppermute(pair, axes, pair_p)
     field, mom, pair, other, part = call(
         kernel_two,
-        [whole(Q + 2), whole(3), whole(3), whole(3), (8, wide)],
+        [whole(Q + 7), whole(3), whole(3), whole(3), (8, wide)],
         [(rows, wide), whole(Q)],
         [odd_p],
         mid,
@@ -540,9 +605,19 @@
     )
     other = lax.ppermute(other, axes, other_p)
     pair = lax.ppermute(pair, axes, pair_p)
-    energy = jnp.broadcast_to(energy, (planes * chunks,) + energy.shape)
+    count = planes * chunks
+    flat, near, energy = call(
+        kernel_near,
+        [less(9), whole(3), (count, 8, wide // 2)],
+        [whole(Q), whole(9), (count, 8, wide // 2)],
+        [],
+        field,
+        mine,
+        energy,
+        hbm_out=1,
+        sems=1,
+    )
     energy = lax.all_to_all(energy, axes, 0, 0, tiled=True)
-    flat, near = call(kernel_near, [less(9), whole(3)], [whole(Q), whole(9)], [], field, mine)
     late, pair, other = call(
         kernel_four,
         [whole(4), less(5), less(5)],
@@ -573,7 +648,7 @@
         pair,
         other,
         energy,
-        hbm_out=True,
+        hbm_out=2,
         sems=own // 8 + 1,
     )
     return sens.reshape(solid_fraction.shape), out.reshape(populations.shape)

time: 50 us -> 49.8 us (level)
  local copies, waits for them, and re-layouts: 2 us -> 1.08 us
  other arithmetic: 0.83 us -> 1.53 us
    another operation x1 -> x2, other arithmetic: 0.01 us -> 0.77 us  [on_device(): cell = jnp.stack([mixed, marks])]
    broadcast_in_dim x1 -> x0, local copies, waits for them, and re-layouts: 0.66 us -> none  [on_device(): energy = jnp.broadcast_to(energy, (planes * chunks,) + energy.shape)]
    pallas_call x8 -> x7, Pallas kernels: 3.76 us -> 4.12 us  [call(): pl.pallas_call(kernel, out_shape=[jax.ShapeDtypeStruct(s, jnp.float32) fo...]
    unnamed x8 -> x4, local copies, waits for them, and re-layouts: 1.33 us -> 1.08 us
  transfers between devices with their start and end apart: 15 -> 15, of which waited for: 5 -> 5; matrix products, arithmetic and copies ran while one was open for 1% -> 0% of each run, Pallas kernels for 2% -> 1%
where the time goes in v5:
time: 49.8 us; the launch traced here: 49.1 us
  starting transfers between devices  27.3 us (55%)
  waiting for transfers between devices  14.3 us (29%)
  Pallas kernels  4.12 us (8%)
  other arithmetic  1.53 us (3%)
  local copies, waits for them, and re-layouts  1.08 us (2%)
  between operations  0.75 us (2%)
    ppermute x4, starting transfers between devices, on_device(): other = lax.ppermute(other, axes, other_p)  6.72 us
    ppermute x4, starting transfers between devices, on_device(): pair = lax.ppermute(pair, axes, pair_p)  6.47 us
    all_to_all x1, starting transfers between devices, on_device(): energy = lax.all_to_all(energy, axes, 0, 0, tiled=True)  5.85 us
    ppermute x4, waiting for transfers between devices, on_device(): other = lax.ppermute(other, axes, other_p)  5.81 us
    pallas_call x7, Pallas kernels, call(): pl.pallas_call(kernel, out_shape=[jax.ShapeDtypeStruct(s, jnp.float32) fo...  4.12 us
    all_to_all x1, waiting for transfers between devices, on_device(): energy = lax.all_to_all(energy, axes, 0, 0, tiled=True)  3.59 us
    ppermute x1, waiting for transfers between devices, on_device(): lax.ppermute(edge_b, 'gy', [(k, (k - side(k)) % chunks) for k in range(ch...  3.08 us
    ppermute x1, starting transfers between devices, on_device(): mid_e = lax.ppermute(mid_e, axes, still_p)  2.72 us
  transfers between devices with their start and end apart: 15, of which 5 were waited for; matrix products, arithmetic and copies ran while one was open for 0% of the time, Pallas kernels for 1%

profile of v5, /device:TPU:0, one launch (start us, length us, event | category | flops | bytes accessed | tf_op | source)
XLA Modules:
  0.0 49.1 jit_solution(14047300252595831657)
XLA Ops:
  0.6 0.8 %convert_bitcast_fusion = f32[32,256]{1,0:T(8,128)S(1)} fusion(s32[1,32,256]{2,1,0:T(8,128)} %param.5), kind=kLoop, calls=%fused_computation.3 | loop fusion | flops 8192 | bytes 65536 | tf_op jit(solution)/shard_map/convert_element_type | solution.py:551
  1.4 0.8 %fusion = f32[1,32,256]{2,1,0:T(8,128)S(1)} fusion(f32[1,32,256]{2,1,0:T(8,128)} %param.4, f32[32,256]{1,0:T(8,128)S(1)} %convert_bitcast_fusion), kind=kLoop, calls=%fused_computation.2 | loop fusion | flops 32768 | bytes 98304 | tf_op jit(solution)/shard_map/stack | solution.py:553
  2.2 0.0 copy-start
  2.2 1.1 %copy-done = f32[19,1,32,256]{3,2,1,0:T(8,128)S(1)} copy-done((f32[19,1,32,256]{3,2,1,0:T(8,128)S(1)}, f32[19,1,32,256]{3,2,1,0:T(8,128)}, u32[]{:S(2)}) %copy-start) | copy-done | bytes 622616
  3.3 0.4 shard_map.50
  3.7 0.4 collective-permute-start
  4.1 2.0 %collective-permute-start.1 = (f32[63,256]{1,0:T(8,128)S(1)}, f32[63,256]{1,0:T(8,128)S(1)}, u32[]{:S(2)}, u32[]{:S(2)}) collective-permute-start(f32[63,256]{1,0:T(8,128)S(1)} %get-tuple-element.29), channel_id=1, source_target_pairs={{0,1},{1,0},{2,3},{3,2},{4,5},{5,4},{6,7},{7,6},{8,9},{9,8},{10,11... | collective-permute-start | bytes 193544 | tf_op jit(solution)/shard_map/ppermute | solution.py:564
  6.2 1.1 %collective-permute-start.2 = (f32[63,256]{1,0:T(8,128)S(1)}, f32[63,256]{1,0:T(8,128)S(1)}, u32[]{:S(2)}, u32[]{:S(2)}) collective-permute-start(f32[63,256]{1,0:T(8,128)S(1)} %get-tuple-element.30), channel_id=1, source_target_pairs={{0,3},{1,2},{2,1},{3,0},{4,7},{5,6},{6,5},{7,4},{8,11},{9,10},{10,... | collective-permute-start | bytes 193544 | tf_op jit(solution)/shard_map/ppermute | solution.py:565
  7.3 0.0 collective-permute-done.1.edge_pair
  7.3 3.1 %collective-permute-done.2.edge_other = f32[63,256]{1,0:T(8,128)S(1)} collective-permute-done((f32[63,256]{1,0:T(8,128)S(1)}, f32[63,256]{1,0:T(8,128)S(1)}, u32[]{:S(2)}, u32[]{:S(2)}) %collective-permute-start.2) | collective-permute-done | bytes 64544 | tf_op jit(solution)/shard_map/ppermute | solution.py:565
  10.4 0.7 %collective-permute-start.3 = (f32[5,40,256]{2,1,0:T(8,128)S(1)}, f32[5,40,256]{2,1,0:T(8,128)S(1)}, u32[]{:S(2)}, u32[]{:S(2)}) collective-permute-start(f32[5,40,256]{2,1,0:T(8,128)S(1)} %get-tuple-element.33), channel_id=1, source_target_pairs={{0,0},{1,4},{2,2},{3,6},{4,1},{5,5},{6,3},{7,7},{8,8},{9,12},{10,1... | collective-permute-start | bytes 614408 | tf_op jit(solution)/shard_map/ppermute | solution.py:581
  11.1 3.7 %collective-permute-start.4 = (f32[5,40,256]{2,1,0:T(8,128)S(1)}, f32[5,40,256]{2,1,0:T(8,128)S(1)}, u32[]{:S(2)}, u32[]{:S(2)}) collective-permute-start(f32[5,40,256]{2,1,0:T(8,128)S(1)} %get-tuple-element.34), channel_id=1, source_target_pairs={{0,24},{1,28},{2,26},{3,30},{4,9},{5,13},{6,11},{7,15},{8,0},{9,4}... | collective-permute-start | bytes 614408 | tf_op jit(solution)/shard_map/ppermute | solution.py:580
  14.8 2.7 %collective-permute-start.5 = (f32[11,8,256]{2,1,0:T(8,128)S(1)}, f32[11,8,256]{2,1,0:T(8,128)S(1)}, u32[]{:S(2)}, u32[]{:S(2)}) collective-permute-start(f32[11,8,256]{2,1,0:T(8,128)S(1)} %get-tuple-element.35), channel_id=1, source_target_pairs={{0,1},{1,5},{2,3},{3,7},{4,0},{5,4},{6,2},{7,6},{8,9},{9,13},{10,1... | collective-permute-start | bytes 270344 | tf_op jit(solution)/shard_map/ppermute | solution.py:579
  17.5 1.8 %collective-permute-done.5.mid_e = f32[11,8,256]{2,1,0:T(8,128)S(1)} collective-permute-done((f32[11,8,256]{2,1,0:T(8,128)S(1)}, f32[11,8,256]{2,1,0:T(8,128)S(1)}, u32[]{:S(2)}, u32[]{:S(2)}) %collective-permute-start.5) | collective-permute-done | bytes 90144 | tf_op jit(solution)/shard_map/ppermute | solution.py:579
  19.3 0.5 %shard_map.52 = (f32[26,40,256]{2,1,0:T(8,128)S(1)}, f32[3,40,256]{2,1,0:T(8,128)S(1)}, f32[3,40,256]{2,1,0:T(8,128)S(1)}, f32[3,40,256]{2,1,0:T(8,128)S(1)}, f32[8,256]{1,0:T(8,128)S(1)}) custom-call(s32[1]{0:T(128)S(6)} %select_n.29.odd_p, f32[11,32,256]{2,1,0:T(8,128)S(1)} %collective-permute-done.mid, f32[5,40,256]{2,1,0:T(8,128)S(1)} %collective-permute-done.3.pair, ...), custom_call_target="tpu_custom_call" | custom-call | tf_op jit(solution)/shard_map/pallas_call | solution.py:499
  19.9 2.1 %collective-permute-start.6 = (f32[3,40,256]{2,1,0:T(8,128)S(1)}, f32[3,40,256]{2,1,0:T(8,128)S(1)}, u32[]{:S(2)}, u32[]{:S(2)}) collective-permute-start(f32[3,40,256]{2,1,0:T(8,128)S(1)} %get-tuple-element.38), channel_id=1, source_target_pairs={{1,0},{5,4},{3,2},{7,6},{0,1},{4,5},{2,3},{6,7},{9,8},{13,12},{11,... | collective-permute-start | bytes 368648 | tf_op jit(solution)/shard_map/ppermute | solution.py:594
  21.9 1.5 %collective-permute-start.7 = (f32[3,40,256]{2,1,0:T(8,128)S(1)}, f32[3,40,256]{2,1,0:T(8,128)S(1)}, u32[]{:S(2)}, u32[]{:S(2)}) collective-permute-start(f32[3,40,256]{2,1,0:T(8,128)S(1)} %get-tuple-element.39), channel_id=1, source_target_pairs={{1,24},{5,28},{3,26},{7,30},{0,9},{4,13},{2,11},{6,15},{9,0},{13,4... | collective-permute-start | bytes 368648 | tf_op jit(solution)/shard_map/ppermute | solution.py:593
  23.5 0.0 collective-permute-done.6.pair
  23.5 2.8 %collective-permute-done.7.other = f32[3,40,256]{2,1,0:T(8,128)S(1)} collective-permute-done((f32[3,40,256]{2,1,0:T(8,128)S(1)}, f32[3,40,256]{2,1,0:T(8,128)S(1)}, u32[]{:S(2)}, u32[]{:S(2)}) %collective-permute-start.7) | collective-permute-done | bytes 122912 | tf_op jit(solution)/shard_map/ppermute | solution.py:593
  26.2 0.1 shard_map.53
  26.3 1.0 %shard_map.54 = (f32[9,32,256]{2,1,0:T(8,128)S(1)}, f32[3,40,256]{2,1,0:T(8,128)S(1)}, f32[32,8,128]{2,1,0:T(8,128)}) custom-call(f32[26,40,256]{2,1,0:T(8,128)S(1)} %get-tuple-element.36.field, f32[3,40,256]{2,1,0:T(8,128)S(1)} %get-tuple-element.41.mine, f32[8,128]{1,0:T(8,128)S(1)} %get-tuple-element.42.energy), custom_call_target="tpu_custom_call" | custom-call | tf_op jit(solution)/shard_map/pallas_call | solution.py:499
  27.3 0.0 copy-start.1
  27.3 0.1 collective-permute-start.8
  27.4 3.1 %collective-permute-start.9 = (f32[3,40,256]{2,1,0:T(8,128)S(1)}, f32[3,40,256]{2,1,0:T(8,128)S(1)}, u32[]{:S(2)}, u32[]{:S(2)}) collective-permute-start(f32[3,40,256]{2,1,0:T(8,128)S(1)} %get-tuple-element.44), channel_id=1, source_target_pairs={{1,0},{5,4},{3,2},{7,6},{0,1},{4,5},{2,3},{6,7},{9,8},{13,12},{11,... | collective-permute-start | bytes 368648 | tf_op jit(solution)/shard_map/ppermute | solution.py:607
  30.5 5.9 %all-to-all-start = ((f32[32,8,128]{2,1,0:T(8,128)}), f32[32,8,128]{2,1,0:T(8,128)S(1)}, u32[]{:S(2)}, u32[]{:S(2)}) async-start(f32[32,8,128]{2,1,0:T(8,128)} %get-tuple-element.51), calls=%async_computation | async-start | bytes 262144 | tf_op jit(solution)/shard_map/all_to_all | solution.py:620
  36.4 0.6 %shard_map.55 = (f32[4,40,256]{2,1,0:T(8,128)S(1)}, f32[5,32,256]{2,1,0:T(8,128)S(1)}, f32[5,32,256]{2,1,0:T(8,128)S(1)}) custom-call(s32[1]{0:T(128)S(6)} %select_n.29.odd_p, f32[26,40,256]{2,1,0:T(8,128)S(1)} %get-tuple-element.36.field, f32[3,40,256]{2,1,0:T(8,128)S(1)} %get-tuple-element.41.mine, f32[3,40,256]{2,1,0:T(8,128)S(1)} %collective-permute-done.9.pair, ...), custom_call_target="tpu_custom_call" | custom-call | tf_op jit(solution)/shard_map/pallas_call | solution.py:499
  37.0 1.8 %collective-permute-start.11 = (f32[4,40,256]{2,1,0:T(8,128)S(1)}, f32[4,40,256]{2,1,0:T(8,128)S(1)}, u32[]{:S(2)}, u32[]{:S(2)}) collective-permute-start(f32[4,40,256]{2,1,0:T(8,128)S(1)} %get-tuple-element.48), channel_id=1, source_target_pairs={{1,0},{5,1},{3,2},{7,3},{0,4},{4,5},{2,6},{6,7},{9,8},{13,9},{11,1... | collective-permute-start | bytes 491528 | tf_op jit(solution)/shard_map/ppermute | solution.py:637
  38.8 0.7 %collective-permute-start.12 = (f32[5,32,256]{2,1,0:T(8,128)S(1)}, f32[5,32,256]{2,1,0:T(8,128)S(1)}, u32[]{:S(2)}, u32[]{:S(2)}) collective-permute-start(f32[5,32,256]{2,1,0:T(8,128)S(1)} %get-tuple-element.49), channel_id=1, source_target_pairs={{1,4},{5,5},{3,6},{7,7},{0,0},{4,1},{2,2},{6,3},{9,12},{13,13},{11... | collective-permute-start | bytes 491528 | tf_op jit(solution)/shard_map/ppermute | solution.py:635
  39.5 1.5 %collective-permute-start.13 = (f32[5,32,256]{2,1,0:T(8,128)S(1)}, f32[5,32,256]{2,1,0:T(8,128)S(1)}, u32[]{:S(2)}, u32[]{:S(2)}) collective-permute-start(f32[5,32,256]{2,1,0:T(8,128)S(1)} %get-tuple-element.50), channel_id=1, source_target_pairs={{1,28},{5,29},{3,30},{7,31},{0,8},{4,9},{2,10},{6,11},{9,4},{13,5}... | collective-permute-start | bytes 491528 | tf_op jit(solution)/shard_map/ppermute | solution.py:636
  41.0 3.6 %all-to-all-done.energy = f32[32,8,128]{2,1,0:T(8,128)S(1)} async-done(((f32[32,8,128]{2,1,0:T(8,128)}), f32[32,8,128]{2,1,0:T(8,128)S(1)}, u32[]{:S(2)}, u32[]{:S(2)}) %all-to-all-start) | async-done | bytes 131104 | tf_op jit(solution)/shard_map/all_to_all | solution.py:620
  44.6 3.1 %collective-permute-done.13.other = f32[5,32,256]{2,1,0:T(8,128)S(1)} collective-permute-done((f32[5,32,256]{2,1,0:T(8,128)S(1)}, f32[5,32,256]{2,1,0:T(8,128)S(1)}, u32[]{:S(2)}, u32[]{:S(2)}) %collective-permute-start.13) | collective-permute-done | bytes 163872 | tf_op jit(solution)/shard_map/ppermute | solution.py:636
  47.6 1.4 %shard_map.56 = (f32[32,256]{1,0:T(8,128)}, f32[19,32,256]{2,1,0:T(8,128)}) custom-call(s32[1]{0:T(128)} %bitcast.odd_z, f32[19,32,256]{2,1,0:T(8,128)S(1)} %bitcast.17, f32[2,32,256]{2,1,0:T(8,128)S(1)} %pad_maximum_fusion.cell, f32[9,32,256]{2,1,0:T(8,128)S(1)} %collective-permute-done.8.flat, f32[4,40,256]{2,1,0:T(8,128)S(1)} %collective-permute-done.11.late, ...), custom_call_target="tpu_custom_call" | custom-call | tf_op jit(solution)/shard_map/pallas_call | solution.py:499
  (12 shorter events, 0.1 us)
Async XLA Ops:
  2.2 1.1 %copy-start = (f32[19,1,32,256]{3,2,1,0:T(8,128)S(1)}, f32[19,1,32,256]{3,2,1,0:T(8,128)}, u32[]{:S(2)}) copy-start(f32[19,1,32,256]{3,2,1,0:T(8,128)} %param.3) | copy-start | bytes 1867780
  3.7 15.6 %collective-permute-start = (f32[11,32,256]{2,1,0:T(8,128)S(1)}, f32[11,32,256]{2,1,0:T(8,128)S(1)}, u32[]{:S(2)}, u32[]{:S(2)}) collective-permute-start(f32[11,32,256]{2,1,0:T(8,128)S(1)} %get-tuple-element.28), channel_id=1, source_target_pairs={{0,1},{1,5},{2,3},{3,7},{4,0},{5,4},{6,2},{7,6},{8,9},{9,13},{10,1... | collective-permute-start | bytes 1081352 | tf_op jit(solution)/shard_map/ppermute | solution.py:567
  4.1 3.2 %collective-permute-start.1 = (f32[63,256]{1,0:T(8,128)S(1)}, f32[63,256]{1,0:T(8,128)S(1)}, u32[]{:S(2)}, u32[]{:S(2)}) collective-permute-start(f32[63,256]{1,0:T(8,128)S(1)} %get-tuple-element.29), channel_id=1, source_target_pairs={{0,1},{1,0},{2,3},{3,2},{4,5},{5,4},{6,7},{7,6},{8,9},{9,8},{10,11... | collective-permute-start | bytes 193544 | tf_op jit(solution)/shard_map/ppermute | solution.py:564
  6.2 4.2 %collective-permute-start.2 = (f32[63,256]{1,0:T(8,128)S(1)}, f32[63,256]{1,0:T(8,128)S(1)}, u32[]{:S(2)}, u32[]{:S(2)}) collective-permute-start(f32[63,256]{1,0:T(8,128)S(1)} %get-tuple-element.30), channel_id=1, source_target_pairs={{0,3},{1,2},{2,1},{3,0},{4,7},{5,6},{6,5},{7,4},{8,11},{9,10},{10,... | collective-permute-start | bytes 193544 | tf_op jit(solution)/shard_map/ppermute | solution.py:565
  10.4 8.9 %collective-permute-start.3 = (f32[5,40,256]{2,1,0:T(8,128)S(1)}, f32[5,40,256]{2,1,0:T(8,128)S(1)}, u32[]{:S(2)}, u32[]{:S(2)}) collective-permute-start(f32[5,40,256]{2,1,0:T(8,128)S(1)} %get-tuple-element.33), channel_id=1, source_target_pairs={{0,0},{1,4},{2,2},{3,6},{4,1},{5,5},{6,3},{7,7},{8,8},{9,12},{10,1... | collective-permute-start | bytes 614408 | tf_op jit(solution)/shard_map/ppermute | solution.py:581
  11.1 8.2 %collective-permute-start.4 = (f32[5,40,256]{2,1,0:T(8,128)S(1)}, f32[5,40,256]{2,1,0:T(8,128)S(1)}, u32[]{:S(2)}, u32[]{:S(2)}) collective-permute-start(f32[5,40,256]{2,1,0:T(8,128)S(1)} %get-tuple-element.34), channel_id=1, source_target_pairs={{0,24},{1,28},{2,26},{3,30},{4,9},{5,13},{6,11},{7,15},{8,0},{9,4}... | collective-permute-start | bytes 614408 | tf_op jit(solution)/shard_map/ppermute | solution.py:580
  14.8 4.5 %collective-permute-start.5 = (f32[11,8,256]{2,1,0:T(8,128)S(1)}, f32[11,8,256]{2,1,0:T(8,128)S(1)}, u32[]{:S(2)}, u32[]{:S(2)}) collective-permute-start(f32[11,8,256]{2,1,0:T(8,128)S(1)} %get-tuple-element.35), channel_id=1, source_target_pairs={{0,1},{1,5},{2,3},{3,7},{4,0},{5,4},{6,2},{7,6},{8,9},{9,13},{10,1... | collective-permute-start | bytes 270344 | tf_op jit(solution)/shard_map/ppermute | solution.py:579
  19.9 3.6 %collective-permute-start.6 = (f32[3,40,256]{2,1,0:T(8,128)S(1)}, f32[3,40,256]{2,1,0:T(8,128)S(1)}, u32[]{:S(2)}, u32[]{:S(2)}) collective-permute-start(f32[3,40,256]{2,1,0:T(8,128)S(1)} %get-tuple-element.38), channel_id=1, source_target_pairs={{1,0},{5,4},{3,2},{7,6},{0,1},{4,5},{2,3},{6,7},{9,8},{13,12},{11,... | collective-permute-start | bytes 368648 | tf_op jit(solution)/shard_map/ppermute | solution.py:594
  21.9 4.3 %collective-permute-start.7 = (f32[3,40,256]{2,1,0:T(8,128)S(1)}, f32[3,40,256]{2,1,0:T(8,128)S(1)}, u32[]{:S(2)}, u32[]{:S(2)}) collective-permute-start(f32[3,40,256]{2,1,0:T(8,128)S(1)} %get-tuple-element.39), channel_id=1, source_target_pairs={{1,24},{5,28},{3,26},{7,30},{0,9},{4,13},{2,11},{6,15},{9,0},{13,4... | collective-permute-start | bytes 368648 | tf_op jit(solution)/shard_map/ppermute | solution.py:593
  27.3 20.4 %copy-start.1 = (f32[19,1,32,256]{3,2,1,0:T(8,128)S(1)}, f32[19,1,32,256]{3,2,1,0:T(8,128)}, u32[]{:S(2)}) copy-start(f32[19,1,32,256]{3,2,1,0:T(8,128)} %param.3) | copy-start | bytes 1867780
  27.3 20.4 %collective-permute-start.8 = (f32[9,32,256]{2,1,0:T(8,128)S(1)}, f32[9,32,256]{2,1,0:T(8,128)S(1)}, u32[]{:S(2)}, u32[]{:S(2)}) collective-permute-start(f32[9,32,256]{2,1,0:T(8,128)S(1)} %get-tuple-element.43), channel_id=1, source_target_pairs={{1,0},{5,1},{3,2},{7,3},{0,4},{4,5},{2,6},{6,7},{9,8},{13,9},{11,1... | collective-permute-start | bytes 884744 | tf_op jit(solution)/shard_map/ppermute | solution.py:634
  27.4 9.0 %collective-permute-start.9 = (f32[3,40,256]{2,1,0:T(8,128)S(1)}, f32[3,40,256]{2,1,0:T(8,128)S(1)}, u32[]{:S(2)}, u32[]{:S(2)}) collective-permute-start(f32[3,40,256]{2,1,0:T(8,128)S(1)} %get-tuple-element.44), channel_id=1, source_target_pairs={{1,0},{5,4},{3,2},{7,6},{0,1},{4,5},{2,3},{6,7},{9,8},{13,12},{11,... | collective-permute-start | bytes 368648 | tf_op jit(solution)/shard_map/ppermute | solution.py:607
  30.5 5.9 %collective-permute-start.10 = (f32[3,40,256]{2,1,0:T(8,128)S(1)}, f32[3,40,256]{2,1,0:T(8,128)S(1)}, u32[]{:S(2)}, u32[]{:S(2)}) collective-permute-start(f32[3,40,256]{2,1,0:T(8,128)S(1)} %get-tuple-element.45), channel_id=1, source_target_pairs={{1,24},{5,28},{3,26},{7,30},{0,9},{4,13},{2,11},{6,15},{9,0},{13,4... | collective-permute-start | bytes 368648 | tf_op jit(solution)/shard_map/ppermute | solution.py:606
  30.5 14.1 %all-to-all-start = ((f32[32,8,128]{2,1,0:T(8,128)}), f32[32,8,128]{2,1,0:T(8,128)S(1)}, u32[]{:S(2)}, u32[]{:S(2)}) async-start(f32[32,8,128]{2,1,0:T(8,128)} %get-tuple-element.51), calls=%async_computation | async-start | bytes 262144 | tf_op jit(solution)/shard_map/all_to_all | solution.py:620
  37.0 7.6 %collective-permute-start.11 = (f32[4,40,256]{2,1,0:T(8,128)S(1)}, f32[4,40,256]{2,1,0:T(8,128)S(1)}, u32[]{:S(2)}, u32[]{:S(2)}) collective-permute-start(f32[4,40,256]{2,1,0:T(8,128)S(1)} %get-tuple-element.48), channel_id=1, source_target_pairs={{1,0},{5,1},{3,2},{7,3},{0,4},{4,5},{2,6},{6,7},{9,8},{13,9},{11,1... | collective-permute-start | bytes 491528 | tf_op jit(solution)/shard_map/ppermute | solution.py:637
  38.8 5.8 %collective-permute-start.12 = (f32[5,32,256]{2,1,0:T(8,128)S(1)}, f32[5,32,256]{2,1,0:T(8,128)S(1)}, u32[]{:S(2)}, u32[]{:S(2)}) collective-permute-start(f32[5,32,256]{2,1,0:T(8,128)S(1)} %get-tuple-element.49), channel_id=1, source_target_pairs={{1,4},{5,5},{3,6},{7,7},{0,0},{4,1},{2,2},{6,3},{9,12},{13,13},{11... | collective-permute-start | bytes 491528 | tf_op jit(solution)/shard_map/ppermute | solution.py:635
  39.5 8.2 %collective-permute-start.13 = (f32[5,32,256]{2,1,0:T(8,128)S(1)}, f32[5,32,256]{2,1,0:T(8,128)S(1)}, u32[]{:S(2)}, u32[]{:S(2)}) collective-permute-start(f32[5,32,256]{2,1,0:T(8,128)S(1)} %get-tuple-element.50), channel_id=1, source_target_pairs={{1,28},{5,29},{3,30},{7,31},{0,8},{4,9},{2,10},{6,11},{9,4},{13,5}... | collective-permute-start | bytes 491528 | tf_op jit(solution)/shard_map/ppermute | solution.py:636

commit v6 on v5

--- a/solution.py
+++ b/solution.py
@@ -140,8 +140,8 @@
     return by_rho, by_mom, along
 
 
-def stored(field, t):
-    return field[Q + 2, t, :], [field[Q + 3 + a, t, :] for a in range(3)], field[Q + 6, t, :]
+def stored(field, t, c):
+    return field[Q + 2, t, c], [field[Q + 3 + a, t, c] for a in range(3)], field[Q + 6, t, c]
 
 
 def rates(s, lab):
@@ -191,8 +191,9 @@
     return value
 
 
-def tiles(rows):
-    return [pl.ds(8 * t, 8) for t in range(rows // 8)]
+def tiles(rows, wide):
+    half = wide // 2
+    return [(pl.ds(8 * t, 8), pl.ds(half * k, half)) for t in range(rows // 8) for k in range(2)]
 
 
 def pick(odd, first, second):
@@ -223,13 +224,16 @@
 def kernel_one(odd_z, odd_y, pop, cell, edge_pair, edge_other, mid, pair, other, post):
     own = pop.shape[1]
     odd, oy = odd_z[0] == 1, odd_y[0] == 1
-    for t in tiles(own):
-        s, label = cell[0, t, :], cell[1, t, :]
-        out, _, _, _ = collide([pop[q, t, :] for q in range(Q)], s, label)
+    for t, c in tiles(own, pop.shape[2]):
+        s, label = cell[0, t, c], cell[1, t, c]
+        out, _, _, _ = collide([pop[q, t, c] for q in range(Q)], s, label)
         for q in range(Q):
-            post[q, t, :] = shifted(out[q], VEL[q][0], 0)
-        mid[len(FLAT), t, :] = s
-        mid[len(FLAT) + 1, t, :] = label
+            post[q, t, c] = out[q]
+        mid[len(FLAT), t, c] = s
+        mid[len(FLAT) + 1, t, c] = label
+    for q in range(Q):
+        if VEL[q][0]:
+            post[q] = shifted(post[q], VEL[q][0], 0)
     low_slots, size = edge_slots(True)
     high_slots, _ = edge_slots(False)
     field = lambda q: post.at[q] if q < Q else cell.at[q - Q]
@@ -252,8 +256,8 @@
     for i, q in enumerate(FLAT):
         mid[i] = post[q]
     for i in range(len(RISE)):
-        for t in tiles(own):
-            write_pair(odd, pair.at[i, t, :], other.at[i, t, :], post[RISE[i], t, :], post[FALL[i], t, :])
+        for t, c in tiles(own, pop.shape[2]):
+            write_pair(odd, pair.at[i, t, c], other.at[i, t, c], post[RISE[i], t, c], post[FALL[i], t, c])
 
 
 def kernel_edge(odd_z, odd_y, edge_pair, edge_other, pair_in, other_in, mid, pair, other):
@@ -306,13 +310,13 @@
         field[Q + i, :own, :] = mid[len(FLAT) + i]
         field[Q + i, own:, :] = mid_e[len(FLAT) + i]
     total = None
-    for t in tiles(rows):
-        s = field[Q, t, :]
-        out, rho, u, speed = collide([field[q, t, :] for q in range(Q)], s, field[Q + 1, t, :])
+    for t, c in tiles(rows, field.shape[2]):
+        s = field[Q, t, c]
+        out, rho, u, speed = collide([field[q, t, c] for q in range(Q)], s, field[Q + 1, t, c])
         for q in range(Q):
-            post[q, t, :] = out[q]
+            post[q, t, c] = out[q]
         for i, value in enumerate([rho] + u + [speed]):
-            field[Q + 2 + i, t, :] = value
+            field[Q + 2 + i, t, c] = value
         if t.start < own:
             e = (1.0 - s) * (rho * speed)
             total = e if total is None else total + e
@@ -340,32 +344,31 @@
     own = rows - 2 * HALO
     odd = odd_p[0] == 1
     total = part[...]
-    for t in tiles(rows):
-        below = [pick(odd, other[k, t, :], pair[k, t, :]) for k in range(3)]
-        above = [pick(odd, pair[k, t, :], other[k, t, :]) for k in range(3)]
-        rho = mom[0, t, :] + below[0] + above[0]
+    for t, c in tiles(rows, field.shape[2]):
+        below = [pick(odd, other[k, t, c], pair[k, t, c]) for k in range(3)]
+        above = [pick(odd, pair[k, t, c], other[k, t, c]) for k in range(3)]
+        rho = mom[0, t, c] + below[0] + above[0]
         inv = 1.0 / rho
-        ux = (mom[1, t, :] + below[1] + above[1]) * inv
-        uy = (mom[2, t, :] + below[2] + above[2]) * inv
+        ux = (mom[1, t, c] + below[1] + above[1]) * inv
+        uy = (mom[2, t, c] + below[2] + above[2]) * inv
         uz = (below[0] - above[0]) * inv
         speed = ux * ux + uy * uy + uz * uz
-        free = 1.0 - field[Q, t, :]
+        free = 1.0 - field[Q, t, c]
         two = 2.0 * free
         ax, ay, az, b = two * ux, two * uy, two * uz, free * speed
-        mine[0, t, :] = ax
-        mine[1, t, :] = ay
-        mine[2, t, :] = b
-        to_pair[0, t, :] = ax
-        to_pair[1, t, :] = ay
-        to_other[0, t, :] = ax
-        to_other[1, t, :] = ay
-        write_pair(odd, to_pair.at[2, t, :], to_other.at[2, t, :], -az - b, az - b)
+        mine[0, t, c] = ax
+        mine[1, t, c] = ay
+        mine[2, t, c] = b
+        to_pair[0, t, c] = ax
+        to_pair[1, t, c] = ay
+        to_other[0, t, c] = ax
+        to_other[1, t, c] = ay
+        write_pair(odd, to_pair.at[2, t, c], to_other.at[2, t, c], -az - b, az - b)
         if t.start < own:
             k = rho * speed
-            kinetic[t, :] = k
+            kinetic[t, c] = k
             total = total + free * k
-    half = total.shape[1] // 2
-    out[...] = total[:, :half] + total[:, half:]
+    out[...] = total
 
 
 def fill_adjoint(lam, group, sources):
@@ -395,24 +398,24 @@
     rows = field.shape[1]
     own = rows - 2 * HALO
     fill_adjoint(lam, FLAT, {0: mine})
-    for t in tiles(rows):
-        s, label = field[Q, t, :], field[Q + 1, t, :]
-        rho, u, speed = stored(field, t)
+    for t, c in tiles(rows, field.shape[2]):
+        s, label = field[Q, t, c], field[Q + 1, t, c]
+        rho, u, speed = stored(field, t, c)
         rate, keep, gain = rates(s, label)
         inlet = label == 3.0
-        here = {q: jnp.where(inlet, 0.0, lam[q, t, :]) for q in FLAT}
+        here = {q: jnp.where(inlet, 0.0, lam[q, t, c]) for q in FLAT}
         by_rho, by_mom, _ = by_moments(here, FLAT, u, speed)
         g0 = gain * by_rho
         gm = [gain * by_mom[a] for a in range(2)]
-        near[0, t, :] = g0
-        near[1, t, :] = gm[0]
-        near[2, t, :] = gm[1]
+        near[0, t, c] = g0
+        near[1, t, c] = gm[0]
+        near[2, t, c] = gm[1]
         out = spread(here, FLAT, s, keep, g0, gm + [None])
         free = 1.0 - s
         two = [2.0 * free * u[a] for a in range(3)]
         less = free * speed
         for i, q in enumerate(FLAT):
-            adj[i, t, :] = energy_part(q, out[q], two, less)
+            adj[i, t, c] = energy_part(q, out[q], two, less)
     for i, q in enumerate(FLAT):
         flat[i] = shifted(adj[i], -VEL[q][0], -VEL[q][1])[:own]
     copy.wait()
@@ -425,27 +428,27 @@
     low = [pick(odd, other[k], pair[k]) for k in range(3)]
     high = [pick(odd, pair[k], other[k]) for k in range(3)]
     fill_adjoint(lam, range(Q), {0: mine, 1: high, -1: low})
-    for t in tiles(rows):
-        s = field[Q, t, :]
+    for t, c in tiles(rows, field.shape[2]):
+        s = field[Q, t, c]
         out, by_s, rho, u, speed, through = pull_back(
-            [lam[q, t, :] for q in range(Q)],
-            [field[q, t, :] for q in range(Q)],
+            [lam[q, t, c] for q in range(Q)],
+            [field[q, t, c] for q in range(Q)],
             s,
-            field[Q + 1, t, :],
+            field[Q + 1, t, c],
             sorted(RISE + FALL),
-            stored(field, t),
+            stored(field, t, c),
         )
         free = 1.0 - s
         two = [2.0 * free * u[a] for a in range(3)]
         less = free * speed
         for q in RISE + FALL:
-            adj[q, t, :] = energy_part(q, out[q], two, less)
+            adj[q, t, c] = energy_part(q, out[q], two, less)
         for k in range(3):
-            late[k, t, :] = through[k] - near[k, t, :]
+            late[k, t, c] = through[k] - near[k, t, c]
         if t.start < own:
-            late[3, t, :] = by_s - rho * speed - kinetic[t, :]
+            late[3, t, c] = by_s - rho * speed - kinetic[t, c]
         else:
-            late[3, t, :] = jnp.zeros_like(s)
+            late[3, t, c] = jnp.zeros_like(s)
 
     def pulled(q):
         return shifted(adj[q], -VEL[q][0], -VEL[q][1])[:own]
@@ -467,27 +470,27 @@
             value = value + late[2] if cy > 0 else value - late[2]
         level[i] = flat[i] + shifted(value, -cx, -cy)[:own]
     scale = cells / jnp.sum(jnp.sum(energy[...], axis=0), keepdims=True)
-    scale = jnp.broadcast_to(scale, (8, pop.shape[2]))
-    for t in tiles(own):
-        s, label = cell[0, t, :], cell[1, t, :]
+    scale = jnp.broadcast_to(scale, (8, pop.shape[2] // 2))
+    for t, c in tiles(own, pop.shape[2]):
+        s, label = cell[0, t, c], cell[1, t, c]
         lam = []
         for q in range(Q):
             if VEL[q][2] == 0:
-                lam.append(level[FLAT.index(q), t, :])
+                lam.append(level[FLAT.index(q), t, c])
             elif VEL[q][2] == 1:
                 i = RISE.index(q)
-                lam.append(pick(odd, pair[i, t, :], other[i, t, :]))
+                lam.append(pick(odd, pair[i, t, c], other[i, t, c]))
             else:
                 i = FALL.index(q)
-                lam.append(pick(odd, other[i, t, :], pair[i, t, :]))
-        grads, by_s, _, _, _, _ = pull_back(lam, [pop[q, t, :] for q in range(Q)], s, label, range(Q))
+                lam.append(pick(odd, other[i, t, c], pair[i, t, c]))
+        grads, by_s, _, _, _, _ = pull_back(lam, [pop[q, t, c] for q in range(Q)], s, label, range(Q))
         for q in range(Q):
-            out[q, t, :] = grads[q] * scale
-        sens[t, :] = jnp.where(label == 1.0, (by_s + late[3, t, :]) * scale, 0.0)
-        n = t.start // 8
-        copies.append(pltpu.make_async_copy(out.at[:, t, :], out_h.at[:, t, :], sems.at[n]))
+            out[q, t, c] = grads[q] * scale
+        sens[t, c] = jnp.where(label == 1.0, (by_s + late[3, t, c]) * scale, 0.0)
+        n = len(copies)
+        copies.append(pltpu.make_async_copy(out.at[:, t, c], out_h.at[:, t, c], sems.at[n]))
         copies[-1].start()
-    copies.append(pltpu.make_async_copy(sens, sens_h, sems.at[own // 8]))
+    copies.append(pltpu.make_async_copy(sens, sens_h, sems.at[own // 4]))
     copies[-1].start()
     for c in copies:
         c.wait()
@@ -581,7 +584,7 @@
     pair = lax.ppermute(pair, axes, pair_p)
     field, mom, pair, other, part = call(
         kernel_two,
-        [whole(Q + 7), whole(3), whole(3), whole(3), (8, wide)],
+        [whole(Q + 7), whole(3), whole(3), whole(3), (8, wide // 2)],
         [(rows, wide), whole(Q)],
         [odd_p],
         mid,
@@ -649,7 +652,7 @@
         other,
         energy,
         hbm_out=2,
-        sems=own // 8 + 1,
+        sems=own // 4 + 1,
     )
     return sens.reshape(solid_fraction.shape), out.reshape(populations.shape)
 

time: 49.8 us -> 49.9 us (level)
  no operation moved by 1% of the time
where the time goes in v6:
time: 49.9 us; the launch traced here: 49.1 us
  starting transfers between devices  27.3 us (55%)
  waiting for transfers between devices  14.3 us (29%)
  Pallas kernels  4.17 us (8%)
  other arithmetic  1.53 us (3%)
  local copies, waits for them, and re-layouts  1.08 us (2%)
  between operations  0.75 us (2%)
    ppermute x4, starting transfers between devices, on_device(): other = lax.ppermute(other, axes, other_p)  6.72 us
    ppermute x4, starting transfers between devices, on_device(): pair = lax.ppermute(pair, axes, pair_p)  6.47 us
    all_to_all x1, starting transfers between devices, on_device(): energy = lax.all_to_all(energy, axes, 0, 0, tiled=True)  5.85 us
    ppermute x4, waiting for transfers between devices, on_device(): other = lax.ppermute(other, axes, other_p)  5.81 us
    pallas_call x7, Pallas kernels, call(): pl.pallas_call(kernel, out_shape=[jax.ShapeDtypeStruct(s, jnp.float32) fo...  4.17 us
    all_to_all x1, waiting for transfers between devices, on_device(): energy = lax.all_to_all(energy, axes, 0, 0, tiled=True)  3.6 us
    ppermute x1, waiting for transfers between devices, on_device(): lax.ppermute(edge_b, 'gy', [(k, (k - side(k)) % chunks) for k in range(ch...  3.08 us
    ppermute x1, starting transfers between devices, on_device(): mid_e = lax.ppermute(mid_e, axes, still_p)  2.72 us
  transfers between devices with their start and end apart: 15, of which 5 were waited for; matrix products, arithmetic and copies ran while one was open for 0% of the time, Pallas kernels for 1%

profile of v6, /device:TPU:0, one launch (start us, length us, event | category | flops | bytes accessed | tf_op | source)
XLA Modules:
  0.0 49.1 jit_solution(7741348191039165336)
XLA Ops:
  0.6 0.8 %convert_bitcast_fusion = f32[32,256]{1,0:T(8,128)S(1)} fusion(s32[1,32,256]{2,1,0:T(8,128)} %param.5), kind=kLoop, calls=%fused_computation.3 | loop fusion | flops 8192 | bytes 65536 | tf_op jit(solution)/shard_map/convert_element_type | solution.py:554
  1.4 0.8 %fusion = f32[1,32,256]{2,1,0:T(8,128)S(1)} fusion(f32[1,32,256]{2,1,0:T(8,128)} %param.4, f32[32,256]{1,0:T(8,128)S(1)} %convert_bitcast_fusion), kind=kLoop, calls=%fused_computation.2 | loop fusion | flops 32768 | bytes 98304 | tf_op jit(solution)/shard_map/stack | solution.py:556
  2.2 0.0 copy-start
  2.2 1.1 %copy-done = f32[19,1,32,256]{3,2,1,0:T(8,128)S(1)} copy-done((f32[19,1,32,256]{3,2,1,0:T(8,128)S(1)}, f32[19,1,32,256]{3,2,1,0:T(8,128)}, u32[]{:S(2)}) %copy-start) | copy-done | bytes 622616
  3.3 0.5 shard_map.50
  3.7 0.4 collective-permute-start
  4.2 2.0 %collective-permute-start.1 = (f32[63,256]{1,0:T(8,128)S(1)}, f32[63,256]{1,0:T(8,128)S(1)}, u32[]{:S(2)}, u32[]{:S(2)}) collective-permute-start(f32[63,256]{1,0:T(8,128)S(1)} %get-tuple-element.29), channel_id=1, source_target_pairs={{0,1},{1,0},{2,3},{3,2},{4,5},{5,4},{6,7},{7,6},{8,9},{9,8},{10,11... | collective-permute-start | bytes 193544 | tf_op jit(solution)/shard_map/ppermute | solution.py:567
  6.2 1.1 %collective-permute-start.2 = (f32[63,256]{1,0:T(8,128)S(1)}, f32[63,256]{1,0:T(8,128)S(1)}, u32[]{:S(2)}, u32[]{:S(2)}) collective-permute-start(f32[63,256]{1,0:T(8,128)S(1)} %get-tuple-element.30), channel_id=1, source_target_pairs={{0,3},{1,2},{2,1},{3,0},{4,7},{5,6},{6,5},{7,4},{8,11},{9,10},{10,... | collective-permute-start | bytes 193544 | tf_op jit(solution)/shard_map/ppermute | solution.py:568
  7.3 0.0 collective-permute-done.1.edge_pair
  7.3 3.1 %collective-permute-done.2.edge_other = f32[63,256]{1,0:T(8,128)S(1)} collective-permute-done((f32[63,256]{1,0:T(8,128)S(1)}, f32[63,256]{1,0:T(8,128)S(1)}, u32[]{:S(2)}, u32[]{:S(2)}) %collective-permute-start.2) | collective-permute-done | bytes 64544 | tf_op jit(solution)/shard_map/ppermute | solution.py:568
  10.5 0.7 %collective-permute-start.3 = (f32[5,40,256]{2,1,0:T(8,128)S(1)}, f32[5,40,256]{2,1,0:T(8,128)S(1)}, u32[]{:S(2)}, u32[]{:S(2)}) collective-permute-start(f32[5,40,256]{2,1,0:T(8,128)S(1)} %get-tuple-element.33), channel_id=1, source_target_pairs={{0,0},{1,4},{2,2},{3,6},{4,1},{5,5},{6,3},{7,7},{8,8},{9,12},{10,1... | collective-permute-start | bytes 614408 | tf_op jit(solution)/shard_map/ppermute | solution.py:584
  11.1 3.7 %collective-permute-start.4 = (f32[5,40,256]{2,1,0:T(8,128)S(1)}, f32[5,40,256]{2,1,0:T(8,128)S(1)}, u32[]{:S(2)}, u32[]{:S(2)}) collective-permute-start(f32[5,40,256]{2,1,0:T(8,128)S(1)} %get-tuple-element.34), channel_id=1, source_target_pairs={{0,24},{1,28},{2,26},{3,30},{4,9},{5,13},{6,11},{7,15},{8,0},{9,4}... | collective-permute-start | bytes 614408 | tf_op jit(solution)/shard_map/ppermute | solution.py:583
  14.8 2.7 %collective-permute-start.5 = (f32[11,8,256]{2,1,0:T(8,128)S(1)}, f32[11,8,256]{2,1,0:T(8,128)S(1)}, u32[]{:S(2)}, u32[]{:S(2)}) collective-permute-start(f32[11,8,256]{2,1,0:T(8,128)S(1)} %get-tuple-element.35), channel_id=1, source_target_pairs={{0,1},{1,5},{2,3},{3,7},{4,0},{5,4},{6,2},{7,6},{8,9},{9,13},{10,1... | collective-permute-start | bytes 270344 | tf_op jit(solution)/shard_map/ppermute | solution.py:582
  17.5 1.8 %collective-permute-done.5.mid_e = f32[11,8,256]{2,1,0:T(8,128)S(1)} collective-permute-done((f32[11,8,256]{2,1,0:T(8,128)S(1)}, f32[11,8,256]{2,1,0:T(8,128)S(1)}, u32[]{:S(2)}, u32[]{:S(2)}) %collective-permute-start.5) | collective-permute-done | bytes 90144 | tf_op jit(solution)/shard_map/ppermute | solution.py:582
  19.3 0.0 collective-permute-done.3.pair
  19.4 0.5 %shard_map.52 = (f32[26,40,256]{2,1,0:T(8,128)S(1)}, f32[3,40,256]{2,1,0:T(8,128)S(1)}, f32[3,40,256]{2,1,0:T(8,128)S(1)}, f32[3,40,256]{2,1,0:T(8,128)S(1)}, f32[8,128]{1,0:T(8,128)S(1)}) custom-call(s32[1]{0:T(128)S(6)} %select_n.29.odd_p, f32[11,32,256]{2,1,0:T(8,128)S(1)} %collective-permute-done.mid, f32[5,40,256]{2,1,0:T(8,128)S(1)} %collective-permute-done.3.pair, ...), custom_call_target="tpu_custom_call" | custom-call | tf_op jit(solution)/shard_map/pallas_call | solution.py:502
  19.9 2.1 %collective-permute-start.6 = (f32[3,40,256]{2,1,0:T(8,128)S(1)}, f32[3,40,256]{2,1,0:T(8,128)S(1)}, u32[]{:S(2)}, u32[]{:S(2)}) collective-permute-start(f32[3,40,256]{2,1,0:T(8,128)S(1)} %get-tuple-element.38), channel_id=1, source_target_pairs={{1,0},{5,4},{3,2},{7,6},{0,1},{4,5},{2,3},{6,7},{9,8},{13,12},{11,... | collective-permute-start | bytes 368648 | tf_op jit(solution)/shard_map/ppermute | solution.py:597
  21.9 1.5 %collective-permute-start.7 = (f32[3,40,256]{2,1,0:T(8,128)S(1)}, f32[3,40,256]{2,1,0:T(8,128)S(1)}, u32[]{:S(2)}, u32[]{:S(2)}) collective-permute-start(f32[3,40,256]{2,1,0:T(8,128)S(1)} %get-tuple-element.39), channel_id=1, source_target_pairs={{1,24},{5,28},{3,26},{7,30},{0,9},{4,13},{2,11},{6,15},{9,0},{13,4... | collective-permute-start | bytes 368648 | tf_op jit(solution)/shard_map/ppermute | solution.py:596
  23.5 2.8 %collective-permute-done.7.other = f32[3,40,256]{2,1,0:T(8,128)S(1)} collective-permute-done((f32[3,40,256]{2,1,0:T(8,128)S(1)}, f32[3,40,256]{2,1,0:T(8,128)S(1)}, u32[]{:S(2)}, u32[]{:S(2)}) %collective-permute-start.7) | collective-permute-done | bytes 122912 | tf_op jit(solution)/shard_map/ppermute | solution.py:596
  26.3 0.1 shard_map.53
  26.3 1.0 %shard_map.54 = (f32[9,32,256]{2,1,0:T(8,128)S(1)}, f32[3,40,256]{2,1,0:T(8,128)S(1)}, f32[32,8,128]{2,1,0:T(8,128)}) custom-call(f32[26,40,256]{2,1,0:T(8,128)S(1)} %get-tuple-element.36.field, f32[3,40,256]{2,1,0:T(8,128)S(1)} %get-tuple-element.41.mine, f32[8,128]{1,0:T(8,128)S(1)} %get-tuple-element.42.energy), custom_call_target="tpu_custom_call" | custom-call | tf_op jit(solution)/shard_map/pallas_call | solution.py:502
  27.3 0.0 copy-start.1
  27.3 0.1 collective-permute-start.8
  27.4 3.1 %collective-permute-start.9 = (f32[3,40,256]{2,1,0:T(8,128)S(1)}, f32[3,40,256]{2,1,0:T(8,128)S(1)}, u32[]{:S(2)}, u32[]{:S(2)}) collective-permute-start(f32[3,40,256]{2,1,0:T(8,128)S(1)} %get-tuple-element.44), channel_id=1, source_target_pairs={{1,0},{5,4},{3,2},{7,6},{0,1},{4,5},{2,3},{6,7},{9,8},{13,12},{11,... | collective-permute-start | bytes 368648 | tf_op jit(solution)/shard_map/ppermute | solution.py:610
  30.5 5.9 %all-to-all-start = ((f32[32,8,128]{2,1,0:T(8,128)}), f32[32,8,128]{2,1,0:T(8,128)S(1)}, u32[]{:S(2)}, u32[]{:S(2)}) async-start(f32[32,8,128]{2,1,0:T(8,128)} %get-tuple-element.51), calls=%async_computation | async-start | bytes 262144 | tf_op jit(solution)/shard_map/all_to_all | solution.py:623
  36.4 0.6 %shard_map.55 = (f32[4,40,256]{2,1,0:T(8,128)S(1)}, f32[5,32,256]{2,1,0:T(8,128)S(1)}, f32[5,32,256]{2,1,0:T(8,128)S(1)}) custom-call(s32[1]{0:T(128)S(6)} %select_n.29.odd_p, f32[26,40,256]{2,1,0:T(8,128)S(1)} %get-tuple-element.36.field, f32[3,40,256]{2,1,0:T(8,128)S(1)} %get-tuple-element.41.mine, f32[3,40,256]{2,1,0:T(8,128)S(1)} %collective-permute-done.9.pair, ...), custom_call_target="tpu_custom_call" | custom-call | tf_op jit(solution)/shard_map/pallas_call | solution.py:502
  37.0 1.8 %collective-permute-start.11 = (f32[4,40,256]{2,1,0:T(8,128)S(1)}, f32[4,40,256]{2,1,0:T(8,128)S(1)}, u32[]{:S(2)}, u32[]{:S(2)}) collective-permute-start(f32[4,40,256]{2,1,0:T(8,128)S(1)} %get-tuple-element.48), channel_id=1, source_target_pairs={{1,0},{5,1},{3,2},{7,3},{0,4},{4,5},{2,6},{6,7},{9,8},{13,9},{11,1... | collective-permute-start | bytes 491528 | tf_op jit(solution)/shard_map/ppermute | solution.py:640
  38.8 0.7 %collective-permute-start.12 = (f32[5,32,256]{2,1,0:T(8,128)S(1)}, f32[5,32,256]{2,1,0:T(8,128)S(1)}, u32[]{:S(2)}, u32[]{:S(2)}) collective-permute-start(f32[5,32,256]{2,1,0:T(8,128)S(1)} %get-tuple-element.49), channel_id=1, source_target_pairs={{1,4},{5,5},{3,6},{7,7},{0,0},{4,1},{2,2},{6,3},{9,12},{13,13},{11... | collective-permute-start | bytes 491528 | tf_op jit(solution)/shard_map/ppermute | solution.py:638
  39.5 1.5 %collective-permute-start.13 = (f32[5,32,256]{2,1,0:T(8,128)S(1)}, f32[5,32,256]{2,1,0:T(8,128)S(1)}, u32[]{:S(2)}, u32[]{:S(2)}) collective-permute-start(f32[5,32,256]{2,1,0:T(8,128)S(1)} %get-tuple-element.50), channel_id=1, source_target_pairs={{1,28},{5,29},{3,30},{7,31},{0,8},{4,9},{2,10},{6,11},{9,4},{13,5}... | collective-permute-start | bytes 491528 | tf_op jit(solution)/shard_map/ppermute | solution.py:639
  41.0 3.6 %all-to-all-done.energy = f32[32,8,128]{2,1,0:T(8,128)S(1)} async-done(((f32[32,8,128]{2,1,0:T(8,128)}), f32[32,8,128]{2,1,0:T(8,128)S(1)}, u32[]{:S(2)}, u32[]{:S(2)}) %all-to-all-start) | async-done | bytes 131104 | tf_op jit(solution)/shard_map/all_to_all | solution.py:623
  44.6 3.0 %collective-permute-done.13.other = f32[5,32,256]{2,1,0:T(8,128)S(1)} collective-permute-done((f32[5,32,256]{2,1,0:T(8,128)S(1)}, f32[5,32,256]{2,1,0:T(8,128)S(1)}, u32[]{:S(2)}, u32[]{:S(2)}) %collective-permute-start.13) | collective-permute-done | bytes 163872 | tf_op jit(solution)/shard_map/ppermute | solution.py:639
  47.7 1.5 %shard_map.56 = (f32[32,256]{1,0:T(8,128)}, f32[19,32,256]{2,1,0:T(8,128)}) custom-call(s32[1]{0:T(128)} %bitcast.odd_z, f32[19,32,256]{2,1,0:T(8,128)S(1)} %bitcast.17, f32[2,32,256]{2,1,0:T(8,128)S(1)} %pad_maximum_fusion.cell, f32[9,32,256]{2,1,0:T(8,128)S(1)} %collective-permute-done.8.flat, f32[4,40,256]{2,1,0:T(8,128)S(1)} %collective-permute-done.11.late, ...), custom_call_target="tpu_custom_call" | custom-call | tf_op jit(solution)/shard_map/pallas_call | solution.py:502
  (12 shorter events, 0.1 us)
Async XLA Ops:
  2.2 1.1 %copy-start = (f32[19,1,32,256]{3,2,1,0:T(8,128)S(1)}, f32[19,1,32,256]{3,2,1,0:T(8,128)}, u32[]{:S(2)}) copy-start(f32[19,1,32,256]{3,2,1,0:T(8,128)} %param.3) | copy-start | bytes 1867780
  3.7 15.6 %collective-permute-start = (f32[11,32,256]{2,1,0:T(8,128)S(1)}, f32[11,32,256]{2,1,0:T(8,128)S(1)}, u32[]{:S(2)}, u32[]{:S(2)}) collective-permute-start(f32[11,32,256]{2,1,0:T(8,128)S(1)} %get-tuple-element.28), channel_id=1, source_target_pairs={{0,1},{1,5},{2,3},{3,7},{4,0},{5,4},{6,2},{7,6},{8,9},{9,13},{10,1... | collective-permute-start | bytes 1081352 | tf_op jit(solution)/shard_map/ppermute | solution.py:570
  4.2 3.2 %collective-permute-start.1 = (f32[63,256]{1,0:T(8,128)S(1)}, f32[63,256]{1,0:T(8,128)S(1)}, u32[]{:S(2)}, u32[]{:S(2)}) collective-permute-start(f32[63,256]{1,0:T(8,128)S(1)} %get-tuple-element.29), channel_id=1, source_target_pairs={{0,1},{1,0},{2,3},{3,2},{4,5},{5,4},{6,7},{7,6},{8,9},{9,8},{10,11... | collective-permute-start | bytes 193544 | tf_op jit(solution)/shard_map/ppermute | solution.py:567
  6.2 4.2 %collective-permute-start.2 = (f32[63,256]{1,0:T(8,128)S(1)}, f32[63,256]{1,0:T(8,128)S(1)}, u32[]{:S(2)}, u32[]{:S(2)}) collective-permute-start(f32[63,256]{1,0:T(8,128)S(1)} %get-tuple-element.30), channel_id=1, source_target_pairs={{0,3},{1,2},{2,1},{3,0},{4,7},{5,6},{6,5},{7,4},{8,11},{9,10},{10,... | collective-permute-start | bytes 193544 | tf_op jit(solution)/shard_map/ppermute | solution.py:568
  10.5 8.9 %collective-permute-start.3 = (f32[5,40,256]{2,1,0:T(8,128)S(1)}, f32[5,40,256]{2,1,0:T(8,128)S(1)}, u32[]{:S(2)}, u32[]{:S(2)}) collective-permute-start(f32[5,40,256]{2,1,0:T(8,128)S(1)} %get-tuple-element.33), channel_id=1, source_target_pairs={{0,0},{1,4},{2,2},{3,6},{4,1},{5,5},{6,3},{7,7},{8,8},{9,12},{10,1... | collective-permute-start | bytes 614408 | tf_op jit(solution)/shard_map/ppermute | solution.py:584
  11.1 8.2 %collective-permute-start.4 = (f32[5,40,256]{2,1,0:T(8,128)S(1)}, f32[5,40,256]{2,1,0:T(8,128)S(1)}, u32[]{:S(2)}, u32[]{:S(2)}) collective-permute-start(f32[5,40,256]{2,1,0:T(8,128)S(1)} %get-tuple-element.34), channel_id=1, source_target_pairs={{0,24},{1,28},{2,26},{3,30},{4,9},{5,13},{6,11},{7,15},{8,0},{9,4}... | collective-permute-start | bytes 614408 | tf_op jit(solution)/shard_map/ppermute | solution.py:583
  14.8 4.5 %collective-permute-start.5 = (f32[11,8,256]{2,1,0:T(8,128)S(1)}, f32[11,8,256]{2,1,0:T(8,128)S(1)}, u32[]{:S(2)}, u32[]{:S(2)}) collective-permute-start(f32[11,8,256]{2,1,0:T(8,128)S(1)} %get-tuple-element.35), channel_id=1, source_target_pairs={{0,1},{1,5},{2,3},{3,7},{4,0},{5,4},{6,2},{7,6},{8,9},{9,13},{10,1... | collective-permute-start | bytes 270344 | tf_op jit(solution)/shard_map/ppermute | solution.py:582
  19.9 3.6 %collective-permute-start.6 = (f32[3,40,256]{2,1,0:T(8,128)S(1)}, f32[3,40,256]{2,1,0:T(8,128)S(1)}, u32[]{:S(2)}, u32[]{:S(2)}) collective-permute-start(f32[3,40,256]{2,1,0:T(8,128)S(1)} %get-tuple-element.38), channel_id=1, source_target_pairs={{1,0},{5,4},{3,2},{7,6},{0,1},{4,5},{2,3},{6,7},{9,8},{13,12},{11,... | collective-permute-start | bytes 368648 | tf_op jit(solution)/shard_map/ppermute | solution.py:597
  21.9 4.3 %collective-permute-start.7 = (f32[3,40,256]{2,1,0:T(8,128)S(1)}, f32[3,40,256]{2,1,0:T(8,128)S(1)}, u32[]{:S(2)}, u32[]{:S(2)}) collective-permute-start(f32[3,40,256]{2,1,0:T(8,128)S(1)} %get-tuple-element.39), channel_id=1, source_target_pairs={{1,24},{5,28},{3,26},{7,30},{0,9},{4,13},{2,11},{6,15},{9,0},{13,4... | collective-permute-start | bytes 368648 | tf_op jit(solution)/shard_map/ppermute | solution.py:596
  27.3 20.4 %copy-start.1 = (f32[19,1,32,256]{3,2,1,0:T(8,128)S(1)}, f32[19,1,32,256]{3,2,1,0:T(8,128)}, u32[]{:S(2)}) copy-start(f32[19,1,32,256]{3,2,1,0:T(8,128)} %param.3) | copy-start | bytes 1867780
  27.3 20.4 %collective-permute-start.8 = (f32[9,32,256]{2,1,0:T(8,128)S(1)}, f32[9,32,256]{2,1,0:T(8,128)S(1)}, u32[]{:S(2)}, u32[]{:S(2)}) collective-permute-start(f32[9,32,256]{2,1,0:T(8,128)S(1)} %get-tuple-element.43), channel_id=1, source_target_pairs={{1,0},{5,1},{3,2},{7,3},{0,4},{4,5},{2,6},{6,7},{9,8},{13,9},{11,1... | collective-permute-start | bytes 884744 | tf_op jit(solution)/shard_map/ppermute | solution.py:637
  27.4 8.9 %collective-permute-start.9 = (f32[3,40,256]{2,1,0:T(8,128)S(1)}, f32[3,40,256]{2,1,0:T(8,128)S(1)}, u32[]{:S(2)}, u32[]{:S(2)}) collective-permute-start(f32[3,40,256]{2,1,0:T(8,128)S(1)} %get-tuple-element.44), channel_id=1, source_target_pairs={{1,0},{5,4},{3,2},{7,6},{0,1},{4,5},{2,3},{6,7},{9,8},{13,12},{11,... | collective-permute-start | bytes 368648 | tf_op jit(solution)/shard_map/ppermute | solution.py:610
  30.5 5.9 %collective-permute-start.10 = (f32[3,40,256]{2,1,0:T(8,128)S(1)}, f32[3,40,256]{2,1,0:T(8,128)S(1)}, u32[]{:S(2)}, u32[]{:S(2)}) collective-permute-start(f32[3,40,256]{2,1,0:T(8,128)S(1)} %get-tuple-element.45), channel_id=1, source_target_pairs={{1,24},{5,28},{3,26},{7,30},{0,9},{4,13},{2,11},{6,15},{9,0},{13,4... | collective-permute-start | bytes 368648 | tf_op jit(solution)/shard_map/ppermute | solution.py:609
  30.5 14.1 %all-to-all-start = ((f32[32,8,128]{2,1,0:T(8,128)}), f32[32,8,128]{2,1,0:T(8,128)S(1)}, u32[]{:S(2)}, u32[]{:S(2)}) async-start(f32[32,8,128]{2,1,0:T(8,128)} %get-tuple-element.51), calls=%async_computation | async-start | bytes 262144 | tf_op jit(solution)/shard_map/all_to_all | solution.py:623
  37.0 7.6 %collective-permute-start.11 = (f32[4,40,256]{2,1,0:T(8,128)S(1)}, f32[4,40,256]{2,1,0:T(8,128)S(1)}, u32[]{:S(2)}, u32[]{:S(2)}) collective-permute-start(f32[4,40,256]{2,1,0:T(8,128)S(1)} %get-tuple-element.48), channel_id=1, source_target_pairs={{1,0},{5,1},{3,2},{7,3},{0,4},{4,5},{2,6},{6,7},{9,8},{13,9},{11,1... | collective-permute-start | bytes 491528 | tf_op jit(solution)/shard_map/ppermute | solution.py:640
  38.8 5.8 %collective-permute-start.12 = (f32[5,32,256]{2,1,0:T(8,128)S(1)}, f32[5,32,256]{2,1,0:T(8,128)S(1)}, u32[]{:S(2)}, u32[]{:S(2)}) collective-permute-start(f32[5,32,256]{2,1,0:T(8,128)S(1)} %get-tuple-element.49), channel_id=1, source_target_pairs={{1,4},{5,5},{3,6},{7,7},{0,0},{4,1},{2,2},{6,3},{9,12},{13,13},{11... | collective-permute-start | bytes 491528 | tf_op jit(solution)/shard_map/ppermute | solution.py:638
  39.5 8.2 %collective-permute-start.13 = (f32[5,32,256]{2,1,0:T(8,128)S(1)}, f32[5,32,256]{2,1,0:T(8,128)S(1)}, u32[]{:S(2)}, u32[]{:S(2)}) collective-permute-start(f32[5,32,256]{2,1,0:T(8,128)S(1)} %get-tuple-element.50), channel_id=1, source_target_pairs={{1,28},{5,29},{3,30},{7,31},{0,8},{4,9},{2,10},{6,11},{9,4},{13,5}... | collective-permute-start | bytes 491528 | tf_op jit(solution)/shard_map/ppermute | solution.py:639

commit v7 on v6

--- a/solution.py
+++ b/solution.py
@@ -191,6 +191,10 @@
     return value
 
 
+def bands(rows):
+    return [pl.ds(8 * t, 8) for t in range(rows // 8)]
+
+
 def tiles(rows, wide):
     half = wide // 2
     return [(pl.ds(8 * t, 8), pl.ds(half * k, half)) for t in range(rows // 8) for k in range(2)]
@@ -224,16 +228,13 @@
 def kernel_one(odd_z, odd_y, pop, cell, edge_pair, edge_other, mid, pair, other, post):
     own = pop.shape[1]
     odd, oy = odd_z[0] == 1, odd_y[0] == 1
-    for t, c in tiles(own, pop.shape[2]):
-        s, label = cell[0, t, c], cell[1, t, c]
-        out, _, _, _ = collide([pop[q, t, c] for q in range(Q)], s, label)
+    for t in bands(own):
+        s, label = cell[0, t, :], cell[1, t, :]
+        out, _, _, _ = collide([pop[q, t, :] for q in range(Q)], s, label)
         for q in range(Q):
-            post[q, t, c] = out[q]
-        mid[len(FLAT), t, c] = s
-        mid[len(FLAT) + 1, t, c] = label
-    for q in range(Q):
-        if VEL[q][0]:
-            post[q] = shifted(post[q], VEL[q][0], 0)
+            post[q, t, :] = shifted(out[q], VEL[q][0], 0)
+        mid[len(FLAT), t, :] = s
+        mid[len(FLAT) + 1, t, :] = label
     low_slots, size = edge_slots(True)
     high_slots, _ = edge_slots(False)
     field = lambda q: post.at[q] if q < Q else cell.at[q - Q]
@@ -256,8 +257,8 @@
     for i, q in enumerate(FLAT):
         mid[i] = post[q]
     for i in range(len(RISE)):
-        for t, c in tiles(own, pop.shape[2]):
-            write_pair(odd, pair.at[i, t, c], other.at[i, t, c], post[RISE[i], t, c], post[FALL[i], t, c])
+        for t in bands(own):
+            write_pair(odd, pair.at[i, t, :], other.at[i, t, :], post[RISE[i], t, :], post[FALL[i], t, :])
 
 
 def kernel_edge(odd_z, odd_y, edge_pair, edge_other, pair_in, other_in, mid, pair, other):
@@ -470,27 +471,27 @@
             value = value + late[2] if cy > 0 else value - late[2]
         level[i] = flat[i] + shifted(value, -cx, -cy)[:own]
     scale = cells / jnp.sum(jnp.sum(energy[...], axis=0), keepdims=True)
-    scale = jnp.broadcast_to(scale, (8, pop.shape[2] // 2))
-    for t, c in tiles(own, pop.shape[2]):
-        s, label = cell[0, t, c], cell[1, t, c]
+    scale = jnp.broadcast_to(scale, (8, pop.shape[2]))
+    for t in bands(own):
+        s, label = cell[0, t, :], cell[1, t, :]
         lam = []
         for q in range(Q):
             if VEL[q][2] == 0:
-                lam.append(level[FLAT.index(q), t, c])
+                lam.append(level[FLAT.index(q), t, :])
             elif VEL[q][2] == 1:
                 i = RISE.index(q)
-                lam.append(pick(odd, pair[i, t, c], other[i, t, c]))
+                lam.append(pick(odd, pair[i, t, :], other[i, t, :]))
             else:
                 i = FALL.index(q)
-                lam.append(pick(odd, other[i, t, c], pair[i, t, c]))
-        grads, by_s, _, _, _, _ = pull_back(lam, [pop[q, t, c] for q in range(Q)], s, label, range(Q))
+                lam.append(pick(odd, other[i, t, :], pair[i, t, :]))
+        grads, by_s, _, _, _, _ = pull_back(lam, [pop[q, t, :] for q in range(Q)], s, label, range(Q))
         for q in range(Q):
-            out[q, t, c] = grads[q] * scale
-        sens[t, c] = jnp.where(label == 1.0, (by_s + late[3, t, c]) * scale, 0.0)
-        n = len(copies)
-        copies.append(pltpu.make_async_copy(out.at[:, t, c], out_h.at[:, t, c], sems.at[n]))
+            out[q, t, :] = grads[q] * scale
+        sens[t, :] = jnp.where(label == 1.0, (by_s + late[3, t, :]) * scale, 0.0)
+        n = t.start // 8
+        copies.append(pltpu.make_async_copy(out.at[:, t, :], out_h.at[:, t, :], sems.at[n]))
         copies[-1].start()
-    copies.append(pltpu.make_async_copy(sens, sens_h, sems.at[own // 4]))
+    copies.append(pltpu.make_async_copy(sens, sens_h, sems.at[own // 8]))
     copies[-1].start()
     for c in copies:
         c.wait()
@@ -652,7 +653,7 @@
         other,
         energy,
         hbm_out=2,
-        sems=own // 4 + 1,
+        sems=own // 8 + 1,
     )
     return sens.reshape(solid_fraction.shape), out.reshape(populations.shape)
 

time: 49.9 us -> 49.8 us (level)
  no operation moved by 1% of the time
where the time goes in v7:
time: 49.8 us; the launch traced here: 49.1 us
  starting transfers between devices  27.3 us (55%)
  waiting for transfers between devices  14.3 us (29%)
  Pallas kernels  4.12 us (8%)
  other arithmetic  1.53 us (3%)
  local copies, waits for them, and re-layouts  1.08 us (2%)
  between operations  0.75 us (2%)
    ppermute x4, starting transfers between devices, on_device(): other = lax.ppermute(other, axes, other_p)  6.72 us
    ppermute x4, starting transfers between devices, on_device(): pair = lax.ppermute(pair, axes, pair_p)  6.47 us
    all_to_all x1, starting transfers between devices, on_device(): energy = lax.all_to_all(energy, axes, 0, 0, tiled=True)  5.85 us
    ppermute x4, waiting for transfers between devices, on_device(): other = lax.ppermute(other, axes, other_p)  5.81 us
    pallas_call x7, Pallas kernels, call(): pl.pallas_call(kernel, out_shape=[jax.ShapeDtypeStruct(s, jnp.float32) fo...  4.12 us
    all_to_all x1, waiting for transfers between devices, on_device(): energy = lax.all_to_all(energy, axes, 0, 0, tiled=True)  3.6 us
    ppermute x1, waiting for transfers between devices, on_device(): lax.ppermute(edge_b, 'gy', [(k, (k - side(k)) % chunks) for k in range(ch...  3.08 us
    ppermute x1, starting transfers between devices, on_device(): mid_e = lax.ppermute(mid_e, axes, still_p)  2.72 us
  transfers between devices with their start and end apart: 15, of which 5 were waited for; matrix products, arithmetic and copies ran while one was open for 0% of the time, Pallas kernels for 1%

profile of v7, /device:TPU:0, one launch (start us, length us, event | category | flops | bytes accessed | tf_op | source)
XLA Modules:
  0.0 49.1 jit_solution(3060641966472087206)
XLA Ops:
  0.6 0.8 %convert_bitcast_fusion = f32[32,256]{1,0:T(8,128)S(1)} fusion(s32[1,32,256]{2,1,0:T(8,128)} %param.5), kind=kLoop, calls=%fused_computation.3 | loop fusion | flops 8192 | bytes 65536 | tf_op jit(solution)/shard_map/convert_element_type | solution.py:555
  1.4 0.8 %fusion = f32[1,32,256]{2,1,0:T(8,128)S(1)} fusion(f32[1,32,256]{2,1,0:T(8,128)} %param.4, f32[32,256]{1,0:T(8,128)S(1)} %convert_bitcast_fusion), kind=kLoop, calls=%fused_computation.2 | loop fusion | flops 32768 | bytes 98304 | tf_op jit(solution)/shard_map/stack | solution.py:557
  2.2 0.0 copy-start
  2.2 1.1 %copy-done = f32[19,1,32,256]{3,2,1,0:T(8,128)S(1)} copy-done((f32[19,1,32,256]{3,2,1,0:T(8,128)S(1)}, f32[19,1,32,256]{3,2,1,0:T(8,128)}, u32[]{:S(2)}) %copy-start) | copy-done | bytes 622616
  3.3 0.4 shard_map.50
  3.7 0.4 collective-permute-start
  4.1 2.0 %collective-permute-start.1 = (f32[63,256]{1,0:T(8,128)S(1)}, f32[63,256]{1,0:T(8,128)S(1)}, u32[]{:S(2)}, u32[]{:S(2)}) collective-permute-start(f32[63,256]{1,0:T(8,128)S(1)} %get-tuple-element.29), channel_id=1, source_target_pairs={{0,1},{1,0},{2,3},{3,2},{4,5},{5,4},{6,7},{7,6},{8,9},{9,8},{10,11... | collective-permute-start | bytes 193544 | tf_op jit(solution)/shard_map/ppermute | solution.py:568
  6.2 1.1 %collective-permute-start.2 = (f32[63,256]{1,0:T(8,128)S(1)}, f32[63,256]{1,0:T(8,128)S(1)}, u32[]{:S(2)}, u32[]{:S(2)}) collective-permute-start(f32[63,256]{1,0:T(8,128)S(1)} %get-tuple-element.30), channel_id=1, source_target_pairs={{0,3},{1,2},{2,1},{3,0},{4,7},{5,6},{6,5},{7,4},{8,11},{9,10},{10,... | collective-permute-start | bytes 193544 | tf_op jit(solution)/shard_map/ppermute | solution.py:569
  7.3 0.0 collective-permute-done.1.edge_pair
  7.3 3.1 %collective-permute-done.2.edge_other = f32[63,256]{1,0:T(8,128)S(1)} collective-permute-done((f32[63,256]{1,0:T(8,128)S(1)}, f32[63,256]{1,0:T(8,128)S(1)}, u32[]{:S(2)}, u32[]{:S(2)}) %collective-permute-start.2) | collective-permute-done | bytes 64544 | tf_op jit(solution)/shard_map/ppermute | solution.py:569
  10.4 0.7 %collective-permute-start.3 = (f32[5,40,256]{2,1,0:T(8,128)S(1)}, f32[5,40,256]{2,1,0:T(8,128)S(1)}, u32[]{:S(2)}, u32[]{:S(2)}) collective-permute-start(f32[5,40,256]{2,1,0:T(8,128)S(1)} %get-tuple-element.33), channel_id=1, source_target_pairs={{0,0},{1,4},{2,2},{3,6},{4,1},{5,5},{6,3},{7,7},{8,8},{9,12},{10,1... | collective-permute-start | bytes 614408 | tf_op jit(solution)/shard_map/ppermute | solution.py:585
  11.1 3.7 %collective-permute-start.4 = (f32[5,40,256]{2,1,0:T(8,128)S(1)}, f32[5,40,256]{2,1,0:T(8,128)S(1)}, u32[]{:S(2)}, u32[]{:S(2)}) collective-permute-start(f32[5,40,256]{2,1,0:T(8,128)S(1)} %get-tuple-element.34), channel_id=1, source_target_pairs={{0,24},{1,28},{2,26},{3,30},{4,9},{5,13},{6,11},{7,15},{8,0},{9,4}... | collective-permute-start | bytes 614408 | tf_op jit(solution)/shard_map/ppermute | solution.py:584
  14.8 2.7 %collective-permute-start.5 = (f32[11,8,256]{2,1,0:T(8,128)S(1)}, f32[11,8,256]{2,1,0:T(8,128)S(1)}, u32[]{:S(2)}, u32[]{:S(2)}) collective-permute-start(f32[11,8,256]{2,1,0:T(8,128)S(1)} %get-tuple-element.35), channel_id=1, source_target_pairs={{0,1},{1,5},{2,3},{3,7},{4,0},{5,4},{6,2},{7,6},{8,9},{9,13},{10,1... | collective-permute-start | bytes 270344 | tf_op jit(solution)/shard_map/ppermute | solution.py:583
  17.5 1.8 %collective-permute-done.5.mid_e = f32[11,8,256]{2,1,0:T(8,128)S(1)} collective-permute-done((f32[11,8,256]{2,1,0:T(8,128)S(1)}, f32[11,8,256]{2,1,0:T(8,128)S(1)}, u32[]{:S(2)}, u32[]{:S(2)}) %collective-permute-start.5) | collective-permute-done | bytes 90144 | tf_op jit(solution)/shard_map/ppermute | solution.py:583
  19.3 0.5 %shard_map.52 = (f32[26,40,256]{2,1,0:T(8,128)S(1)}, f32[3,40,256]{2,1,0:T(8,128)S(1)}, f32[3,40,256]{2,1,0:T(8,128)S(1)}, f32[3,40,256]{2,1,0:T(8,128)S(1)}, f32[8,128]{1,0:T(8,128)S(1)}) custom-call(s32[1]{0:T(128)S(6)} %select_n.29.odd_p, f32[11,32,256]{2,1,0:T(8,128)S(1)} %collective-permute-done.mid, f32[5,40,256]{2,1,0:T(8,128)S(1)} %collective-permute-done.3.pair, ...), custom_call_target="tpu_custom_call" | custom-call | tf_op jit(solution)/shard_map/pallas_call | solution.py:503
  19.9 2.1 %collective-permute-start.6 = (f32[3,40,256]{2,1,0:T(8,128)S(1)}, f32[3,40,256]{2,1,0:T(8,128)S(1)}, u32[]{:S(2)}, u32[]{:S(2)}) collective-permute-start(f32[3,40,256]{2,1,0:T(8,128)S(1)} %get-tuple-element.38), channel_id=1, source_target_pairs={{1,0},{5,4},{3,2},{7,6},{0,1},{4,5},{2,3},{6,7},{9,8},{13,12},{11,... | collective-permute-start | bytes 368648 | tf_op jit(solution)/shard_map/ppermute | solution.py:598
  21.9 1.5 %collective-permute-start.7 = (f32[3,40,256]{2,1,0:T(8,128)S(1)}, f32[3,40,256]{2,1,0:T(8,128)S(1)}, u32[]{:S(2)}, u32[]{:S(2)}) collective-permute-start(f32[3,40,256]{2,1,0:T(8,128)S(1)} %get-tuple-element.39), channel_id=1, source_target_pairs={{1,24},{5,28},{3,26},{7,30},{0,9},{4,13},{2,11},{6,15},{9,0},{13,4... | collective-permute-start | bytes 368648 | tf_op jit(solution)/shard_map/ppermute | solution.py:597
  23.5 2.8 %collective-permute-done.7.other = f32[3,40,256]{2,1,0:T(8,128)S(1)} collective-permute-done((f32[3,40,256]{2,1,0:T(8,128)S(1)}, f32[3,40,256]{2,1,0:T(8,128)S(1)}, u32[]{:S(2)}, u32[]{:S(2)}) %collective-permute-start.7) | collective-permute-done | bytes 122912 | tf_op jit(solution)/shard_map/ppermute | solution.py:597
  26.2 0.1 shard_map.53
  26.3 1.0 %shard_map.54 = (f32[9,32,256]{2,1,0:T(8,128)S(1)}, f32[3,40,256]{2,1,0:T(8,128)S(1)}, f32[32,8,128]{2,1,0:T(8,128)}) custom-call(f32[26,40,256]{2,1,0:T(8,128)S(1)} %get-tuple-element.36.field, f32[3,40,256]{2,1,0:T(8,128)S(1)} %get-tuple-element.41.mine, f32[8,128]{1,0:T(8,128)S(1)} %get-tuple-element.42.energy), custom_call_target="tpu_custom_call" | custom-call | tf_op jit(solution)/shard_map/pallas_call | solution.py:503
  27.3 0.0 copy-start.1
  27.3 0.1 collective-permute-start.8
  27.4 3.1 %collective-permute-start.9 = (f32[3,40,256]{2,1,0:T(8,128)S(1)}, f32[3,40,256]{2,1,0:T(8,128)S(1)}, u32[]{:S(2)}, u32[]{:S(2)}) collective-permute-start(f32[3,40,256]{2,1,0:T(8,128)S(1)} %get-tuple-element.44), channel_id=1, source_target_pairs={{1,0},{5,4},{3,2},{7,6},{0,1},{4,5},{2,3},{6,7},{9,8},{13,12},{11,... | collective-permute-start | bytes 368648 | tf_op jit(solution)/shard_map/ppermute | solution.py:611
  30.5 0.0 collective-permute-start.10
  30.5 5.9 %all-to-all-start = ((f32[32,8,128]{2,1,0:T(8,128)}), f32[32,8,128]{2,1,0:T(8,128)S(1)}, u32[]{:S(2)}, u32[]{:S(2)}) async-start(f32[32,8,128]{2,1,0:T(8,128)} %get-tuple-element.51), calls=%async_computation | async-start | bytes 262144 | tf_op jit(solution)/shard_map/all_to_all | solution.py:624
  36.4 0.6 %shard_map.55 = (f32[4,40,256]{2,1,0:T(8,128)S(1)}, f32[5,32,256]{2,1,0:T(8,128)S(1)}, f32[5,32,256]{2,1,0:T(8,128)S(1)}) custom-call(s32[1]{0:T(128)S(6)} %select_n.29.odd_p, f32[26,40,256]{2,1,0:T(8,128)S(1)} %get-tuple-element.36.field, f32[3,40,256]{2,1,0:T(8,128)S(1)} %get-tuple-element.41.mine, f32[3,40,256]{2,1,0:T(8,128)S(1)} %collective-permute-done.9.pair, ...), custom_call_target="tpu_custom_call" | custom-call | tf_op jit(solution)/shard_map/pallas_call | solution.py:503
  37.0 1.8 %collective-permute-start.11 = (f32[4,40,256]{2,1,0:T(8,128)S(1)}, f32[4,40,256]{2,1,0:T(8,128)S(1)}, u32[]{:S(2)}, u32[]{:S(2)}) collective-permute-start(f32[4,40,256]{2,1,0:T(8,128)S(1)} %get-tuple-element.48), channel_id=1, source_target_pairs={{1,0},{5,1},{3,2},{7,3},{0,4},{4,5},{2,6},{6,7},{9,8},{13,9},{11,1... | collective-permute-start | bytes 491528 | tf_op jit(solution)/shard_map/ppermute | solution.py:641
  38.8 0.7 %collective-permute-start.12 = (f32[5,32,256]{2,1,0:T(8,128)S(1)}, f32[5,32,256]{2,1,0:T(8,128)S(1)}, u32[]{:S(2)}, u32[]{:S(2)}) collective-permute-start(f32[5,32,256]{2,1,0:T(8,128)S(1)} %get-tuple-element.49), channel_id=1, source_target_pairs={{1,4},{5,5},{3,6},{7,7},{0,0},{4,1},{2,2},{6,3},{9,12},{13,13},{11... | collective-permute-start | bytes 491528 | tf_op jit(solution)/shard_map/ppermute | solution.py:639
  39.5 1.5 %collective-permute-start.13 = (f32[5,32,256]{2,1,0:T(8,128)S(1)}, f32[5,32,256]{2,1,0:T(8,128)S(1)}, u32[]{:S(2)}, u32[]{:S(2)}) collective-permute-start(f32[5,32,256]{2,1,0:T(8,128)S(1)} %get-tuple-element.50), channel_id=1, source_target_pairs={{1,28},{5,29},{3,30},{7,31},{0,8},{4,9},{2,10},{6,11},{9,4},{13,5}... | collective-permute-start | bytes 491528 | tf_op jit(solution)/shard_map/ppermute | solution.py:640
  41.0 3.6 %all-to-all-done.energy = f32[32,8,128]{2,1,0:T(8,128)S(1)} async-done(((f32[32,8,128]{2,1,0:T(8,128)}), f32[32,8,128]{2,1,0:T(8,128)S(1)}, u32[]{:S(2)}, u32[]{:S(2)}) %all-to-all-start) | async-done | bytes 131104 | tf_op jit(solution)/shard_map/all_to_all | solution.py:624
  44.6 3.0 %collective-permute-done.13.other = f32[5,32,256]{2,1,0:T(8,128)S(1)} collective-permute-done((f32[5,32,256]{2,1,0:T(8,128)S(1)}, f32[5,32,256]{2,1,0:T(8,128)S(1)}, u32[]{:S(2)}, u32[]{:S(2)}) %collective-permute-start.13) | collective-permute-done | bytes 163872 | tf_op jit(solution)/shard_map/ppermute | solution.py:640
  47.6 1.4 %shard_map.56 = (f32[32,256]{1,0:T(8,128)}, f32[19,32,256]{2,1,0:T(8,128)}) custom-call(s32[1]{0:T(128)} %bitcast.odd_z, f32[19,32,256]{2,1,0:T(8,128)S(1)} %bitcast.17, f32[2,32,256]{2,1,0:T(8,128)S(1)} %pad_maximum_fusion.cell, f32[9,32,256]{2,1,0:T(8,128)S(1)} %collective-permute-done.8.flat, f32[4,40,256]{2,1,0:T(8,128)S(1)} %collective-permute-done.11.late, ...), custom_call_target="tpu_custom_call" | custom-call | tf_op jit(solution)/shard_map/pallas_call | solution.py:503
  (12 shorter events, 0.1 us)
Async XLA Ops:
  2.2 1.1 %copy-start = (f32[19,1,32,256]{3,2,1,0:T(8,128)S(1)}, f32[19,1,32,256]{3,2,1,0:T(8,128)}, u32[]{:S(2)}) copy-start(f32[19,1,32,256]{3,2,1,0:T(8,128)} %param.3) | copy-start | bytes 1867780
  3.7 15.6 %collective-permute-start = (f32[11,32,256]{2,1,0:T(8,128)S(1)}, f32[11,32,256]{2,1,0:T(8,128)S(1)}, u32[]{:S(2)}, u32[]{:S(2)}) collective-permute-start(f32[11,32,256]{2,1,0:T(8,128)S(1)} %get-tuple-element.28), channel_id=1, source_target_pairs={{0,1},{1,5},{2,3},{3,7},{4,0},{5,4},{6,2},{7,6},{8,9},{9,13},{10,1... | collective-permute-start | bytes 1081352 | tf_op jit(solution)/shard_map/ppermute | solution.py:571
  4.1 3.2 %collective-permute-start.1 = (f32[63,256]{1,0:T(8,128)S(1)}, f32[63,256]{1,0:T(8,128)S(1)}, u32[]{:S(2)}, u32[]{:S(2)}) collective-permute-start(f32[63,256]{1,0:T(8,128)S(1)} %get-tuple-element.29), channel_id=1, source_target_pairs={{0,1},{1,0},{2,3},{3,2},{4,5},{5,4},{6,7},{7,6},{8,9},{9,8},{10,11... | collective-permute-start | bytes 193544 | tf_op jit(solution)/shard_map/ppermute | solution.py:568
  6.2 4.2 %collective-permute-start.2 = (f32[63,256]{1,0:T(8,128)S(1)}, f32[63,256]{1,0:T(8,128)S(1)}, u32[]{:S(2)}, u32[]{:S(2)}) collective-permute-start(f32[63,256]{1,0:T(8,128)S(1)} %get-tuple-element.30), channel_id=1, source_target_pairs={{0,3},{1,2},{2,1},{3,0},{4,7},{5,6},{6,5},{7,4},{8,11},{9,10},{10,... | collective-permute-start | bytes 193544 | tf_op jit(solution)/shard_map/ppermute | solution.py:569
  10.4 8.9 %collective-permute-start.3 = (f32[5,40,256]{2,1,0:T(8,128)S(1)}, f32[5,40,256]{2,1,0:T(8,128)S(1)}, u32[]{:S(2)}, u32[]{:S(2)}) collective-permute-start(f32[5,40,256]{2,1,0:T(8,128)S(1)} %get-tuple-element.33), channel_id=1, source_target_pairs={{0,0},{1,4},{2,2},{3,6},{4,1},{5,5},{6,3},{7,7},{8,8},{9,12},{10,1... | collective-permute-start | bytes 614408 | tf_op jit(solution)/shard_map/ppermute | solution.py:585
  11.1 8.2 %collective-permute-start.4 = (f32[5,40,256]{2,1,0:T(8,128)S(1)}, f32[5,40,256]{2,1,0:T(8,128)S(1)}, u32[]{:S(2)}, u32[]{:S(2)}) collective-permute-start(f32[5,40,256]{2,1,0:T(8,128)S(1)} %get-tuple-element.34), channel_id=1, source_target_pairs={{0,24},{1,28},{2,26},{3,30},{4,9},{5,13},{6,11},{7,15},{8,0},{9,4}... | collective-permute-start | bytes 614408 | tf_op jit(solution)/shard_map/ppermute | solution.py:584
  14.8 4.5 %collective-permute-start.5 = (f32[11,8,256]{2,1,0:T(8,128)S(1)}, f32[11,8,256]{2,1,0:T(8,128)S(1)}, u32[]{:S(2)}, u32[]{:S(2)}) collective-permute-start(f32[11,8,256]{2,1,0:T(8,128)S(1)} %get-tuple-element.35), channel_id=1, source_target_pairs={{0,1},{1,5},{2,3},{3,7},{4,0},{5,4},{6,2},{7,6},{8,9},{9,13},{10,1... | collective-permute-start | bytes 270344 | tf_op jit(solution)/shard_map/ppermute | solution.py:583
  19.9 3.6 %collective-permute-start.6 = (f32[3,40,256]{2,1,0:T(8,128)S(1)}, f32[3,40,256]{2,1,0:T(8,128)S(1)}, u32[]{:S(2)}, u32[]{:S(2)}) collective-permute-start(f32[3,40,256]{2,1,0:T(8,128)S(1)} %get-tuple-element.38), channel_id=1, source_target_pairs={{1,0},{5,4},{3,2},{7,6},{0,1},{4,5},{2,3},{6,7},{9,8},{13,12},{11,... | collective-permute-start | bytes 368648 | tf_op jit(solution)/shard_map/ppermute | solution.py:598
  21.9 4.3 %collective-permute-start.7 = (f32[3,40,256]{2,1,0:T(8,128)S(1)}, f32[3,40,256]{2,1,0:T(8,128)S(1)}, u32[]{:S(2)}, u32[]{:S(2)}) collective-permute-start(f32[3,40,256]{2,1,0:T(8,128)S(1)} %get-tuple-element.39), channel_id=1, source_target_pairs={{1,24},{5,28},{3,26},{7,30},{0,9},{4,13},{2,11},{6,15},{9,0},{13,4... | collective-permute-start | bytes 368648 | tf_op jit(solution)/shard_map/ppermute | solution.py:597
  27.3 20.4 %copy-start.1 = (f32[19,1,32,256]{3,2,1,0:T(8,128)S(1)}, f32[19,1,32,256]{3,2,1,0:T(8,128)}, u32[]{:S(2)}) copy-start(f32[19,1,32,256]{3,2,1,0:T(8,128)} %param.3) | copy-start | bytes 1867780
  27.3 20.4 %collective-permute-start.8 = (f32[9,32,256]{2,1,0:T(8,128)S(1)}, f32[9,32,256]{2,1,0:T(8,128)S(1)}, u32[]{:S(2)}, u32[]{:S(2)}) collective-permute-start(f32[9,32,256]{2,1,0:T(8,128)S(1)} %get-tuple-element.43), channel_id=1, source_target_pairs={{1,0},{5,1},{3,2},{7,3},{0,4},{4,5},{2,6},{6,7},{9,8},{13,9},{11,1... | collective-permute-start | bytes 884744 | tf_op jit(solution)/shard_map/ppermute | solution.py:638
  27.4 9.0 %collective-permute-start.9 = (f32[3,40,256]{2,1,0:T(8,128)S(1)}, f32[3,40,256]{2,1,0:T(8,128)S(1)}, u32[]{:S(2)}, u32[]{:S(2)}) collective-permute-start(f32[3,40,256]{2,1,0:T(8,128)S(1)} %get-tuple-element.44), channel_id=1, source_target_pairs={{1,0},{5,4},{3,2},{7,6},{0,1},{4,5},{2,3},{6,7},{9,8},{13,12},{11,... | collective-permute-start | bytes 368648 | tf_op jit(solution)/shard_map/ppermute | solution.py:611
  30.5 5.9 %collective-permute-start.10 = (f32[3,40,256]{2,1,0:T(8,128)S(1)}, f32[3,40,256]{2,1,0:T(8,128)S(1)}, u32[]{:S(2)}, u32[]{:S(2)}) collective-permute-start(f32[3,40,256]{2,1,0:T(8,128)S(1)} %get-tuple-element.45), channel_id=1, source_target_pairs={{1,24},{5,28},{3,26},{7,30},{0,9},{4,13},{2,11},{6,15},{9,0},{13,4... | collective-permute-start | bytes 368648 | tf_op jit(solution)/shard_map/ppermute | solution.py:610
  30.5 14.1 %all-to-all-start = ((f32[32,8,128]{2,1,0:T(8,128)}), f32[32,8,128]{2,1,0:T(8,128)S(1)}, u32[]{:S(2)}, u32[]{:S(2)}) async-start(f32[32,8,128]{2,1,0:T(8,128)} %get-tuple-element.51), calls=%async_computation | async-start | bytes 262144 | tf_op jit(solution)/shard_map/all_to_all | solution.py:624
  37.0 7.6 %collective-permute-start.11 = (f32[4,40,256]{2,1,0:T(8,128)S(1)}, f32[4,40,256]{2,1,0:T(8,128)S(1)}, u32[]{:S(2)}, u32[]{:S(2)}) collective-permute-start(f32[4,40,256]{2,1,0:T(8,128)S(1)} %get-tuple-element.48), channel_id=1, source_target_pairs={{1,0},{5,1},{3,2},{7,3},{0,4},{4,5},{2,6},{6,7},{9,8},{13,9},{11,1... | collective-permute-start | bytes 491528 | tf_op jit(solution)/shard_map/ppermute | solution.py:641
  38.8 5.8 %collective-permute-start.12 = (f32[5,32,256]{2,1,0:T(8,128)S(1)}, f32[5,32,256]{2,1,0:T(8,128)S(1)}, u32[]{:S(2)}, u32[]{:S(2)}) collective-permute-start(f32[5,32,256]{2,1,0:T(8,128)S(1)} %get-tuple-element.49), channel_id=1, source_target_pairs={{1,4},{5,5},{3,6},{7,7},{0,0},{4,1},{2,2},{6,3},{9,12},{13,13},{11... | collective-permute-start | bytes 491528 | tf_op jit(solution)/shard_map/ppermute | solution.py:639
  39.5 8.2 %collective-permute-start.13 = (f32[5,32,256]{2,1,0:T(8,128)S(1)}, f32[5,32,256]{2,1,0:T(8,128)S(1)}, u32[]{:S(2)}, u32[]{:S(2)}) collective-permute-start(f32[5,32,256]{2,1,0:T(8,128)S(1)} %get-tuple-element.50), channel_id=1, source_target_pairs={{1,28},{5,29},{3,30},{7,31},{0,8},{4,9},{2,10},{6,11},{9,4},{13,5}... | collective-permute-start | bytes 491528 | tf_op jit(solution)/shard_map/ppermute | solution.py:640
